TPU v7x, 32 devices: a whole 2x2x4 slice. The times are simulated.
32 devices in a mesh: fsdp: 32 (over z, y, x, core).
Axes of the slice: x: 2, y: 2, z: 4, core: 2. Of those that a mesh axis runs over, the one named last changes fastest.
Arguments:
- inputs: bfloat16 [8192, 384], P('fsdp'), may hold values from -6 to 6
- attn_blocks: bfloat16 [32, 18560], P('fsdp')
- mlp_blocks: bfloat16 [32, 36992], P('fsdp')
- image_id: int32 [8192], P('fsdp'), may hold values from 0 to 42, as said below
- bias_id: int32 [8192], P('fsdp'), may hold values from 0 to 15
- out_grad: bfloat16 [8192, 384], P('fsdp'), may hold values from -6 to 6
Outputs:
- output: bfloat16 [8192, 384], P('fsdp')
- grad_inputs: float32 [8192, 384], P('fsdp')
- grad_attn: float32 [32, 18560], P('fsdp')
- grad_mlp: float32 [32, 36992], P('fsdp')
Inputs may be any that keep to these rules, and one draw needn't show every extreme that they name: `image_id`: tokens of one image are contiguous and image numbers rise by one from image to image, starting at 0 and ending at (42); every image holds 197 tokens except the first and the last, which may hold fewer.
All inputs are finite; a program needn't handle non-finite values.
Results may differ from a plain program's by a relative error of at most 0.009.
Values may be sent and summed in bfloat16 or wider, within the bound.
No kernel may reach another device: no remote copies, remote signals or barrier semaphores. Data moves between devices by JAX's collectives and lax.ppermute only.
A program may use at most 128 MiB of HBM per device.

v0:
```python
import functools
import math

import jax
import jax.numpy as jnp
from jax import lax
from jax.experimental import pallas as pl
from jax.experimental.pallas import tpu as pltpu
from jax.sharding import PartitionSpec as P

D = 384
FF = 1536
HEADS = 6
HEAD_DIM = 64
IMG = 197
NB = 16

LANES = 128
CORES = 2
SQUARE = 4
SLOT = 208
SPAN = 2 * SLOT
HALO = 112
WIDE = 2 * D + LANES
D_ROWS = D // LANES
FF_ROWS = FF // LANES
QKV_ROWS = 3 * D // LANES

GAIN_AT = 0
SHIFT_AT = D_ROWS
W_QKV_AT = 2 * D_ROWS
BIAS_QUERY_AT = W_QKV_AT + D * QKV_ROWS
BIAS_VALUE_AT = BIAS_QUERY_AT + D_ROWS
W_OUT_AT = BIAS_VALUE_AT + D_ROWS
BIAS_OUT_AT = W_OUT_AT + D * D_ROWS
TABLE_AT = BIAS_OUT_AT + D_ROWS
W_UP_AT = 2 * D_ROWS
BIAS_UP_AT = W_UP_AT + D * FF_ROWS
W_DOWN_AT = BIAS_UP_AT + FF_ROWS
BIAS_DOWN_AT = W_DOWN_AT + FF * D_ROWS
FEED_END = BIAS_DOWN_AT + D_ROWS

epsilon = 1e-06
score_scale = HEAD_DIM ** (-0.5)
masked_score = -1e30
f32 = jnp.float32
bf16 = jnp.bfloat16


def dot(left, right):
    return lax.dot_general(left, right, (((1,), (0,)), ((), ())), preferred_element_type=f32)


def dot_rows(left, right):
    return lax.dot_general(left, right, (((0,), (0,)), ((), ())), preferred_element_type=f32)


def dot_cols(left, right):
    return lax.dot_general(left, right, (((1,), (1,)), ((), ())), preferred_element_type=f32)


def groups_of(devices):
    inner = CORES * SQUARE
    chips = [
        [base + CORES * spot + core for spot in range(SQUARE)]
        for base in range(0, devices, inner)
        for core in range(CORES)
    ]
    columns = [[base + inner * spot for spot in range(devices // inner)] for base in range(inner)]
    return (chips, columns)


def swap_cores(value, devices):
    return lax.ppermute(value, "fsdp", [(i, i ^ 1) for i in range(devices)])


def gather_blocks(block, devices):
    chips, columns = groups_of(devices)
    rows = block.shape[1] // LANES
    depth = devices // (CORES * SQUARE)
    part = jnp.broadcast_to(block.reshape(1, rows, LANES), (depth, rows, LANES))
    part = lax.all_to_all(part, "fsdp", 0, 0, axis_index_groups=columns, tiled=True)
    part = jnp.broadcast_to(part[None], (SQUARE, depth, rows, LANES))
    part = lax.all_to_all(part, "fsdp", 0, 0, axis_index_groups=chips, tiled=True)
    return (part, swap_cores(part, devices))


def add_cores(keep, send, devices):
    other = swap_cores(send, devices)
    return (keep.astype(f32) + other.astype(f32)).astype(bf16)


def add_chips(part, devices):
    chips, columns = groups_of(devices)
    part = lax.all_to_all(part, "fsdp", 1, 1, axis_index_groups=chips, tiled=True)
    return jnp.sum(part.astype(f32), axis=1).astype(bf16)


def add_columns(part, devices):
    chips, columns = groups_of(devices)
    part = lax.all_to_all(part, "fsdp", 0, 0, axis_index_groups=columns, tiled=True)
    return jnp.sum(part.astype(f32), axis=0).reshape(1, -1)


def lay_out_blocks(core, mine_ref, other_ref, flat_ref):
    spots, depth, rows, lanes = mine_ref.shape
    for layer in range(depth):
        for spot in range(spots):
            base = (layer * spots + spot) * CORES * rows
            mine = mine_ref[spot, layer].astype(f32)
            other = other_ref[spot, layer].astype(f32)
            flat_ref[base : base + rows] = jnp.where(core == 0, mine, other)
            flat_ref[base + rows : base + 2 * rows] = jnp.where(core == 0, other, mine)


def cut_blocks(core, flat_ref, keep_ref, send_ref):
    depth, spots, rows, lanes = keep_ref.shape
    for layer in range(depth):
        for spot in range(spots):
            base = (layer * spots + spot) * CORES * rows
            first = flat_ref[base : base + rows]
            second = flat_ref[base + rows : base + 2 * rows]
            keep_ref[layer, spot] = jnp.where(core == 0, first, second).astype(bf16)
            send_ref[layer, spot] = jnp.where(core == 0, second, first).astype(bf16)


def read_vector(flat_ref, at, amount):
    return jnp.concatenate([flat_ref[at + i : at + i + 1] for i in range(amount)], axis=1)


def write_vector(flat_ref, at, amount, value):
    for i in range(amount):
        flat_ref[at + i : at + i + 1] = value[:, i * LANES : (i + 1) * LANES]


def read_matrix(flat_ref, at, height, amount, out_ref):
    for i in range(amount):
        chunk = flat_ref[pl.ds(at + i, height, stride=amount), :]
        out_ref[:, i * LANES : (i + 1) * LANES] = chunk.astype(bf16)


def normalise(values):
    average = jnp.mean(values, axis=-1, keepdims=True)
    centred = values - average
    variance = jnp.mean(centred * centred, axis=-1, keepdims=True)
    inverse = lax.rsqrt(variance + epsilon)
    return (centred * inverse, inverse)


def norm_back(grad, unit, inverse, gain):
    scaled = grad * gain
    first = jnp.mean(scaled, axis=-1, keepdims=True)
    second = jnp.mean(scaled * unit, axis=-1, keepdims=True)
    return inverse * (scaled - first - unit * second)


def slot_mask(meta_ref, window, by_column):
    shape = (window, SPAN) if by_column else (SPAN, window)
    spot = lax.broadcasted_iota(jnp.int32, shape, 0 if by_column else 1)
    row = lax.broadcasted_iota(jnp.int32, shape, 1 if by_column else 0)
    start = jnp.where(row < SLOT, meta_ref[0], meta_ref[2] - SLOT)
    limit = jnp.where(row < SLOT, meta_ref[1], meta_ref[3] + SLOT)
    return jnp.where((spot == row + start) & (row < limit), 1.0, 0.0).astype(bf16)


def head_lanes(half):
    lane = lax.broadcasted_iota(jnp.int32, (1, LANES), 1)
    return (lane < HEAD_DIM) if half == 0 else (lane >= HEAD_DIM)


def attend_kernel(
    meta_ref, before_ref, own_ref, after_ref, mask_ref, mine_ref, other_ref,
    middle_ref, cotangent_ref, inputs_ref, normed_ref, qkv_ref, probability_ref,
    context_ref, classes_ref, w_qkv_ref, w_out_ref, gain_ref,
    flat_ref, window_ref,
):
    core = meta_ref[4]
    window = window_ref.shape[0]
    lay_out_blocks(core, mine_ref, other_ref, flat_ref)
    read_matrix(flat_ref, W_QKV_AT, D, QKV_ROWS, w_qkv_ref)
    read_matrix(flat_ref, W_OUT_AT, D, D_ROWS, w_out_ref)
    gain = read_vector(flat_ref, GAIN_AT, D_ROWS)
    shift = read_vector(flat_ref, SHIFT_AT, D_ROWS)
    gain_ref[...] = gain
    bias_query = read_vector(flat_ref, BIAS_QUERY_AT, D_ROWS)
    bias_value = read_vector(flat_ref, BIAS_VALUE_AT, D_ROWS)
    bias_out = read_vector(flat_ref, BIAS_OUT_AT, D_ROWS)
    table = (mask_ref[...] * flat_ref[TABLE_AT : TABLE_AT + 1]).astype(bf16)

    halo = before_ref.shape[0]
    own = own_ref.shape[0]
    window_ref[0:halo] = before_ref[...]
    window_ref[halo : halo + own] = own_ref[...]
    window_ref[halo + own : window] = after_ref[...]
    picked = dot(slot_mask(meta_ref, window, False), window_ref[...])
    inputs = picked[:, :D]
    inputs_ref[...] = inputs.astype(bf16)
    cotangent_ref[...] = picked[:, D : 2 * D].astype(bf16)
    classes_ref[...] = picked[:, 2 * D :].astype(bf16)

    unit, _ = normalise(inputs)
    normed_ref[...] = (unit * gain + shift).astype(bf16)
    normed = normed_ref[...]
    qkv_ref[:, :D] = (dot(normed, w_qkv_ref[:, :D]) + bias_query).astype(bf16)
    qkv_ref[:, D : 2 * D] = dot(normed, w_qkv_ref[:, D : 2 * D]).astype(bf16)
    qkv_ref[:, 2 * D :] = (dot(normed, w_qkv_ref[:, 2 * D :]) + bias_value).astype(bf16)

    for slot in range(2):
        rows = slice(slot * SLOT, (slot + 1) * SLOT)
        key = lax.broadcasted_iota(jnp.int32, (1, SLOT), 1)
        key_bias = dot_cols(table, classes_ref[rows])
        key_bias = jnp.where(key < meta_ref[2 * slot + 1], key_bias, masked_score)
        for pair in range(HEADS // 2):
            lanes = slice(pair * LANES, (pair + 1) * LANES)
            queries = qkv_ref[rows, lanes]
            keys = qkv_ref[rows, D + pair * LANES : D + (pair + 1) * LANES]
            values = qkv_ref[rows, 2 * D + pair * LANES : 2 * D + (pair + 1) * LANES]
            mixed = []
            for half in range(2):
                head = 2 * pair + half
                chosen = jnp.where(head_lanes(half), queries, jnp.zeros_like(queries))
                scores = dot_cols(chosen, keys) * score_scale + key_bias[head : head + 1]
                peak = jnp.max(scores, axis=-1, keepdims=True)
                weights = jnp.exp(scores - peak)
                total = jnp.sum(weights, axis=-1, keepdims=True)
                probability = (weights * (1.0 / total)).astype(bf16)
                probability_ref[slot * HEADS + head] = probability
                mixed.append(dot(probability, values))
            context_ref[rows, lanes] = jnp.where(head_lanes(0), mixed[0], mixed[1]).astype(bf16)
    middle_ref[...] = inputs + dot(context_ref[...], w_out_ref[...]) + bias_out


def feed_kernel(
    meta_ref, middle_ref, cotangent_ref, mine_ref, other_ref,
    output_ref, grad_middle_ref, keep_ref, send_ref,
    flat_ref, w_up_ref, w_down_ref, normed_ref,
):
    core = meta_ref[4]
    window = output_ref.shape[0]
    lay_out_blocks(core, mine_ref, other_ref, flat_ref)
    read_matrix(flat_ref, W_UP_AT, D, FF_ROWS, w_up_ref)
    read_matrix(flat_ref, W_DOWN_AT, FF, D_ROWS, w_down_ref)
    gain = read_vector(flat_ref, GAIN_AT, D_ROWS)
    shift = read_vector(flat_ref, SHIFT_AT, D_ROWS)
    bias_up = read_vector(flat_ref, BIAS_UP_AT, FF_ROWS)
    bias_down = read_vector(flat_ref, BIAS_DOWN_AT, D_ROWS)

    middle = middle_ref[...]
    cotangent = cotangent_ref[...]
    unit, inverse = normalise(middle)
    normed_ref[...] = (unit * gain + shift).astype(bf16)
    normed = normed_ref[...]
    output = middle + bias_down
    grad = jnp.zeros((SPAN, D), f32)
    slope = math.sqrt(2.0 / math.pi)
    for step in range(FF // D):
        cols = slice(step * D, (step + 1) * D)
        w_up = w_up_ref[:, cols]
        w_down = w_down_ref[cols]
        hidden = dot(normed, w_up) + bias_up[:, cols]
        square = hidden * hidden
        bend = jnp.tanh(slope * hidden * (1.0 + 0.044715 * square))
        half = 0.5 * (1.0 + bend)
        active = (hidden * half).astype(bf16)
        steep = half + 0.5 * hidden * (1.0 - bend * bend) * (
            slope * (1.0 + (3 * 0.044715) * square)
        )
        grad_hidden_wide = dot_cols(cotangent, w_down) * steep
        grad_hidden = grad_hidden_wide.astype(bf16)
        output = output + dot(active, w_down)
        grad = grad + dot_cols(grad_hidden, w_up)
        grad_down = dot_rows(active, cotangent)
        grad_up = dot_rows(normed, grad_hidden)
        grad_bias = jnp.sum(grad_hidden.astype(f32), axis=0, keepdims=True)
        write_vector(flat_ref, BIAS_UP_AT + step * D_ROWS, D_ROWS, grad_bias)
        for i in range(D_ROWS):
            lanes = slice(i * LANES, (i + 1) * LANES)
            flat_ref[pl.ds(W_UP_AT + step * D_ROWS + i, D, stride=FF_ROWS), :] = grad_up[:, lanes]
            flat_ref[pl.ds(W_DOWN_AT + step * D * D_ROWS + i, D, stride=D_ROWS), :] = grad_down[
                :, lanes
            ]
    output_ref[...] = dot(slot_mask(meta_ref, window, True), output.astype(bf16)).astype(bf16)
    grad_output = cotangent.astype(f32)
    write_vector(flat_ref, GAIN_AT, D_ROWS, jnp.sum(grad * unit, axis=0, keepdims=True))
    write_vector(flat_ref, SHIFT_AT, D_ROWS, jnp.sum(grad, axis=0, keepdims=True))
    write_vector(flat_ref, BIAS_DOWN_AT, D_ROWS, jnp.sum(grad_output, axis=0, keepdims=True))
    flat_ref[FEED_END:] = jnp.zeros((flat_ref.shape[0] - FEED_END, LANES), f32)
    grad_middle_ref[...] = grad_output + norm_back(grad, unit, inverse, gain)
    cut_blocks(core, flat_ref, keep_ref, send_ref)


def attend_back_kernel(
    meta_ref, grad_middle_ref, mask_ref, inputs_ref, normed_ref, qkv_ref, probability_ref,
    context_ref, classes_ref, w_qkv_ref, w_out_ref, gain_ref,
    grad_inputs_ref, keep_ref, send_ref,
    flat_ref, grad_qkv_ref, grad_context_ref,
):
    core = meta_ref[4]
    window = grad_inputs_ref.shape[0]
    grad_middle = grad_middle_ref[...]
    grad_branch = grad_middle.astype(bf16)
    grad_bias_out = jnp.sum(grad_branch.astype(f32), axis=0, keepdims=True)
    write_vector(flat_ref, BIAS_OUT_AT, D_ROWS, grad_bias_out)
    grad_w_out = dot_rows(context_ref[...], grad_branch)
    for i in range(D_ROWS):
        flat_ref[pl.ds(W_OUT_AT + i, D, stride=D_ROWS), :] = grad_w_out[
            :, i * LANES : (i + 1) * LANES
        ]
    grad_context_ref[...] = dot_cols(grad_branch, w_out_ref[...]).astype(bf16)
    grad_table = jnp.zeros((8, LANES), f32)
    for slot in range(2):
        rows = slice(slot * SLOT, (slot + 1) * SLOT)
        key_sums = []
        for pair in range(HEADS // 2):
            lanes = slice(pair * LANES, (pair + 1) * LANES)
            key_lanes = slice(D + pair * LANES, D + (pair + 1) * LANES)
            value_lanes = slice(2 * D + pair * LANES, 2 * D + (pair + 1) * LANES)
            queries = qkv_ref[rows, lanes]
            keys = qkv_ref[rows, key_lanes]
            values = qkv_ref[rows, value_lanes]
            grad_context = grad_context_ref[rows, lanes]
            parts = []
            for half in range(2):
                head = 2 * pair + half
                chosen = jnp.where(head_lanes(half), grad_context, jnp.zeros_like(grad_context))
                grad_probs = dot_cols(chosen, values)
                narrow = probability_ref[slot * HEADS + head]
                probability = narrow.astype(f32)
                weighted = probability * grad_probs
                grad_scores = weighted - probability * jnp.sum(weighted, axis=-1, keepdims=True)
                key_sums.append(jnp.sum(grad_scores, axis=0, keepdims=True))
                grad_raw = (grad_scores * score_scale).astype(bf16)
                parts.append(
                    (dot(grad_raw, keys), dot_rows(grad_raw, queries), dot_rows(narrow, grad_context))
                )
            low = head_lanes(0)
            for where, first, second in zip((lanes, key_lanes, value_lanes), *parts):
                grad_qkv_ref[rows, where] = jnp.where(low, first, second).astype(bf16)
        sums = jnp.concatenate(key_sums + [jnp.zeros((8 - HEADS, SLOT), f32)], axis=0)
        sums_high = sums.astype(bf16)
        sums_low = (sums - sums_high.astype(f32)).astype(bf16)
        classes = classes_ref[rows]
        grad_table = grad_table + dot(sums_high, classes) + dot(sums_low, classes)
    flat_ref[TABLE_AT:] = jnp.zeros((flat_ref.shape[0] - TABLE_AT, LANES), f32)
    flat_ref[TABLE_AT : TABLE_AT + 1] = jnp.sum(grad_table * mask_ref[...], axis=0, keepdims=True)

    grad_qkv = grad_qkv_ref[...]
    column_sums = jnp.sum(grad_qkv.astype(f32), axis=0, keepdims=True)
    write_vector(flat_ref, BIAS_QUERY_AT, D_ROWS, column_sums[:, :D])
    write_vector(flat_ref, BIAS_VALUE_AT, D_ROWS, column_sums[:, 2 * D :])
    normed = normed_ref[...]
    for part in range(3):
        grad_w = dot_rows(normed, grad_qkv_ref[:, part * D : (part + 1) * D])
        for i in range(D_ROWS):
            flat_ref[pl.ds(W_QKV_AT + part * D_ROWS + i, D, stride=QKV_ROWS), :] = grad_w[
                :, i * LANES : (i + 1) * LANES
            ]
    grad_normed = dot_cols(grad_qkv, w_qkv_ref[...])
    gain = gain_ref[...]
    unit, inverse = normalise(inputs_ref[...].astype(f32))
    write_vector(flat_ref, GAIN_AT, D_ROWS, jnp.sum(grad_normed * unit, axis=0, keepdims=True))
    write_vector(flat_ref, SHIFT_AT, D_ROWS, jnp.sum(grad_normed, axis=0, keepdims=True))
    grad_inputs = grad_middle + norm_back(grad_normed, unit, inverse, gain)
    high = grad_inputs.astype(bf16)
    low_part = (grad_inputs - high.astype(f32)).astype(bf16)
    back = slot_mask(meta_ref, window, True)
    grad_inputs_ref[...] = dot(back, high) + dot(back, low_part)
    cut_blocks(core, flat_ref, keep_ref, send_ref)


def call_kernel(kernel, out_shapes, scratch, flops, operands):
    vmem = pl.BlockSpec(memory_space=pltpu.VMEM)
    specs = [pl.BlockSpec(memory_space=pltpu.SMEM)] + [vmem] * (len(operands) - 1)
    moved = sum(math.prod(o.shape) * o.dtype.itemsize for o in list(operands) + list(out_shapes))
    return pl.pallas_call(
        kernel,
        out_shape=out_shapes,
        in_specs=specs,
        out_specs=[vmem] * len(out_shapes),
        scratch_shapes=scratch,
        compiler_params=pltpu.CompilerParams(vmem_limit_bytes=50 * 1024 * 1024),
        cost_estimate=pl.CostEstimate(flops=flops, bytes_accessed=moved, transcendentals=0),
    )(*operands)


def plan_slots(image_id, devices):
    token_rows = image_id.shape[0]
    device = lax.axis_index("fsdp")
    ends = jnp.sum((image_id == image_id[0]).astype(jnp.int32))
    first, last = device == 0, device == devices - 1
    holds = first | (ends >= IMG // 2 + 1)
    start = jnp.where(first, 0, jnp.where(holds, ends - IMG, ends))
    stop = jnp.where(last, token_rows, token_rows + IMG)
    stop_one = jnp.where(holds, ends, jnp.minimum(ends + IMG, stop))
    next_centre = stop_one + IMG // 2
    has_next = (stop_one < stop) & (last | (next_centre < token_rows))
    stop_two = jnp.where(has_next, jnp.minimum(stop_one + IMG, stop), stop_one)
    zero = jnp.zeros((), jnp.int32)
    return jnp.stack(
        [start + HALO, stop_one - start, stop_one + HALO, stop_two - stop_one, device % CORES]
        + [zero] * 3
    ).astype(jnp.int32)


def struct(shape, kind):
    return jax.ShapeDtypeStruct(shape, kind)


def shards(inputs, attn_blocks, mlp_blocks, image_id, bias_id, out_grad):
    token_rows = inputs.shape[0]
    devices = lax.axis_size("fsdp")
    depth = devices // (CORES * SQUARE)
    window = token_rows + 2 * HALO
    attn_rows = attn_blocks.shape[1] // LANES
    mlp_rows = mlp_blocks.shape[1] // LANES
    attn_mine, attn_other = gather_blocks(attn_blocks, devices)

    lane = jnp.arange(LANES, dtype=jnp.int32)
    classes = ((lane // HEADS)[None, :] == bias_id[:, None]) & (lane < NB * HEADS)[None, :]
    tokens = jnp.concatenate([inputs, out_grad, classes.astype(bf16)], axis=1)
    up = [(i, i + 1) for i in range(devices - 1)]
    down = [(i + 1, i) for i in range(devices - 1)]
    before = lax.ppermute(tokens[token_rows - HALO :], "fsdp", up)
    after = lax.ppermute(tokens[:HALO], "fsdp", down)
    meta = plan_slots(image_id, devices)
    head = jnp.arange(8, dtype=jnp.int32)
    head_mask = ((lane % HEADS)[None, :] == head[:, None]) & (lane < NB * HEADS)[None, :]
    head_mask = head_mask.astype(f32)
    mlp_mine, mlp_other = gather_blocks(mlp_blocks, devices)

    (
        middle, cotangent, inputs_span, normed, qkv, probability, context, classes_span,
        w_qkv, w_out, gain,
    ) = call_kernel(
        attend_kernel,
        [
            struct((SPAN, D), f32),
            struct((SPAN, D), bf16),
            struct((SPAN, D), bf16),
            struct((SPAN, D), bf16),
            struct((SPAN, 3 * D), bf16),
            struct((2 * HEADS, SLOT, SLOT), bf16),
            struct((SPAN, D), bf16),
            struct((SPAN, LANES), bf16),
            struct((D, 3 * D), bf16),
            struct((D, D), bf16),
            struct((1, D), f32),
        ],
        [pltpu.VMEM((devices * attn_rows, LANES), f32), pltpu.VMEM((window, WIDE), bf16)],
        2 * 10**9,
        [meta, before, tokens, after, head_mask, attn_mine, attn_other],
    )
    output, grad_middle, feed_keep, feed_send = call_kernel(
        feed_kernel,
        [
            struct((window, D), bf16),
            struct((SPAN, D), f32),
            struct((depth, SQUARE, mlp_rows, LANES), bf16),
            struct((depth, SQUARE, mlp_rows, LANES), bf16),
        ],
        [
            pltpu.VMEM((devices * mlp_rows, LANES), f32),
            pltpu.VMEM((D, FF), bf16),
            pltpu.VMEM((FF, D), bf16),
            pltpu.VMEM((SPAN, D), bf16),
        ],
        4 * 10**9,
        [meta, middle, cotangent, mlp_mine, mlp_other],
    )
    feed_part = add_chips(add_cores(feed_keep, feed_send, devices), devices)
    grad_mlp = add_columns(feed_part, devices)
    grad_inputs, attn_keep, attn_send = call_kernel(
        attend_back_kernel,
        [
            struct((window, D), f32),
            struct((depth, SQUARE, attn_rows, LANES), bf16),
            struct((depth, SQUARE, attn_rows, LANES), bf16),
        ],
        [
            pltpu.VMEM((devices * attn_rows, LANES), f32),
            pltpu.VMEM((SPAN, 3 * D), bf16),
            pltpu.VMEM((SPAN, D), bf16),
        ],
        3 * 10**9,
        [
            meta, grad_middle, head_mask, inputs_span, normed, qkv, probability, context,
            classes_span, w_qkv, w_out, gain,
        ],
    )
    attn_part = add_chips(add_cores(attn_keep, attn_send, devices), devices)
    grad_attn = add_columns(attn_part, devices)
    edges = jnp.concatenate([output, grad_inputs.astype(bf16)], axis=1)
    from_next = lax.ppermute(edges[:HALO], "fsdp", down)
    from_last = lax.ppermute(edges[window - HALO :], "fsdp", up)
    gap = jnp.zeros((token_rows - HALO, 2 * D), bf16)
    extra = jnp.concatenate([from_last, gap]) + jnp.concatenate([gap, from_next])
    own = slice(HALO, HALO + token_rows)
    output = output[own] + extra[:, :D]
    grad_inputs = grad_inputs[own] + extra[:, D:].astype(f32)
    return (output, grad_inputs, grad_attn, grad_mlp)


def solution(mesh):
    return jax.shard_map(
        shards,
        mesh=mesh,
        in_specs=(
            P("fsdp", None),
            P("fsdp", None),
            P("fsdp", None),
            P("fsdp"),
            P("fsdp"),
            P("fsdp", None),
        ),
        out_specs=(P("fsdp", None), P("fsdp", None), P("fsdp", None), P("fsdp", None)),
        check_vma=False,
    )
```

profile of v0, /device:TPU:0, one launch (start us, length us, event | category | flops | bytes accessed | tf_op | source)
XLA Modules:
  0.0 165.3 jit_solution(4796130664110015954)
XLA Ops:
  2.8 6.3 %all-to-all-start.2 = ((bf16[4,289,128]{2,1,0:T(8,128)(2,1)}), bf16[4,289,128]{2,1,0:T(8,128)(2,1)S(1)}, u32[]{:S(2)}, u32[]{:S(2)}) async-start(bf16[4,289,128]{2,1,0:T(8,128)(2,1)} %broadcast_in_dim.16), calls=%async_computation.2 | async-start | bytes 606208 | tf_op jit(solution)/shard_map/all_to_all | solution.py:82
  9.3 9.6 %all-to-all-done.2 = bf16[4,289,128]{2,1,0:T(8,128)(2,1)S(1)} async-done(((bf16[4,289,128]{2,1,0:T(8,128)(2,1)}), bf16[4,289,128]{2,1,0:T(8,128)(2,1)S(1)}, u32[]{:S(2)}, u32[]{:S(2)}) %all-to-all-start.2) | async-done | bytes 295968 | tf_op jit(solution)/shard_map/all_to_all | solution.py:82
  19.5 3.3 %all-to-all-start = ((bf16[4,145,128]{2,1,0:T(8,128)(2,1)}), bf16[4,145,128]{2,1,0:T(8,128)(2,1)S(1)}, u32[]{:S(2)}, u32[]{:S(2)}) async-start(bf16[4,145,128]{2,1,0:T(8,128)(2,1)} %broadcast_in_dim.13), calls=%async_computation | async-start | bytes 311296 | tf_op jit(solution)/shard_map/all_to_all | solution.py:82
  23.0 5.8 %all-to-all-done = bf16[4,145,128]{2,1,0:T(8,128)(2,1)S(1)} async-done(((bf16[4,145,128]{2,1,0:T(8,128)(2,1)}), bf16[4,145,128]{2,1,0:T(8,128)(2,1)S(1)}, u32[]{:S(2)}, u32[]{:S(2)}) %all-to-all-start) | async-done | bytes 148512 | tf_op jit(solution)/shard_map/all_to_all | solution.py:82
  30.2 3.7 %all-to-all-start.3 = ((bf16[4,4,289,128]{3,1,2,0:T(4,128)(2,1)}), bf16[4,4,289,128]{3,1,2,0:T(4,128)(2,1)S(1)}, u32[]{:S(2)}, u32[]{:S(2)}) async-start(bf16[4,4,289,128]{3,1,2,0:T(4,128)(2,1)} %broadcast_in_dim.17), calls=%async_computation.3 | async-start | bytes 2367488 | tf_op jit(solution)/shard_map/all_to_all | solution.py:84
  34.0 12.2 %all-to-all-done.3 = bf16[4,4,289,128]{3,1,2,0:T(4,128)(2,1)S(1)} async-done(((bf16[4,4,289,128]{3,1,2,0:T(4,128)(2,1)}), bf16[4,4,289,128]{3,1,2,0:T(4,128)(2,1)S(1)}, u32[]{:S(2)}, u32[]{:S(2)}) %all-to-all-start.3) | async-done | bytes 1183776 | tf_op jit(solution)/shard_map/all_to_all | solution.py:84
  47.2 3.6 %all-to-all-start.1 = ((bf16[4,4,145,128]{3,1,2,0:T(4,128)(2,1)}), bf16[4,4,145,128]{3,1,2,0:T(4,128)(2,1)S(1)}, u32[]{:S(2)}, u32[]{:S(2)}) async-start(bf16[4,4,145,128]{3,1,2,0:T(4,128)(2,1)} %broadcast_in_dim.14), calls=%async_computation.1 | async-start | bytes 1187840 | tf_op jit(solution)/shard_map/all_to_all | solution.py:84
  51.1 7.7 %all-to-all-done.1 = bf16[4,4,145,128]{3,1,2,0:T(4,128)(2,1)S(1)} async-done(((bf16[4,4,145,128]{3,1,2,0:T(4,128)(2,1)}), bf16[4,4,145,128]{3,1,2,0:T(4,128)(2,1)S(1)}, u32[]{:S(2)}, u32[]{:S(2)}) %all-to-all-start.1) | async-done | bytes 593952 | tf_op jit(solution)/shard_map/all_to_all | solution.py:84
  60.8 3.2 %collective-permute-start = (bf16[112,896]{1,0:T(8,128)(2,1)S(1)}, bf16[112,896]{1,0:T(8,128)(2,1)S(1)}, u32[]{:S(2)}, u32[]{:S(2)}) collective-permute-start(bf16[112,896]{1,0:T(8,128)(2,1)S(1)} %get-tuple-element.43), channel_id=1, source_target_pairs={{0,1},{1,2},{2,3},{3,4},{4,5},{5,6},{6,7},{7,8},{8,9},{9,10},{10,1... | collective-permute-start | bytes 602120 | tf_op jit(solution)/shard_map/ppermute | solution.py:423
  69.4 5.9 %shard_map.93 = (f32[416,384]{1,0:T(8,128)}, bf16[416,384]{1,0:T(8,128)(2,1)S(1)}, bf16[416,384]{1,0:T(8,128)(2,1)S(1)}, bf16[416,384]{1,0:T(8,128)(2,1)S(1)}, b...) custom-call(s32[8]{0:T(128)S(1)} %stack.23.meta_ref, ...), custom_call_target="tpu_custom_call" | custom-call | flops 2000000000 | bytes 7253536 | tf_op jit(solution)/shard_map/pallas_call | solution.py:375
  76.5 2.5 %copy.37.other_ref = bf16[4,4,289,128]{3,2,1,0:T(8,128)(2,1)} copy(bf16[4,4,289,128]{3,1,2,0:T(4,128)(2,1)} %collective-permute-done.3) | data formatting | bytes 2367488 | tf_op jit(solution)/shard_map/ppermute | solution.py:74
  79.1 9.4 %shard_map.94 = (bf16[480,384]{1,0:T(8,128)(2,1)S(1)}, f32[416,384]{1,0:T(8,128)S(1)}, bf16[4,4,289,128]{3,2,1,0:T(8,128)(2,1)S(1)}, bf16[4,4,289,128]{3,2,1,0:T(8,128)(2,1)}) custom-call(s32[8]{0:T(128)S(1)} %stack.23.meta_ref, f32[416,384]{1,0:T(8,128)S(1)} %copy-done, bf16[416,384]{1,0:T(8,128)(2,1)S(1)} %get-tuple-element.23.cotangent_ref, ...), custom_call_target="tpu_custom_call" | custom-call | flops 4000000000 | bytes 6701088 | tf_op jit(solution)/shard_map/pallas_call | solution.py:375
  88.5 2.8 %copy.42 = bf16[4,4,289,128]{3,1,2,0:T(4,128)(2,1)} copy(bf16[4,4,289,128]{3,2,1,0:T(8,128)(2,1)} %get-tuple-element.39) | data formatting | bytes 2367488 | tf_op jit(solution)/shard_map/pallas_call | solution.py:375
  91.2 1.7 %collective-permute-start.7 = (bf16[4,4,289,128]{3,1,2,0:T(4,128)(2,1)}, bf16[4,4,289,128]{3,1,2,0:T(4,128)(2,1)}, u32[]{:S(2)}, u32[]{:S(2)}) collective-permute-start(bf16[4,4,289,128]{3,1,2,0:T(4,128)(2,1)} %copy.42), channel_id=1, source_target_pairs={{0,1},{1,0},{2,3},{3,2},{4,5},{5,4},{6,7},{7,6},{8,9},{9,8},{10,11... | collective-permute-start | bytes 3551240 | tf_op jit(solution)/shard_map/ppermute | solution.py:74
  92.9 9.4 %shard_map.95 = (f32[480,384]{1,0:T(8,128)S(1)}, bf16[4,4,145,128]{3,2,1,0:T(8,128)(2,1)S(1)}, bf16[4,4,145,128]{3,2,1,0:T(8,128)(2,1)S(1)}) custom-call(s32[8]{0:T(128)S(1)} %stack.23.meta_ref, f32[416,384]{1,0:T(8,128)S(1)} %get-tuple-element.25.grad_middle_ref, f32[8,128]{1,0:T(8,128)S(1)} %fusion.3.mask_ref, ...), custom_call_target="tpu_custom_call" | custom-call | flops 3000000000 | bytes 6811168 | tf_op jit(solution)/shard_map/pallas_call | solution.py:375
  102.7 2.0 %collective-permute-done.6 = bf16[4,4,145,128]{3,1,2,0:T(4,128)(2,1)S(1)} collective-permute-done((bf16[4,4,145,128]{3,1,2,0:T(4,128)(2,1)S(1)}, bf16[4,4,145,128]{3,1,2,0:T(4,128)(2,1)S(1)}, u32[]{:S(2)}, u32[]{:S(2)}) %collective-permute-start.6) | collective-permute-done | bytes 593952 | tf_op jit(solution)/shard_map/ppermute | solution.py:74
  105.9 4.5 %all-to-all-start.4 = ((bf16[4,4,145,128]{3,0,2,1:T(4,128)(2,1)}), bf16[4,4,145,128]{3,0,2,1:T(4,128)(2,1)S(1)}, u32[]{:S(2)}, u32[]{:S(2)}) async-start(bf16[4,4,145,128]{3,0,2,1:T(4,128)(2,1)} %copy.40), calls=%async_computation.4 | async-start | bytes 1187840 | tf_op jit(solution)/shard_map/all_to_all | solution.py:95
  113.6 5.9 %all-to-all-done.4 = bf16[4,4,145,128]{3,0,2,1:T(4,128)(2,1)S(1)} async-done(((bf16[4,4,145,128]{3,0,2,1:T(4,128)(2,1)}), bf16[4,4,145,128]{3,0,2,1:T(4,128)(2,1)S(1)}, u32[]{:S(2)}, u32[]{:S(2)}) %all-to-all-start.4) | async-done | bytes 593952 | tf_op jit(solution)/shard_map/all_to_all | solution.py:95
  119.5 3.5 %all-to-all-start.6 = ((bf16[4,4,289,128]{3,0,2,1:T(4,128)(2,1)}), bf16[4,4,289,128]{3,0,2,1:T(4,128)(2,1)S(1)}, u32[]{:S(2)}, u32[]{:S(2)}) async-start(bf16[4,4,289,128]{3,0,2,1:T(4,128)(2,1)} %copy.44), calls=%async_computation.6 | async-start | bytes 2367488 | tf_op jit(solution)/shard_map/all_to_all | solution.py:95
  124.1 13.4 %all-to-all-done.6 = bf16[4,4,289,128]{3,0,2,1:T(4,128)(2,1)S(1)} async-done(((bf16[4,4,289,128]{3,0,2,1:T(4,128)(2,1)}), bf16[4,4,289,128]{3,0,2,1:T(4,128)(2,1)S(1)}, u32[]{:S(2)}, u32[]{:S(2)}) %all-to-all-start.6) | async-done | bytes 1183776 | tf_op jit(solution)/shard_map/all_to_all | solution.py:95
  137.6 4.2 %all-to-all-start.5 = ((bf16[4,145,128]{2,1,0:T(8,128)(2,1)}), bf16[4,145,128]{2,1,0:T(8,128)(2,1)S(1)}, u32[]{:S(2)}, u32[]{:S(2)}) async-start(bf16[4,145,128]{2,1,0:T(8,128)(2,1)} %copy.41), calls=%async_computation.5 | async-start | bytes 311296 | tf_op jit(solution)/shard_map/all_to_all | solution.py:101
  143.9 3.0 %collective-permute-start.4 = (bf16[112,768]{1,0:T(8,128)(2,1)}, bf16[112,768]{1,0:T(8,128)(2,1)S(1)}, u32[]{:S(2)}, u32[]{:S(2)}) collective-permute-start(bf16[112,768]{1,0:T(8,128)(2,1)} %get-tuple-element.41), channel_id=1, source_target_pairs={{0,1},{1,2},{2,3},{3,4},{4,5},{5,6},{6,7},{7,8},{8,9},{9,10},{10,1... | collective-permute-start | bytes 516104 | tf_op jit(solution)/shard_map/ppermute | solution.py:494
  148.4 5.1 %all-to-all-start.7 = ((bf16[4,289,128]{2,1,0:T(8,128)(2,1)}), bf16[4,289,128]{2,1,0:T(8,128)(2,1)S(1)}, u32[]{:S(2)}, u32[]{:S(2)}) async-start(bf16[4,289,128]{2,1,0:T(8,128)(2,1)} %copy.45), calls=%async_computation.7 | async-start | bytes 606208 | tf_op jit(solution)/shard_map/all_to_all | solution.py:101
  155.8 8.7 %all-to-all-done.7 = bf16[4,289,128]{2,1,0:T(8,128)(2,1)S(1)} async-done(((bf16[4,289,128]{2,1,0:T(8,128)(2,1)}), bf16[4,289,128]{2,1,0:T(8,128)(2,1)S(1)}, u32[]{:S(2)}, u32[]{:S(2)}) %all-to-all-start.7) | async-done | bytes 295968 | tf_op jit(solution)/shard_map/all_to_all | solution.py:101
  (64 shorter events, 23.5 us)
Async XLA Ops:
  0.6 8.4 %copy-start.3 = (bf16[1,18560]{1,0:T(2,128)(2,1)S(1)}, bf16[1,18560]{1,0:T(2,128)(2,1)}, u32[]{:S(2)}) copy-start(bf16[1,18560]{1,0:T(2,128)(2,1)} %param.7) | copy-start | bytes 111364
  2.8 16.1 %all-to-all-start.2 = ((bf16[4,289,128]{2,1,0:T(8,128)(2,1)}), bf16[4,289,128]{2,1,0:T(8,128)(2,1)S(1)}, u32[]{:S(2)}, u32[]{:S(2)}) async-start(bf16[4,289,128]{2,1,0:T(8,128)(2,1)} %broadcast_in_dim.16), calls=%async_computation.2 | async-start | bytes 606208 | tf_op jit(solution)/shard_map/all_to_all | solution.py:82
  19.5 9.3 %all-to-all-start = ((bf16[4,145,128]{2,1,0:T(8,128)(2,1)}), bf16[4,145,128]{2,1,0:T(8,128)(2,1)S(1)}, u32[]{:S(2)}, u32[]{:S(2)}) async-start(bf16[4,145,128]{2,1,0:T(8,128)(2,1)} %broadcast_in_dim.13), calls=%async_computation | async-start | bytes 311296 | tf_op jit(solution)/shard_map/all_to_all | solution.py:82
  30.2 16.0 %all-to-all-start.3 = ((bf16[4,4,289,128]{3,1,2,0:T(4,128)(2,1)}), bf16[4,4,289,128]{3,1,2,0:T(4,128)(2,1)S(1)}, u32[]{:S(2)}, u32[]{:S(2)}) async-start(bf16[4,4,289,128]{3,1,2,0:T(4,128)(2,1)} %broadcast_in_dim.17), calls=%async_computation.3 | async-start | bytes 2367488 | tf_op jit(solution)/shard_map/all_to_all | solution.py:84
  33.9 17.0 %copy-start.4 = (s32[256]{0:T(256)S(1)}, s32[256]{0:T(256)}, u32[]{:S(2)}) copy-start(s32[256]{0:T(256)} %param.10) | copy-start | bytes 3076
  33.9 17.1 %copy-start.1 = (bf16[256,384]{1,0:T(8,128)(2,1)S(1)}, bf16[256,384]{1,0:T(8,128)(2,1)}, u32[]{:S(2)}) copy-start(bf16[256,384]{1,0:T(8,128)(2,1)} %param.11) | copy-start | bytes 589828
  33.9 17.1 %copy-start.2 = (bf16[256,384]{1,0:T(8,128)(2,1)S(1)}, bf16[256,384]{1,0:T(8,128)(2,1)}, u32[]{:S(2)}) copy-start(bf16[256,384]{1,0:T(8,128)(2,1)} %param.6) | copy-start | bytes 589828
  47.2 16.9 %copy-start.5 = (s32[256]{0:T(256)S(1)}, s32[256]{0:T(256)}, u32[]{:S(2)}) copy-start(s32[256]{0:T(256)} %param.9) | copy-start | bytes 3076
  47.2 11.6 %all-to-all-start.1 = ((bf16[4,4,145,128]{3,1,2,0:T(4,128)(2,1)}), bf16[4,4,145,128]{3,1,2,0:T(4,128)(2,1)S(1)}, u32[]{:S(2)}, u32[]{:S(2)}) async-start(bf16[4,4,145,128]{3,1,2,0:T(4,128)(2,1)} %broadcast_in_dim.14), calls=%async_computation.1 | async-start | bytes 1187840 | tf_op jit(solution)/shard_map/all_to_all | solution.py:84
  50.8 25.8 %collective-permute-start.3 = (bf16[4,4,289,128]{3,1,2,0:T(4,128)(2,1)S(1)}, bf16[4,4,289,128]{3,1,2,0:T(4,128)(2,1)}, u32[]{:S(2)}, u32[]{:S(2)}) collective-permute-start(bf16[4,4,289,128]{3,1,2,0:T(4,128)(2,1)S(1)} %all-to-all-done.3), channel_id=1, source_target_pairs={{0,1},{1,0},{2,3},{3,2},{4,5},{5,4},{6,7},{7,6},{8,9},{9,8},{10,11... | collective-permute-start | bytes 3551240 | tf_op jit(solution)/shard_map/ppermute | solution.py:74
  58.8 10.5 %collective-permute-start.2 = (bf16[4,4,145,128]{3,1,2,0:T(4,128)(2,1)S(1)}, bf16[4,4,145,128]{3,1,2,0:T(4,128)(2,1)S(1)}, u32[]{:S(2)}, u32[]{:S(2)}) collective-permute-start(bf16[4,4,145,128]{3,1,2,0:T(4,128)(2,1)S(1)} %all-to-all-done.1), channel_id=1, source_target_pairs={{0,1},{1,0},{2,3},{3,2},{4,5},{5,4},{6,7},{7,6},{8,9},{9,8},{10,11... | collective-permute-start | bytes 1781768 | tf_op jit(solution)/shard_map/ppermute | solution.py:74
  59.5 9.9 %collective-permute-start.1 = (bf16[112,896]{1,0:T(8,128)(2,1)}, bf16[112,896]{1,0:T(8,128)(2,1)S(1)}, u32[]{:S(2)}, u32[]{:S(2)}) collective-permute-start(bf16[112,896]{1,0:T(8,128)(2,1)} %get-tuple-element.42), channel_id=1, source_target_pairs={{1,0},{2,1},{3,2},{4,3},{5,4},{6,5},{7,6},{8,7},{9,8},{10,9},{11,1... | collective-permute-start | bytes 602120 | tf_op jit(solution)/shard_map/ppermute | solution.py:424
  60.8 8.7 %collective-permute-start = (bf16[112,896]{1,0:T(8,128)(2,1)S(1)}, bf16[112,896]{1,0:T(8,128)(2,1)S(1)}, u32[]{:S(2)}, u32[]{:S(2)}) collective-permute-start(bf16[112,896]{1,0:T(8,128)(2,1)S(1)} %get-tuple-element.43), channel_id=1, source_target_pairs={{0,1},{1,2},{2,3},{3,4},{4,5},{5,6},{6,7},{7,8},{8,9},{9,10},{10,1... | collective-permute-start | bytes 602120 | tf_op jit(solution)/shard_map/ppermute | solution.py:423
  76.5 2.5 %copy-start = (f32[416,384]{1,0:T(8,128)S(1)}, f32[416,384]{1,0:T(8,128)}, u32[]{:S(2)}) copy-start(f32[416,384]{1,0:T(8,128)} %get-tuple-element.22.middle_ref) | copy-start | bytes 1916932
  91.2 19.2 %collective-permute-start.7 = (bf16[4,4,289,128]{3,1,2,0:T(4,128)(2,1)}, bf16[4,4,289,128]{3,1,2,0:T(4,128)(2,1)}, u32[]{:S(2)}, u32[]{:S(2)}) collective-permute-start(bf16[4,4,289,128]{3,1,2,0:T(4,128)(2,1)} %copy.42), channel_id=1, source_target_pairs={{0,1},{1,0},{2,3},{3,2},{4,5},{5,4},{6,7},{7,6},{8,9},{9,8},{10,11... | collective-permute-start | bytes 3551240 | tf_op jit(solution)/shard_map/ppermute | solution.py:74
  102.6 2.1 %collective-permute-start.6 = (bf16[4,4,145,128]{3,1,2,0:T(4,128)(2,1)S(1)}, bf16[4,4,145,128]{3,1,2,0:T(4,128)(2,1)S(1)}, u32[]{:S(2)}, u32[]{:S(2)}) collective-permute-start(bf16[4,4,145,128]{3,1,2,0:T(4,128)(2,1)S(1)} %copy.38), channel_id=1, source_target_pairs={{0,1},{1,0},{2,3},{3,2},{4,5},{5,4},{6,7},{7,6},{8,9},{9,8},{10,11... | collective-permute-start | bytes 1781768 | tf_op jit(solution)/shard_map/ppermute | solution.py:74
  105.9 13.6 %all-to-all-start.4 = ((bf16[4,4,145,128]{3,0,2,1:T(4,128)(2,1)}), bf16[4,4,145,128]{3,0,2,1:T(4,128)(2,1)S(1)}, u32[]{:S(2)}, u32[]{:S(2)}) async-start(bf16[4,4,145,128]{3,0,2,1:T(4,128)(2,1)} %copy.40), calls=%async_computation.4 | async-start | bytes 1187840 | tf_op jit(solution)/shard_map/all_to_all | solution.py:95
  119.5 18.1 %all-to-all-start.6 = ((bf16[4,4,289,128]{3,0,2,1:T(4,128)(2,1)}), bf16[4,4,289,128]{3,0,2,1:T(4,128)(2,1)S(1)}, u32[]{:S(2)}, u32[]{:S(2)}) async-start(bf16[4,4,289,128]{3,0,2,1:T(4,128)(2,1)} %copy.44), calls=%async_computation.6 | async-start | bytes 2367488 | tf_op jit(solution)/shard_map/all_to_all | solution.py:95
  137.6 10.9 %all-to-all-start.5 = ((bf16[4,145,128]{2,1,0:T(8,128)(2,1)}), bf16[4,145,128]{2,1,0:T(8,128)(2,1)S(1)}, u32[]{:S(2)}, u32[]{:S(2)}) async-start(bf16[4,145,128]{2,1,0:T(8,128)(2,1)} %copy.41), calls=%async_computation.5 | async-start | bytes 311296 | tf_op jit(solution)/shard_map/all_to_all | solution.py:101
  142.6 11.0 %collective-permute-start.5 = (bf16[112,768]{1,0:T(8,128)(2,1)}, bf16[112,768]{1,0:T(8,128)(2,1)S(1)}, u32[]{:S(2)}, u32[]{:S(2)}) collective-permute-start(bf16[112,768]{1,0:T(8,128)(2,1)} %get-tuple-element.40), channel_id=1, source_target_pairs={{1,0},{2,1},{3,2},{4,3},{5,4},{6,5},{7,6},{8,7},{9,8},{10,9},{11,1... | collective-permute-start | bytes 516104 | tf_op jit(solution)/shard_map/ppermute | solution.py:493
  143.9 9.7 %collective-permute-start.4 = (bf16[112,768]{1,0:T(8,128)(2,1)}, bf16[112,768]{1,0:T(8,128)(2,1)S(1)}, u32[]{:S(2)}, u32[]{:S(2)}) collective-permute-start(bf16[112,768]{1,0:T(8,128)(2,1)} %get-tuple-element.41), channel_id=1, source_target_pairs={{0,1},{1,2},{2,3},{3,4},{4,5},{5,6},{6,7},{7,8},{8,9},{9,10},{10,1... | collective-permute-start | bytes 516104 | tf_op jit(solution)/shard_map/ppermute | solution.py:494
  148.4 16.0 %all-to-all-start.7 = ((bf16[4,289,128]{2,1,0:T(8,128)(2,1)}), bf16[4,289,128]{2,1,0:T(8,128)(2,1)S(1)}, u32[]{:S(2)}, u32[]{:S(2)}) async-start(bf16[4,289,128]{2,1,0:T(8,128)(2,1)} %copy.45), calls=%async_computation.7 | async-start | bytes 606208 | tf_op jit(solution)/shard_map/all_to_all | solution.py:101
where the time goes:
time: 166 us; the launch traced here: 165 us
  waiting for transfers between devices  65.4 us (39%)
  starting transfers between devices  45 us (27%)
  Pallas kernels  24.7 us (15%)
  local copies, waits for them, and re-layouts  17.9 us (11%)
  other arithmetic  8.17 us (5%)
  between operations  4.19 us (3%)
    pallas_call x3, Pallas kernels, call_kernel(): pl.pallas_call(kernel, out_shape=out_shapes, in_specs=specs, out_specs=[v...  24.7 us
    all_to_all x2, waiting for transfers between devices, gather_blocks(): lax.all_to_all(part, 'fsdp', 0, 0, axis_index_groups=chips, tiled=True)  19.9 us
    all_to_all x2, waiting for transfers between devices, add_chips(): lax.all_to_all(part, 'fsdp', 1, 1, axis_index_groups=chips, tiled=True)  19.3 us
    all_to_all x2, waiting for transfers between devices, gather_blocks(): lax.all_to_all(part, 'fsdp', 0, 0, axis_index_groups=columns, tiled=True)  15.4 us
    all_to_all x2, starting transfers between devices, gather_blocks(): lax.all_to_all(part, 'fsdp', 0, 0, axis_index_groups=columns, tiled=True)  9.66 us
    all_to_all x2, starting transfers between devices, add_columns(): lax.all_to_all(part, 'fsdp', 0, 0, axis_index_groups=columns, tiled=True)  9.33 us
    all_to_all x2, waiting for transfers between devices, add_columns(): lax.all_to_all(part, 'fsdp', 0, 0, axis_index_groups=columns, tiled=True)  8.69 us
    all_to_all x2, starting transfers between devices, add_chips(): lax.all_to_all(part, 'fsdp', 1, 1, axis_index_groups=chips, tiled=True)  8.02 us
  transfers between devices with their start and end apart: 16, of which 8 were waited for; matrix products, arithmetic and copies ran while one was open for 9% of the time, Pallas kernels for 9%

commit v1 on v0

--- a/solution.py
+++ b/solution.py
@@ -74,15 +74,21 @@
     return lax.ppermute(value, "fsdp", [(i, i ^ 1) for i in range(devices)])
 
 
-def gather_blocks(block, devices):
-    chips, columns = groups_of(devices)
+def rounded(amount, step):
+    return -(-amount // step) * step
+
+
+def as_rows(block):
     rows = block.shape[1] // LANES
-    depth = devices // (CORES * SQUARE)
-    part = jnp.broadcast_to(block.reshape(1, rows, LANES), (depth, rows, LANES))
-    part = lax.all_to_all(part, "fsdp", 0, 0, axis_index_groups=columns, tiled=True)
-    part = jnp.broadcast_to(part[None], (SQUARE, depth, rows, LANES))
-    part = lax.all_to_all(part, "fsdp", 0, 0, axis_index_groups=chips, tiled=True)
-    return (part, swap_cores(part, devices))
+    return jnp.pad(block.reshape(rows, LANES), ((0, rounded(rows, 8) - rows), (0, 0)))
+
+
+def exchange(part, groups):
+    return lax.all_to_all(part, "fsdp", 0, 0, axis_index_groups=groups, tiled=True)
+
+
+def gather_exchange(block, groups):
+    return exchange(jnp.broadcast_to(block[None], (len(groups[0]),) + block.shape), groups)
 
 
 def add_cores(keep, send, devices):
@@ -90,38 +96,37 @@
     return (keep.astype(f32) + other.astype(f32)).astype(bf16)
 
 
-def add_chips(part, devices):
-    chips, columns = groups_of(devices)
-    part = lax.all_to_all(part, "fsdp", 1, 1, axis_index_groups=chips, tiled=True)
-    return jnp.sum(part.astype(f32), axis=1).astype(bf16)
-
-
-def add_columns(part, devices):
-    chips, columns = groups_of(devices)
-    part = lax.all_to_all(part, "fsdp", 0, 0, axis_index_groups=columns, tiled=True)
-    return jnp.sum(part.astype(f32), axis=0).reshape(1, -1)
+def sum_exchange(part, groups):
+    return jnp.sum(exchange(part, groups).astype(f32), axis=0)
+
+
+def as_block(part, like):
+    width = like.shape[1]
+    return part.astype(f32)[: width // LANES].reshape(1, width)
 
 
 def lay_out_blocks(core, mine_ref, other_ref, flat_ref):
-    spots, depth, rows, lanes = mine_ref.shape
+    spots, depth, padded, lanes = mine_ref.shape
+    rows = flat_ref.shape[0] // (CORES * spots * depth)
     for layer in range(depth):
         for spot in range(spots):
             base = (layer * spots + spot) * CORES * rows
-            mine = mine_ref[spot, layer].astype(f32)
-            other = other_ref[spot, layer].astype(f32)
+            mine = mine_ref[spot, layer].astype(f32)[:rows]
+            other = other_ref[spot, layer].astype(f32)[:rows]
             flat_ref[base : base + rows] = jnp.where(core == 0, mine, other)
             flat_ref[base + rows : base + 2 * rows] = jnp.where(core == 0, other, mine)
 
 
 def cut_blocks(core, flat_ref, keep_ref, send_ref):
-    depth, spots, rows, lanes = keep_ref.shape
+    spots, depth, padded, lanes = keep_ref.shape
+    rows = flat_ref.shape[0] // (CORES * spots * depth)
     for layer in range(depth):
         for spot in range(spots):
             base = (layer * spots + spot) * CORES * rows
-            first = flat_ref[base : base + rows]
-            second = flat_ref[base + rows : base + 2 * rows]
-            keep_ref[layer, spot] = jnp.where(core == 0, first, second).astype(bf16)
-            send_ref[layer, spot] = jnp.where(core == 0, second, first).astype(bf16)
+            first = flat_ref[base : base + padded]
+            second = flat_ref[base + rows : base + rows + padded]
+            keep_ref[spot, layer] = jnp.where(core == 0, first, second).astype(bf16)
+            send_ref[spot, layer] = jnp.where(core == 0, second, first).astype(bf16)
 
 
 def read_vector(flat_ref, at, amount):
@@ -290,22 +295,14 @@
 
 
 def attend_back_kernel(
-    meta_ref, grad_middle_ref, mask_ref, inputs_ref, normed_ref, qkv_ref, probability_ref,
-    context_ref, classes_ref, w_qkv_ref, w_out_ref, gain_ref,
-    grad_inputs_ref, keep_ref, send_ref,
-    flat_ref, grad_qkv_ref, grad_context_ref,
+    meta_ref, grad_middle_ref, mask_ref, qkv_ref, probability_ref, context_ref, classes_ref,
+    w_out_ref,
+    grad_qkv_ref, grad_w_out_ref, grad_bias_out_ref, grad_table_ref,
+    grad_context_ref,
 ):
-    core = meta_ref[4]
-    window = grad_inputs_ref.shape[0]
-    grad_middle = grad_middle_ref[...]
-    grad_branch = grad_middle.astype(bf16)
-    grad_bias_out = jnp.sum(grad_branch.astype(f32), axis=0, keepdims=True)
-    write_vector(flat_ref, BIAS_OUT_AT, D_ROWS, grad_bias_out)
-    grad_w_out = dot_rows(context_ref[...], grad_branch)
-    for i in range(D_ROWS):
-        flat_ref[pl.ds(W_OUT_AT + i, D, stride=D_ROWS), :] = grad_w_out[
-            :, i * LANES : (i + 1) * LANES
-        ]
+    grad_branch = grad_middle_ref[...].astype(bf16)
+    grad_bias_out_ref[...] = jnp.sum(grad_branch.astype(f32), axis=0, keepdims=True)
+    grad_w_out_ref[...] = dot_rows(context_ref[...], grad_branch)
     grad_context_ref[...] = dot_cols(grad_branch, w_out_ref[...]).astype(bf16)
     grad_table = jnp.zeros((8, LANES), f32)
     for slot in range(2):
@@ -341,9 +338,24 @@
         sums_low = (sums - sums_high.astype(f32)).astype(bf16)
         classes = classes_ref[rows]
         grad_table = grad_table + dot(sums_high, classes) + dot(sums_low, classes)
+    grad_table_ref[...] = jnp.sum(grad_table * mask_ref[...], axis=0, keepdims=True)
+
+
+def inputs_back_kernel(
+    meta_ref, grad_middle_ref, inputs_ref, normed_ref, w_qkv_ref, gain_ref,
+    grad_qkv_ref, grad_w_out_ref, grad_bias_out_ref, grad_table_ref,
+    grad_inputs_ref, keep_ref, send_ref,
+    flat_ref,
+):
+    core = meta_ref[4]
+    window = grad_inputs_ref.shape[0]
     flat_ref[TABLE_AT:] = jnp.zeros((flat_ref.shape[0] - TABLE_AT, LANES), f32)
-    flat_ref[TABLE_AT : TABLE_AT + 1] = jnp.sum(grad_table * mask_ref[...], axis=0, keepdims=True)
-
+    flat_ref[TABLE_AT : TABLE_AT + 1] = grad_table_ref[...]
+    write_vector(flat_ref, BIAS_OUT_AT, D_ROWS, grad_bias_out_ref[...])
+    for i in range(D_ROWS):
+        flat_ref[pl.ds(W_OUT_AT + i, D, stride=D_ROWS), :] = grad_w_out_ref[
+            :, i * LANES : (i + 1) * LANES
+        ]
     grad_qkv = grad_qkv_ref[...]
     column_sums = jnp.sum(grad_qkv.astype(f32), axis=0, keepdims=True)
     write_vector(flat_ref, BIAS_QUERY_AT, D_ROWS, column_sums[:, :D])
@@ -360,7 +372,7 @@
     unit, inverse = normalise(inputs_ref[...].astype(f32))
     write_vector(flat_ref, GAIN_AT, D_ROWS, jnp.sum(grad_normed * unit, axis=0, keepdims=True))
     write_vector(flat_ref, SHIFT_AT, D_ROWS, jnp.sum(grad_normed, axis=0, keepdims=True))
-    grad_inputs = grad_middle + norm_back(grad_normed, unit, inverse, gain)
+    grad_inputs = grad_middle_ref[...] + norm_back(grad_normed, unit, inverse, gain)
     high = grad_inputs.astype(bf16)
     low_part = (grad_inputs - high.astype(f32)).astype(bf16)
     back = slot_mask(meta_ref, window, True)
@@ -409,24 +421,33 @@
 def shards(inputs, attn_blocks, mlp_blocks, image_id, bias_id, out_grad):
     token_rows = inputs.shape[0]
     devices = lax.axis_size("fsdp")
+    chips, columns = groups_of(devices)
     depth = devices // (CORES * SQUARE)
     window = token_rows + 2 * HALO
-    attn_rows = attn_blocks.shape[1] // LANES
-    mlp_rows = mlp_blocks.shape[1] // LANES
-    attn_mine, attn_other = gather_blocks(attn_blocks, devices)
+    attn_flat = devices * attn_blocks.shape[1] // LANES
+    mlp_flat = devices * mlp_blocks.shape[1] // LANES
+    barrier = lax.optimization_barrier
 
     lane = jnp.arange(LANES, dtype=jnp.int32)
     classes = ((lane // HEADS)[None, :] == bias_id[:, None]) & (lane < NB * HEADS)[None, :]
     tokens = jnp.concatenate([inputs, out_grad, classes.astype(bf16)], axis=1)
     up = [(i, i + 1) for i in range(devices - 1)]
     down = [(i + 1, i) for i in range(devices - 1)]
-    before = lax.ppermute(tokens[token_rows - HALO :], "fsdp", up)
-    after = lax.ppermute(tokens[:HALO], "fsdp", down)
     meta = plan_slots(image_id, devices)
     head = jnp.arange(8, dtype=jnp.int32)
     head_mask = ((lane % HEADS)[None, :] == head[:, None]) & (lane < NB * HEADS)[None, :]
     head_mask = head_mask.astype(f32)
-    mlp_mine, mlp_other = gather_blocks(mlp_blocks, devices)
+
+    mlp_column = lax.all_gather(as_rows(mlp_blocks), "fsdp", axis_index_groups=columns)
+    attn_column = gather_exchange(as_rows(attn_blocks), columns)
+    before = lax.ppermute(tokens[token_rows - HALO :], "fsdp", up)
+    after = lax.ppermute(tokens[:HALO], "fsdp", down)
+    attn_column, before, after = barrier((attn_column, before, after))
+    attn_mine = gather_exchange(attn_column, chips)
+    mlp_column, attn_mine = barrier((mlp_column, attn_mine))
+    mlp_mine = gather_exchange(mlp_column, chips)
+    attn_other = swap_cores(attn_mine, devices)
+    mlp_other = swap_cores(mlp_mine, devices)
 
     (
         middle, cotangent, inputs_span, normed, qkv, probability, context, classes_span,
@@ -446,49 +467,55 @@
             struct((D, D), bf16),
             struct((1, D), f32),
         ],
-        [pltpu.VMEM((devices * attn_rows, LANES), f32), pltpu.VMEM((window, WIDE), bf16)],
-        2 * 10**9,
+        [pltpu.VMEM((attn_flat, LANES), f32), pltpu.VMEM((window, WIDE), bf16)],
+        5 * 10**9,
         [meta, before, tokens, after, head_mask, attn_mine, attn_other],
     )
+    feed_blocks = struct((SQUARE, depth, mlp_column.shape[1], LANES), bf16)
     output, grad_middle, feed_keep, feed_send = call_kernel(
         feed_kernel,
+        [struct((window, D), bf16), struct((SPAN, D), f32), feed_blocks, feed_blocks],
         [
-            struct((window, D), bf16),
-            struct((SPAN, D), f32),
-            struct((depth, SQUARE, mlp_rows, LANES), bf16),
-            struct((depth, SQUARE, mlp_rows, LANES), bf16),
-        ],
-        [
-            pltpu.VMEM((devices * mlp_rows, LANES), f32),
+            pltpu.VMEM((mlp_flat + 8, LANES), f32),
             pltpu.VMEM((D, FF), bf16),
             pltpu.VMEM((FF, D), bf16),
             pltpu.VMEM((SPAN, D), bf16),
         ],
-        4 * 10**9,
+        9 * 10**9,
         [meta, middle, cotangent, mlp_mine, mlp_other],
     )
-    feed_part = add_chips(add_cores(feed_keep, feed_send, devices), devices)
-    grad_mlp = add_columns(feed_part, devices)
-    grad_inputs, attn_keep, attn_send = call_kernel(
+    feed_part = add_cores(feed_keep, feed_send, devices)
+    grad_qkv, grad_w_out, grad_bias_out, grad_table = call_kernel(
         attend_back_kernel,
         [
-            struct((window, D), f32),
-            struct((depth, SQUARE, attn_rows, LANES), bf16),
-            struct((depth, SQUARE, attn_rows, LANES), bf16),
+            struct((SPAN, 3 * D), bf16),
+            struct((D, D), f32),
+            struct((1, D), f32),
+            struct((1, LANES), f32),
         ],
+        [pltpu.VMEM((SPAN, D), bf16)],
+        5 * 10**9,
+        [meta, grad_middle, head_mask, qkv, probability, context, classes_span, w_out],
+    )
+    feed_part, grad_qkv = barrier((feed_part, grad_qkv))
+    feed_part = sum_exchange(feed_part, chips).astype(bf16)
+    attn_blocks_out = struct((SQUARE, depth, attn_column.shape[1], LANES), bf16)
+    grad_inputs, attn_keep, attn_send = call_kernel(
+        inputs_back_kernel,
+        [struct((window, D), f32), attn_blocks_out, attn_blocks_out],
+        [pltpu.VMEM((attn_flat + 8, LANES), f32)],
+        5 * 10**9,
         [
-            pltpu.VMEM((devices * attn_rows, LANES), f32),
-            pltpu.VMEM((SPAN, 3 * D), bf16),
-            pltpu.VMEM((SPAN, D), bf16),
-        ],
-        3 * 10**9,
-        [
-            meta, grad_middle, head_mask, inputs_span, normed, qkv, probability, context,
-            classes_span, w_qkv, w_out, gain,
+            meta, grad_middle, inputs_span, normed, w_qkv, gain,
+            grad_qkv, grad_w_out, grad_bias_out, grad_table,
         ],
     )
-    attn_part = add_chips(add_cores(attn_keep, attn_send, devices), devices)
-    grad_attn = add_columns(attn_part, devices)
+    attn_part = add_cores(attn_keep, attn_send, devices)
+    attn_part, feed_part = barrier((attn_part, feed_part))
+    feed_sum = lax.psum_scatter(feed_part, "fsdp", scatter_dimension=0, axis_index_groups=columns)
+    feed_sum = barrier(feed_sum)
+    attn_part = sum_exchange(attn_part, chips).astype(bf16)
+    attn_sum = sum_exchange(attn_part, columns)
     edges = jnp.concatenate([output, grad_inputs.astype(bf16)], axis=1)
     from_next = lax.ppermute(edges[:HALO], "fsdp", down)
     from_last = lax.ppermute(edges[window - HALO :], "fsdp", up)
@@ -497,7 +524,7 @@
     own = slice(HALO, HALO + token_rows)
     output = output[own] + extra[:, :D]
     grad_inputs = grad_inputs[own] + extra[:, D:].astype(f32)
-    return (output, grad_inputs, grad_attn, grad_mlp)
+    return (output, grad_inputs, as_block(attn_sum, attn_blocks), as_block(feed_sum, mlp_blocks))
 
 
 def solution(mesh):

time: 166 us -> 159 us (0.958)
  waiting for transfers between devices: 65.4 us -> 26 us
  blocking collectives: 0 us -> 31.7 us
  between operations: 4.19 us -> 17.5 us
  local copies, waits for them, and re-layouts: 17.9 us -> 5.04 us
  starting transfers between devices: 45 us -> 39.5 us
  other arithmetic: 8.17 us -> 12.6 us
    all_to_all x8 -> x5, waiting for transfers between devices: 63.3 us -> 12.9 us  [exchange(): lax.all_to_all(part, 'fsdp', 0, 0, axis_index_groups=groups, tiled=True)]
    all_gather x0 -> x1, blocking collectives: none -> 16.6 us  [shards(): lax.all_gather(as_rows(mlp_blocks), 'fsdp', axis_index_groups=columns)]
    all_to_all x0 -> x1, blocking collectives: none -> 15.1 us  [exchange(): lax.all_to_all(part, 'fsdp', 0, 0, axis_index_groups=groups, tiled=True)]
    unnamed x0 -> x2, waiting for transfers between devices: none -> 9.42 us
    all_to_all x8 -> x5, starting transfers between devices: 34.3 us -> 29.6 us  [exchange(): lax.all_to_all(part, 'fsdp', 0, 0, axis_index_groups=groups, tiled=True)]
    pallas_call x2 -> x0, local copies, waits for them, and re-layouts: 2.98 us -> none  [call_kernel(): pl.pallas_call(kernel, out_shape=out_shapes, in_specs=specs, out_specs=[v...]
    convert_element_type x2 -> x0, local copies, waits for them, and re-layouts: 2.78 us -> none  [add_cores(): return (keep.astype(f32) + other.astype(f32)).astype(bf16)]
    ppermute x2 -> x0, local copies, waits for them, and re-layouts: 2.62 us -> none  [swap_cores(): return lax.ppermute(value, 'fsdp', [(i, i ^ 1) for i in range(devices)])]
  transfers between devices with their start and end apart: 16 -> 14, of which waited for: 8 -> 6; matrix products, arithmetic and copies ran while one was open for 9% -> 6% of each run, Pallas kernels for 9% -> 10%
where the time goes in v1:
time: 159 us; the launch traced here: 158 us
  starting transfers between devices  39.5 us (25%)
  blocking collectives  31.7 us (20%)
  waiting for transfers between devices  26 us (16%)
  Pallas kernels  25.8 us (16%)
  between operations  17.5 us (11%)
  other arithmetic  12.6 us (8%)
  local copies, waits for them, and re-layouts  5.04 us (3%)
    all_to_all x5, starting transfers between devices, exchange(): lax.all_to_all(part, 'fsdp', 0, 0, axis_index_groups=groups, tiled=True)  29.6 us
    pallas_call x4, Pallas kernels, call_kernel(): pl.pallas_call(kernel, out_shape=out_shapes, in_specs=specs, out_specs=[v...  25.8 us
    all_gather x1, blocking collectives, shards(): lax.all_gather(as_rows(mlp_blocks), 'fsdp', axis_index_groups=columns)  16.6 us
    all_to_all x1, blocking collectives, exchange(): lax.all_to_all(part, 'fsdp', 0, 0, axis_index_groups=groups, tiled=True)  15.1 us
    all_to_all x5, waiting for transfers between devices, exchange(): lax.all_to_all(part, 'fsdp', 0, 0, axis_index_groups=groups, tiled=True)  12.9 us
    unnamed x2, waiting for transfers between devices  9.42 us
  transfers between devices with their start and end apart: 14, of which 6 were waited for; matrix products, arithmetic and copies ran while one was open for 6% of the time, Pallas kernels for 10%

profile of v1, /device:TPU:0, one launch (start us, length us, event | category | flops | bytes accessed | tf_op | source)
XLA Modules:
  0.0 158.1 jit_solution(17604347700866891695)
XLA Ops:
  7.2 1.1 reduce.2
  9.0 6.3 %all-to-all-start = ((bf16[4,152,128]{2,1,0:T(8,128)(2,1)}), bf16[4,152,128]{2,1,0:T(8,128)(2,1)S(1)}, u32[]{:S(2)}, u32[]{:S(2)}) async-start(bf16[4,152,128]{2,1,0:T(8,128)(2,1)} %broadcast_in_dim.6), calls=%async_computation | async-start | bytes 311296 | tf_op jit(solution)/shard_map/all_to_all | solution.py:87
  17.2 1.4 collective-permute-start.1
  18.6 3.0 %collective-permute-start = (bf16[112,896]{1,0:T(8,128)(2,1)S(1)}, bf16[112,896]{1,0:T(8,128)(2,1)S(1)}, u32[]{:S(2)}, u32[]{:S(2)}) collective-permute-start(bf16[112,896]{1,0:T(8,128)(2,1)S(1)} %get-tuple-element.69), channel_id=1, source_target_pairs={{0,1},{1,2},{2,3},{3,4},{4,5},{5,6},{6,7},{7,8},{8,9},{9,10},{10,1... | collective-permute-start | bytes 602120 | tf_op jit(solution)/shard_map/ppermute | solution.py:443
  23.6 8.1 %all-to-all-start.1 = ((bf16[4,4,152,128]{3,2,1,0:T(8,128)(2,1)}), bf16[4,4,152,128]{3,2,1,0:T(8,128)(2,1)S(1)}, u32[]{:S(2)}, u32[]{:S(2)}) async-start(bf16[4,4,152,128]{3,2,1,0:T(8,128)(2,1)} %broadcast_in_dim.7), calls=%async_computation.1 | async-start | bytes 1245184 | tf_op jit(solution)/shard_map/all_to_all | solution.py:87
  32.2 16.6 %all-gather = bf16[1184,128]{1,0:T(8,128)(2,1)S(1)} all-gather(bf16[296,128]{1,0:T(8,128)(2,1)S(1)} %pad.11), channel_id=2, replica_groups={{0,8,16,24},{1,9,17,25},{2,10,18,26},{3,11,19,27},{4,12,20,28},{5,13,21..., dimensions={0}, use_global_device_ids=true | all-gather | bytes 378880 | tf_op jit(solution)/shard_map/all_gather | solution.py:441
  49.0 15.1 %all_to_all.30.mine_ref = bf16[4,4,296,128]{3,2,1,0:T(8,128)(2,1)} all-to-all(bf16[4,4,296,128]{3,2,1,0:T(8,128)(2,1)S(1)} %broadcast_in_dim.8), channel_id=1, replica_groups={{0,2,4,6},{1,3,5,7},{8,10,12,14},{9,11,13,15},{16,18,20,22},{17,19,21,2..., dimensions={0} | all-to-all | bytes 2424832 | tf_op jit(solution)/shard_map/all_to_all | solution.py:87
  65.1 1.3 fusion.4
  69.8 5.9 %shard_map.93 = (f32[416,384]{1,0:T(8,128)}, bf16[416,384]{1,0:T(8,128)(2,1)S(1)}, bf16[416,384]{1,0:T(8,128)(2,1)S(1)}, bf16[416,384]{1,0:T(8,128)(2,1)S(1)}, b...) custom-call(s32[8]{0:T(128)S(1)} %stack.23.meta_ref, ...), custom_call_target="tpu_custom_call" | custom-call | flops 5000000000 | bytes 7310880 | tf_op jit(solution)/shard_map/pallas_call | solution.py:387
  75.7 1.1 copy-done.2
  76.8 9.5 %shard_map.94 = (bf16[480,384]{1,0:T(8,128)(2,1)S(1)}, f32[416,384]{1,0:T(8,128)S(1)}, bf16[4,4,296,128]{3,2,1,0:T(8,128)(2,1)S(1)}, bf16[4,4,296,128]{3,2,1,0:T(8,128)(2,1)}) custom-call(s32[8]{0:T(128)S(1)} %stack.23.meta_ref, f32[416,384]{1,0:T(8,128)S(1)} %copy-done.2, bf16[416,384]{1,0:T(8,128)(2,1)S(1)} %get-tuple-element.40.cotangent_ref, ...), custom_call_target="tpu_custom_call" | custom-call | flops 8999999488 | bytes 6815776 | tf_op jit(solution)/shard_map/pallas_call | solution.py:387
  86.3 6.5 %shard_map.95 = (bf16[416,1152]{1,0:T(8,128)(2,1)S(1)}, f32[384,384]{1,0:T(8,128)S(1)}, f32[1,384]{1,0:T(1,128)S(1)}, f32[1,128]{1,0:T(1,128)S(1)}) custom-call(s32[8]{0:T(128)S(1)} %stack.23.meta_ref, f32[416,384]{1,0:T(8,128)S(1)} %get-tuple-element.43.grad_middle_ref, f32[8,128]{1,0:T(8,128)S(1)} %fusion.3.mask_ref, bf16[416,1152]{1,0:T(8,128)(2,1)S(1)} %copy-done.1, ...), custom_call_target="tpu_custom_call" | custom-call | flops 5000000000 | bytes 4911136 | tf_op jit(solution)/shard_map/pallas_call | solution.py:387
  92.8 1.3 add_convert_fusion
  94.2 4.3 %all-to-all-start.3 = ((bf16[4,4,296,128]{3,2,1,0:T(8,128)(2,1)}), bf16[4,4,296,128]{3,2,1,0:T(8,128)(2,1)}, u32[]{:S(2)}, u32[]{:S(2)}) async-start(bf16[4,4,296,128]{3,2,1,0:T(8,128)(2,1)} %add_convert_fusion), calls=%async_computation.3 | async-start | bytes 2424832 | tf_op jit(solution)/shard_map/all_to_all | solution.py:87
  98.4 3.9 %shard_map.96 = (f32[480,384]{1,0:T(8,128)S(1)}, bf16[4,4,152,128]{3,2,1,0:T(8,128)(2,1)S(1)}, bf16[4,4,152,128]{3,2,1,0:T(8,128)(2,1)S(1)}) custom-call(s32[8]{0:T(128)S(1)} %stack.23.meta_ref, f32[416,384]{1,0:T(8,128)S(1)} %get-tuple-element.43.grad_middle_ref, bf16[416,384]{1,0:T(8,128)(2,1)S(1)} %get-tuple-element.44.inputs_ref, ...), custom_call_target="tpu_custom_call" | custom-call | flops 5000000000 | bytes 5697056 | tf_op jit(solution)/shard_map/pallas_call | solution.py:387
  103.0 1.6 %collective-permute-done.7 = bf16[4,4,152,128]{3,2,1,0:T(8,128)(2,1)S(1)} collective-permute-done((bf16[4,4,152,128]{3,2,1,0:T(8,128)(2,1)S(1)}, bf16[4,4,152,128]{3,2,1,0:T(8,128)(2,1)S(1)}, u32[]{:S(2)}, u32[]{:S(2)}) %collective-permute-start.7) | collective-permute-done | bytes 622624 | tf_op jit(solution)/shard_map/ppermute | solution.py:74
  105.7 9.2 %all-to-all-done.3 = bf16[4,4,296,128]{3,2,1,0:T(8,128)(2,1)} async-done(((bf16[4,4,296,128]{3,2,1,0:T(8,128)(2,1)}), bf16[4,4,296,128]{3,2,1,0:T(8,128)(2,1)}, u32[]{:S(2)}, u32[]{:S(2)}) %all-to-all-start.3) | async-done | bytes 1212448 | tf_op jit(solution)/shard_map/all_to_all | solution.py:87
  114.9 2.2 %reduce_sum.43 = bf16[4,296,128]{2,1,0:T(8,128)(2,1)} reduce(bf16[4,4,296,128]{3,2,1,0:T(8,128)(2,1)} %all-to-all-done.3, bf16[]{:T(256)} %constant.59.clone.1), dimensions={0}, to_apply=%region_1.2 | reduce | flops 454656 | bytes 1515522 | tf_op jit(solution)/shard_map/reduce_sum | solution.py:100
  117.1 3.5 %all-to-all-start.4 = ((bf16[4,4,152,128]{3,2,1,0:T(8,128)(2,1)}), bf16[4,4,152,128]{3,2,1,0:T(8,128)(2,1)S(1)}, u32[]{:S(2)}, u32[]{:S(2)}) async-start(bf16[4,4,152,128]{3,2,1,0:T(8,128)(2,1)} %add_convert_fusion.1), calls=%async_computation.4 | async-start | bytes 1245184 | tf_op jit(solution)/shard_map/all_to_all | solution.py:87
  120.7 1.3 collective-permute-start.6
  122.0 3.0 %collective-permute-start.5 = (bf16[112,768]{1,0:T(8,128)(2,1)S(1)}, bf16[112,768]{1,0:T(8,128)(2,1)S(1)}, u32[]{:S(2)}, u32[]{:S(2)}) collective-permute-start(bf16[112,768]{1,0:T(8,128)(2,1)S(1)} %get-tuple-element.67), channel_id=1, source_target_pairs={{0,1},{1,2},{2,3},{3,4},{4,5},{5,6},{6,7},{7,8},{8,9},{9,10},{10,1... | collective-permute-start | bytes 516104 | tf_op jit(solution)/shard_map/ppermute | solution.py:521
  126.8 3.7 %all-to-all-done.4 = bf16[4,4,152,128]{3,2,1,0:T(8,128)(2,1)S(1)} async-done(((bf16[4,4,152,128]{3,2,1,0:T(8,128)(2,1)}), bf16[4,4,152,128]{3,2,1,0:T(8,128)(2,1)S(1)}, u32[]{:S(2)}, u32[]{:S(2)}) %all-to-all-start.4) | async-done | bytes 622624 | tf_op jit(solution)/shard_map/all_to_all | solution.py:87
  131.3 7.4 %all-to-all-start.5 = ((bf16[4,152,128]{2,1,0:T(8,128)(2,1)}), bf16[4,152,128]{2,1,0:T(8,128)(2,1)S(1)}, u32[]{:S(2)}, u32[]{:S(2)}) async-start(bf16[4,152,128]{2,1,0:T(8,128)(2,1)} %reduce_sum.44), calls=%async_computation.5 | async-start | bytes 311296 | tf_op jit(solution)/shard_map/all_to_all | solution.py:87
  139.4 9.4 %reduce-scatter.4.cloned.1.call-done = bf16[1,296,128]{2,1,0:T(8,128)(2,1)} async-done(((bf16[4,296,128]{2,1,0:T(8,128)(2,1)}), bf16[1,296,128]{2,1,0:T(8,128)(2,1)}) %reduce-scatter.4.cloned.1.call-update) | async-done | bytes 75792
  (52 shorter events, 13.7 us)
Async XLA Ops:
  9.0 13.8 %all-to-all-start = ((bf16[4,152,128]{2,1,0:T(8,128)(2,1)}), bf16[4,152,128]{2,1,0:T(8,128)(2,1)S(1)}, u32[]{:S(2)}, u32[]{:S(2)}) async-start(bf16[4,152,128]{2,1,0:T(8,128)(2,1)} %broadcast_in_dim.6), calls=%async_computation | async-start | bytes 311296 | tf_op jit(solution)/shard_map/all_to_all | solution.py:87
  17.2 14.6 %copy-start.3 = (bf16[1,36992]{1,0:T(2,128)(2,1)S(1)}, bf16[1,36992]{1,0:T(2,128)(2,1)}, u32[]{:S(2)}) copy-start(bf16[1,36992]{1,0:T(2,128)(2,1)} %param.8) | copy-start | bytes 221956
  17.2 4.5 %collective-permute-start.1 = (bf16[112,896]{1,0:T(8,128)(2,1)S(1)}, bf16[112,896]{1,0:T(8,128)(2,1)S(1)}, u32[]{:S(2)}, u32[]{:S(2)}) collective-permute-start(bf16[112,896]{1,0:T(8,128)(2,1)S(1)} %get-tuple-element.68), channel_id=1, source_target_pairs={{1,0},{2,1},{3,2},{4,3},{5,4},{6,5},{7,6},{8,7},{9,8},{10,9},{11,1... | collective-permute-start | bytes 602120 | tf_op jit(solution)/shard_map/ppermute | solution.py:444
  18.6 4.1 %collective-permute-start = (bf16[112,896]{1,0:T(8,128)(2,1)S(1)}, bf16[112,896]{1,0:T(8,128)(2,1)S(1)}, u32[]{:S(2)}, u32[]{:S(2)}) collective-permute-start(bf16[112,896]{1,0:T(8,128)(2,1)S(1)} %get-tuple-element.69), channel_id=1, source_target_pairs={{0,1},{1,2},{2,3},{3,4},{4,5},{5,6},{6,7},{7,8},{8,9},{9,10},{10,1... | collective-permute-start | bytes 602120 | tf_op jit(solution)/shard_map/ppermute | solution.py:443
  23.6 25.2 %all-to-all-start.1 = ((bf16[4,4,152,128]{3,2,1,0:T(8,128)(2,1)}), bf16[4,4,152,128]{3,2,1,0:T(8,128)(2,1)S(1)}, u32[]{:S(2)}, u32[]{:S(2)}) async-start(bf16[4,4,152,128]{3,2,1,0:T(8,128)(2,1)} %broadcast_in_dim.7), calls=%async_computation.1 | async-start | bytes 1245184 | tf_op jit(solution)/shard_map/all_to_all | solution.py:87
  49.0 15.6 %copy-start.4 = (s32[256]{0:T(256)S(1)}, s32[256]{0:T(256)}, u32[]{:S(2)}) copy-start(s32[256]{0:T(256)} %param.9) | copy-start | bytes 3076
  64.1 11.6 %collective-permute-start.3 = (bf16[4,4,296,128]{3,2,1,0:T(8,128)(2,1)}, bf16[4,4,296,128]{3,2,1,0:T(8,128)(2,1)}, u32[]{:S(2)}, u32[]{:S(2)}) collective-permute-start(bf16[4,4,296,128]{3,2,1,0:T(8,128)(2,1)} %all_to_all.30.mine_ref), channel_id=1, source_target_pairs={{0,1},{1,0},{2,3},{3,2},{4,5},{5,4},{6,7},{7,6},{8,9},{9,8},{10,11... | collective-permute-start | bytes 3637256 | tf_op jit(solution)/shard_map/ppermute | solution.py:74
  64.1 5.7 %collective-permute-start.2 = (bf16[4,4,152,128]{3,2,1,0:T(8,128)(2,1)S(1)}, bf16[4,4,152,128]{3,2,1,0:T(8,128)(2,1)S(1)}, u32[]{:S(2)}, u32[]{:S(2)}) collective-permute-start(bf16[4,4,152,128]{3,2,1,0:T(8,128)(2,1)S(1)} %all-to-all-done.1.mine_ref), channel_id=1, source_target_pairs={{0,1},{1,0},{2,3},{3,2},{4,5},{5,4},{6,7},{7,6},{8,9},{9,8},{10,11... | collective-permute-start | bytes 1867784 | tf_op jit(solution)/shard_map/ppermute | solution.py:74
  75.7 1.1 copy-start.2
  76.8 9.5 %copy-start.1 = (bf16[416,1152]{1,0:T(8,128)(2,1)S(1)}, bf16[416,1152]{1,0:T(8,128)(2,1)}, u32[]{:S(2)}) copy-start(bf16[416,1152]{1,0:T(8,128)(2,1)} %get-tuple-element.50.qkv_ref) | copy-start | bytes 2875396
  86.3 6.5 %collective-permute-start.4 = (bf16[4,4,296,128]{3,2,1,0:T(8,128)(2,1)}, bf16[4,4,296,128]{3,2,1,0:T(8,128)(2,1)S(1)}, u32[]{:S(2)}, u32[]{:S(2)}) collective-permute-start(bf16[4,4,296,128]{3,2,1,0:T(8,128)(2,1)} %get-tuple-element.49), channel_id=1, source_target_pairs={{0,1},{1,0},{2,3},{3,2},{4,5},{5,4},{6,7},{7,6},{8,9},{9,8},{10,11... | collective-permute-start | bytes 3637256 | tf_op jit(solution)/shard_map/ppermute | solution.py:74
  92.8 1.4 copy-start
  94.2 20.7 %all-to-all-start.3 = ((bf16[4,4,296,128]{3,2,1,0:T(8,128)(2,1)}), bf16[4,4,296,128]{3,2,1,0:T(8,128)(2,1)}, u32[]{:S(2)}, u32[]{:S(2)}) async-start(bf16[4,4,296,128]{3,2,1,0:T(8,128)(2,1)} %add_convert_fusion), calls=%async_computation.3 | async-start | bytes 2424832 | tf_op jit(solution)/shard_map/all_to_all | solution.py:87
  102.4 2.3 %collective-permute-start.7 = (bf16[4,4,152,128]{3,2,1,0:T(8,128)(2,1)S(1)}, bf16[4,4,152,128]{3,2,1,0:T(8,128)(2,1)S(1)}, u32[]{:S(2)}, u32[]{:S(2)}) collective-permute-start(bf16[4,4,152,128]{3,2,1,0:T(8,128)(2,1)S(1)} %get-tuple-element.62), channel_id=1, source_target_pairs={{0,1},{1,0},{2,3},{3,2},{4,5},{5,4},{6,7},{7,6},{8,9},{9,8},{10,11... | collective-permute-start | bytes 1867784 | tf_op jit(solution)/shard_map/ppermute | solution.py:74
  117.1 13.4 %all-to-all-start.4 = ((bf16[4,4,152,128]{3,2,1,0:T(8,128)(2,1)}), bf16[4,4,152,128]{3,2,1,0:T(8,128)(2,1)S(1)}, u32[]{:S(2)}, u32[]{:S(2)}) async-start(bf16[4,4,152,128]{3,2,1,0:T(8,128)(2,1)} %add_convert_fusion.1), calls=%async_computation.4 | async-start | bytes 1245184 | tf_op jit(solution)/shard_map/all_to_all | solution.py:87
  120.6 28.2 %reduce-scatter.4.cloned.1.call-start = ((), (), s32[]{:S(2)}) async-start(), calls=%async_computation.7 | async-start | bytes 378880
  120.7 4.4 %collective-permute-start.6 = (bf16[112,768]{1,0:T(8,128)(2,1)S(1)}, bf16[112,768]{1,0:T(8,128)(2,1)S(1)}, u32[]{:S(2)}, u32[]{:S(2)}) collective-permute-start(bf16[112,768]{1,0:T(8,128)(2,1)S(1)} %get-tuple-element.66), channel_id=1, source_target_pairs={{1,0},{2,1},{3,2},{4,3},{5,4},{6,5},{7,6},{8,7},{9,8},{10,9},{11,1... | collective-permute-start | bytes 516104 | tf_op jit(solution)/shard_map/ppermute | solution.py:520
  122.0 4.1 %collective-permute-start.5 = (bf16[112,768]{1,0:T(8,128)(2,1)S(1)}, bf16[112,768]{1,0:T(8,128)(2,1)S(1)}, u32[]{:S(2)}, u32[]{:S(2)}) collective-permute-start(bf16[112,768]{1,0:T(8,128)(2,1)S(1)} %get-tuple-element.67), channel_id=1, source_target_pairs={{0,1},{1,2},{2,3},{3,4},{4,5},{5,6},{6,7},{7,8},{8,9},{9,10},{10,1... | collective-permute-start | bytes 516104 | tf_op jit(solution)/shard_map/ppermute | solution.py:521
  131.3 19.2 %all-to-all-start.5 = ((bf16[4,152,128]{2,1,0:T(8,128)(2,1)}), bf16[4,152,128]{2,1,0:T(8,128)(2,1)S(1)}, u32[]{:S(2)}, u32[]{:S(2)}) async-start(bf16[4,152,128]{2,1,0:T(8,128)(2,1)} %reduce_sum.44), calls=%async_computation.5 | async-start | bytes 311296 | tf_op jit(solution)/shard_map/all_to_all | solution.py:87
Sparse Core Ops, SparseCore 0:
  125.2 23.5 reduce-scatter.3

commit v2 on v1

--- a/solution.py
+++ b/solution.py
@@ -70,6 +70,11 @@
     return (chips, columns)
 
 
+def pass_column(value, step, devices):
+    inner = CORES * SQUARE
+    return lax.ppermute(value, "fsdp", [(i, i ^ (step * inner)) for i in range(devices)])
+
+
 def swap_cores(value, devices):
     return lax.ppermute(value, "fsdp", [(i, i ^ 1) for i in range(devices)])
 
@@ -127,6 +132,23 @@
             second = flat_ref[base + rows : base + rows + padded]
             keep_ref[spot, layer] = jnp.where(core == 0, first, second).astype(bf16)
             send_ref[spot, layer] = jnp.where(core == 0, second, first).astype(bf16)
+
+
+def spread_kernel(meta_ref, *refs):
+    spread_ref = refs[-1]
+    for step, part_ref in enumerate(refs[:-1]):
+        block = part_ref[...]
+        for spot in range(SQUARE):
+            spread_ref[spot, meta_ref[5] ^ step] = block
+
+
+def sum_chips_kernel(meta_ref, parts_ref, *out_refs):
+    for step, out_ref in enumerate(out_refs):
+        layer = meta_ref[5] ^ step
+        total = parts_ref[0, layer].astype(f32)
+        for spot in range(1, SQUARE):
+            total = total + parts_ref[spot, layer].astype(f32)
+        out_ref[...] = total.astype(bf16)
 
 
 def read_vector(flat_ref, at, amount):
@@ -294,63 +316,72 @@
     cut_blocks(core, flat_ref, keep_ref, send_ref)
 
 
+def slot_back(
+    slot, qkv_ref, probability_ref, classes_ref, grad_context_ref, grad_qkv_ref
+):
+    rows = slice(slot * SLOT, (slot + 1) * SLOT)
+    key_sums = []
+    for pair in range(HEADS // 2):
+        lanes = slice(pair * LANES, (pair + 1) * LANES)
+        key_lanes = slice(D + pair * LANES, D + (pair + 1) * LANES)
+        value_lanes = slice(2 * D + pair * LANES, 2 * D + (pair + 1) * LANES)
+        queries = qkv_ref[rows, lanes]
+        keys = qkv_ref[rows, key_lanes]
+        values = qkv_ref[rows, value_lanes]
+        grad_context = grad_context_ref[rows, lanes]
+        parts = []
+        for half in range(2):
+            head = 2 * pair + half
+            chosen = jnp.where(head_lanes(half), grad_context, jnp.zeros_like(grad_context))
+            grad_probs = dot_cols(chosen, values)
+            narrow = probability_ref[slot * HEADS + head]
+            probability = narrow.astype(f32)
+            weighted = probability * grad_probs
+            grad_scores = weighted - probability * jnp.sum(weighted, axis=-1, keepdims=True)
+            key_sums.append(jnp.sum(grad_scores, axis=0, keepdims=True))
+            grad_raw = (grad_scores * score_scale).astype(bf16)
+            parts.append(
+                (dot(grad_raw, keys), dot_rows(grad_raw, queries), dot_rows(narrow, grad_context))
+            )
+        low = head_lanes(0)
+        for where, first, second in zip((lanes, key_lanes, value_lanes), *parts):
+            grad_qkv_ref[:, where] = jnp.where(low, first, second).astype(bf16)
+    sums = jnp.concatenate(key_sums + [jnp.zeros((8 - HEADS, SLOT), f32)], axis=0)
+    sums_high = sums.astype(bf16)
+    sums_low = (sums - sums_high.astype(f32)).astype(bf16)
+    classes = classes_ref[rows]
+    return dot(sums_high, classes) + dot(sums_low, classes)
+
+
 def attend_back_kernel(
-    meta_ref, grad_middle_ref, mask_ref, qkv_ref, probability_ref, context_ref, classes_ref,
-    w_out_ref,
-    grad_qkv_ref, grad_w_out_ref, grad_bias_out_ref, grad_table_ref,
-    grad_context_ref,
+    meta_ref, grad_middle_ref, qkv_ref, probability_ref, context_ref, classes_ref, w_out_ref,
+    grad_qkv_ref, grad_w_out_ref, grad_bias_out_ref, grad_table_ref, grad_context_ref,
 ):
     grad_branch = grad_middle_ref[...].astype(bf16)
     grad_bias_out_ref[...] = jnp.sum(grad_branch.astype(f32), axis=0, keepdims=True)
     grad_w_out_ref[...] = dot_rows(context_ref[...], grad_branch)
     grad_context_ref[...] = dot_cols(grad_branch, w_out_ref[...]).astype(bf16)
-    grad_table = jnp.zeros((8, LANES), f32)
-    for slot in range(2):
-        rows = slice(slot * SLOT, (slot + 1) * SLOT)
-        key_sums = []
-        for pair in range(HEADS // 2):
-            lanes = slice(pair * LANES, (pair + 1) * LANES)
-            key_lanes = slice(D + pair * LANES, D + (pair + 1) * LANES)
-            value_lanes = slice(2 * D + pair * LANES, 2 * D + (pair + 1) * LANES)
-            queries = qkv_ref[rows, lanes]
-            keys = qkv_ref[rows, key_lanes]
-            values = qkv_ref[rows, value_lanes]
-            grad_context = grad_context_ref[rows, lanes]
-            parts = []
-            for half in range(2):
-                head = 2 * pair + half
-                chosen = jnp.where(head_lanes(half), grad_context, jnp.zeros_like(grad_context))
-                grad_probs = dot_cols(chosen, values)
-                narrow = probability_ref[slot * HEADS + head]
-                probability = narrow.astype(f32)
-                weighted = probability * grad_probs
-                grad_scores = weighted - probability * jnp.sum(weighted, axis=-1, keepdims=True)
-                key_sums.append(jnp.sum(grad_scores, axis=0, keepdims=True))
-                grad_raw = (grad_scores * score_scale).astype(bf16)
-                parts.append(
-                    (dot(grad_raw, keys), dot_rows(grad_raw, queries), dot_rows(narrow, grad_context))
-                )
-            low = head_lanes(0)
-            for where, first, second in zip((lanes, key_lanes, value_lanes), *parts):
-                grad_qkv_ref[rows, where] = jnp.where(low, first, second).astype(bf16)
-        sums = jnp.concatenate(key_sums + [jnp.zeros((8 - HEADS, SLOT), f32)], axis=0)
-        sums_high = sums.astype(bf16)
-        sums_low = (sums - sums_high.astype(f32)).astype(bf16)
-        classes = classes_ref[rows]
-        grad_table = grad_table + dot(sums_high, classes) + dot(sums_low, classes)
-    grad_table_ref[...] = jnp.sum(grad_table * mask_ref[...], axis=0, keepdims=True)
+    grad_table_ref[...] = slot_back(
+        0, qkv_ref, probability_ref, classes_ref, grad_context_ref, grad_qkv_ref
+    )
 
 
 def inputs_back_kernel(
-    meta_ref, grad_middle_ref, inputs_ref, normed_ref, w_qkv_ref, gain_ref,
-    grad_qkv_ref, grad_w_out_ref, grad_bias_out_ref, grad_table_ref,
+    meta_ref, grad_middle_ref, mask_ref, inputs_ref, normed_ref, qkv_ref, probability_ref,
+    classes_ref, w_qkv_ref, gain_ref,
+    grad_first_ref, grad_w_out_ref, grad_bias_out_ref, grad_table_ref, grad_context_ref,
     grad_inputs_ref, keep_ref, send_ref,
-    flat_ref,
+    flat_ref, grad_second_ref, grad_qkv_ref,
 ):
     core = meta_ref[4]
     window = grad_inputs_ref.shape[0]
+    grad_table = grad_table_ref[...] + slot_back(
+        1, qkv_ref, probability_ref, classes_ref, grad_context_ref, grad_second_ref
+    )
+    grad_qkv_ref[:SLOT] = grad_first_ref[...]
+    grad_qkv_ref[SLOT:] = grad_second_ref[...]
     flat_ref[TABLE_AT:] = jnp.zeros((flat_ref.shape[0] - TABLE_AT, LANES), f32)
-    flat_ref[TABLE_AT : TABLE_AT + 1] = grad_table_ref[...]
+    flat_ref[TABLE_AT : TABLE_AT + 1] = jnp.sum(grad_table * mask_ref[...], axis=0, keepdims=True)
     write_vector(flat_ref, BIAS_OUT_AT, D_ROWS, grad_bias_out_ref[...])
     for i in range(D_ROWS):
         flat_ref[pl.ds(W_OUT_AT + i, D, stride=D_ROWS), :] = grad_w_out_ref[
@@ -390,7 +421,7 @@
         in_specs=specs,
         out_specs=[vmem] * len(out_shapes),
         scratch_shapes=scratch,
-        compiler_params=pltpu.CompilerParams(vmem_limit_bytes=50 * 1024 * 1024),
+        compiler_params=pltpu.CompilerParams(vmem_limit_bytes=32 * 1024 * 1024),
         cost_estimate=pl.CostEstimate(flops=flops, bytes_accessed=moved, transcendentals=0),
     )(*operands)
 
@@ -409,8 +440,10 @@
     stop_two = jnp.where(has_next, jnp.minimum(stop_one + IMG, stop), stop_one)
     zero = jnp.zeros((), jnp.int32)
     return jnp.stack(
-        [start + HALO, stop_one - start, stop_one + HALO, stop_two - stop_one, device % CORES]
-        + [zero] * 3
+        [
+            start + HALO, stop_one - start, stop_one + HALO, stop_two - stop_one,
+            device % CORES, device // (CORES * SQUARE), zero, zero,
+        ]
     ).astype(jnp.int32)
 
 
@@ -438,14 +471,21 @@
     head_mask = ((lane % HEADS)[None, :] == head[:, None]) & (lane < NB * HEADS)[None, :]
     head_mask = head_mask.astype(f32)
 
-    mlp_column = lax.all_gather(as_rows(mlp_blocks), "fsdp", axis_index_groups=columns)
     attn_column = gather_exchange(as_rows(attn_blocks), columns)
     before = lax.ppermute(tokens[token_rows - HALO :], "fsdp", up)
     after = lax.ppermute(tokens[:HALO], "fsdp", down)
-    attn_column, before, after = barrier((attn_column, before, after))
+    mlp_rows = as_rows(mlp_blocks)
+    attn_column, before, after, meta, head_mask, mlp_rows = barrier(
+        (attn_column, before, after, meta, head_mask, mlp_rows)
+    )
     attn_mine = gather_exchange(attn_column, chips)
-    mlp_column, attn_mine = barrier((mlp_column, attn_mine))
-    mlp_mine = gather_exchange(mlp_column, chips)
+    mlp_parts = [mlp_rows] + [pass_column(mlp_rows, k, devices) for k in range(1, depth)]
+    (mlp_spread,) = call_kernel(
+        spread_kernel, [struct((SQUARE, depth) + mlp_rows.shape, bf16)], [], 10**6,
+        [meta] + mlp_parts,
+    )
+    mlp_spread, attn_mine = barrier((mlp_spread, attn_mine))
+    mlp_mine = exchange(mlp_spread, chips)
     attn_other = swap_cores(attn_mine, devices)
     mlp_other = swap_cores(mlp_mine, devices)
 
@@ -471,7 +511,7 @@
         5 * 10**9,
         [meta, before, tokens, after, head_mask, attn_mine, attn_other],
     )
-    feed_blocks = struct((SQUARE, depth, mlp_column.shape[1], LANES), bf16)
+    feed_blocks = struct((SQUARE, depth, mlp_rows.shape[0], LANES), bf16)
     output, grad_middle, feed_keep, feed_send = call_kernel(
         feed_kernel,
         [struct((window, D), bf16), struct((SPAN, D), f32), feed_blocks, feed_blocks],
@@ -485,36 +525,47 @@
         [meta, middle, cotangent, mlp_mine, mlp_other],
     )
     feed_part = add_cores(feed_keep, feed_send, devices)
-    grad_qkv, grad_w_out, grad_bias_out, grad_table = call_kernel(
+    grad_first, grad_w_out, grad_bias_out, grad_table, grad_context = call_kernel(
         attend_back_kernel,
         [
-            struct((SPAN, 3 * D), bf16),
+            struct((SLOT, 3 * D), bf16),
             struct((D, D), f32),
             struct((1, D), f32),
-            struct((1, LANES), f32),
+            struct((8, LANES), f32),
+            struct((SPAN, D), bf16),
         ],
-        [pltpu.VMEM((SPAN, D), bf16)],
-        5 * 10**9,
-        [meta, grad_middle, head_mask, qkv, probability, context, classes_span, w_out],
-    )
-    feed_part, grad_qkv = barrier((feed_part, grad_qkv))
-    feed_part = sum_exchange(feed_part, chips).astype(bf16)
+        [],
+        4 * 10**9,
+        [meta, grad_middle, qkv, probability, context, classes_span, w_out],
+    )
+    feed_part, grad_first = barrier((feed_part, grad_first))
+    feed_part = exchange(feed_part, chips)
     attn_blocks_out = struct((SQUARE, depth, attn_column.shape[1], LANES), bf16)
     grad_inputs, attn_keep, attn_send = call_kernel(
         inputs_back_kernel,
         [struct((window, D), f32), attn_blocks_out, attn_blocks_out],
-        [pltpu.VMEM((attn_flat + 8, LANES), f32)],
-        5 * 10**9,
         [
-            meta, grad_middle, inputs_span, normed, w_qkv, gain,
-            grad_qkv, grad_w_out, grad_bias_out, grad_table,
+            pltpu.VMEM((attn_flat + 8, LANES), f32),
+            pltpu.VMEM((SLOT, 3 * D), bf16),
+            pltpu.VMEM((SPAN, 3 * D), bf16),
+        ],
+        8 * 10**9,
+        [
+            meta, grad_middle, head_mask, inputs_span, normed, qkv, probability, classes_span,
+            w_qkv, gain, grad_first, grad_w_out, grad_bias_out, grad_table, grad_context,
         ],
     )
     attn_part = add_cores(attn_keep, attn_send, devices)
     attn_part, feed_part = barrier((attn_part, feed_part))
-    feed_sum = lax.psum_scatter(feed_part, "fsdp", scatter_dimension=0, axis_index_groups=columns)
-    feed_sum = barrier(feed_sum)
-    attn_part = sum_exchange(attn_part, chips).astype(bf16)
+    feed_sums = call_kernel(
+        sum_chips_kernel, [struct(mlp_rows.shape, bf16)] * depth, [], 10**6, [meta, feed_part]
+    )
+    attn_part = exchange(attn_part, chips)
+    feed_parts = [feed_sums[0]] + [
+        pass_column(feed_sums[k], k, devices) for k in range(1, depth)
+    ]
+    feed_sum = sum(part.astype(f32) for part in feed_parts)
+    attn_part = jnp.sum(attn_part.astype(f32), axis=0).astype(bf16)
     attn_sum = sum_exchange(attn_part, columns)
     edges = jnp.concatenate([output, grad_inputs.astype(bf16)], axis=1)
     from_next = lax.ppermute(edges[:HALO], "fsdp", down)

time: 159 us -> 133 us (0.84)
  between operations: 17.5 us -> 4.25 us
  blocking collectives: 31.7 us -> 19.5 us
  waiting for transfers between devices: 26 us -> 15.2 us
  local copies, waits for them, and re-layouts: 5.04 us -> 14.7 us
  starting transfers between devices: 39.5 us -> 45.9 us
  Pallas kernels: 25.8 us -> 22.2 us
  other arithmetic: 12.6 us -> 10.2 us
    all_gather x1 -> x0, blocking collectives: 16.6 us -> none  [shards(): lax.all_gather(as_rows(mlp_blocks), 'fsdp', axis_index_groups=columns)]
    ppermute x0 -> x6, starting transfers between devices: none -> 14.1 us  [pass_column(): lax.ppermute(value, 'fsdp', [(i, i ^ step * inner) for i in range(devices)])]
    unnamed x13 -> x43, local copies, waits for them, and re-layouts: 2.63 us -> 12.5 us
    unnamed x2 -> x0, waiting for transfers between devices: 9.42 us -> none
    all_to_all x5, starting transfers between devices: 29.6 us -> 22.1 us  [exchange(): lax.all_to_all(part, 'fsdp', 0, 0, axis_index_groups=groups, tiled=True)]
    all_to_all x5, waiting for transfers between devices: 12.9 us -> 5.65 us  [exchange(): lax.all_to_all(part, 'fsdp', 0, 0, axis_index_groups=groups, tiled=True)]
    ppermute x0 -> x6, waiting for transfers between devices: none -> 6.25 us  [pass_column(): lax.ppermute(value, 'fsdp', [(i, i ^ step * inner) for i in range(devices)])]
    all_to_all x1, blocking collectives: 15.1 us -> 19.5 us  [exchange(): lax.all_to_all(part, 'fsdp', 0, 0, axis_index_groups=groups, tiled=True)]
  transfers between devices with their start and end apart: 14 -> 19, of which waited for: 6 -> 4; matrix products, arithmetic and copies ran while one was open for 6% -> 7% of each run, Pallas kernels for 10% -> 11%
where the time goes in v2:
time: 133 us; the launch traced here: 132 us
  starting transfers between devices  45.9 us (35%)
  Pallas kernels  22.2 us (17%)
  blocking collectives  19.5 us (15%)
  waiting for transfers between devices  15.2 us (11%)
  local copies, waits for them, and re-layouts  14.7 us (11%)
  other arithmetic  10.2 us (8%)
  between operations  4.25 us (3%)
    pallas_call x6, Pallas kernels, call_kernel(): pl.pallas_call(kernel, out_shape=out_shapes, in_specs=specs, out_specs=[v...  22.2 us
    all_to_all x5, starting transfers between devices, exchange(): lax.all_to_all(part, 'fsdp', 0, 0, axis_index_groups=groups, tiled=True)  22.1 us
    all_to_all x1, blocking collectives, exchange(): lax.all_to_all(part, 'fsdp', 0, 0, axis_index_groups=groups, tiled=True)  19.5 us
    ppermute x6, starting transfers between devices, pass_column(): lax.ppermute(value, 'fsdp', [(i, i ^ step * inner) for i in range(devices)])  14.1 us
    unnamed x43, local copies, waits for them, and re-layouts  12.5 us
    ppermute x6, waiting for transfers between devices, pass_column(): lax.ppermute(value, 'fsdp', [(i, i ^ step * inner) for i in range(devices)])  6.25 us
    all_to_all x5, waiting for transfers between devices, exchange(): lax.all_to_all(part, 'fsdp', 0, 0, axis_index_groups=groups, tiled=True)  5.65 us
    ppermute x4, waiting for transfers between devices, swap_cores(): return lax.ppermute(value, 'fsdp', [(i, i ^ 1) for i in range(devices)])  3.28 us
  transfers between devices with their start and end apart: 19, of which 4 were waited for; matrix products, arithmetic and copies ran while one was open for 7% of the time, Pallas kernels for 11%

profile of v2, /device:TPU:0, one launch (start us, length us, event | category | flops | bytes accessed | tf_op | source)
XLA Modules:
  0.0 131.9 jit_solution(18280607696283410570)
XLA Ops:
  2.4 6.3 %all-to-all-start = ((bf16[4,152,128]{2,1,0:T(8,128)(2,1)}), bf16[4,152,128]{2,1,0:T(8,128)(2,1)S(1)}, u32[]{:S(2)}, u32[]{:S(2)}) async-start(bf16[4,152,128]{2,1,0:T(8,128)(2,1)} %broadcast_in_dim.4), calls=%async_computation | async-start | bytes 311296 | tf_op jit(solution)/shard_map/all_to_all | solution.py:92
  10.7 1.3 collective-permute-start.1
  12.0 3.0 %collective-permute-start = (bf16[112,896]{1,0:T(8,128)(2,1)S(1)}, bf16[112,896]{1,0:T(8,128)(2,1)S(1)}, u32[]{:S(2)}, u32[]{:S(2)}) collective-permute-start(bf16[112,896]{1,0:T(8,128)(2,1)S(1)} %get-tuple-element.85), channel_id=1, source_target_pairs={{0,1},{1,2},{2,3},{3,4},{4,5},{5,6},{6,7},{7,8},{8,9},{9,10},{10,1... | collective-permute-start | bytes 602120 | tf_op jit(solution)/shard_map/ppermute | solution.py:475
  15.6 1.3 fusion.4
  21.6 3.7 %all-to-all-start.1 = ((bf16[4,4,152,128]{3,2,1,0:T(8,128)(2,1)}), bf16[4,4,152,128]{3,2,1,0:T(8,128)(2,1)S(1)}, u32[]{:S(2)}, u32[]{:S(2)}) async-start(bf16[4,4,152,128]{3,2,1,0:T(8,128)(2,1)} %broadcast_in_dim.5), calls=%async_computation.1 | async-start | bytes 1245184 | tf_op jit(solution)/shard_map/all_to_all | solution.py:92
  25.3 5.7 %collective-permute-start.4 = (bf16[296,128]{1,0:T(8,128)(2,1)S(1)}, bf16[296,128]{1,0:T(8,128)(2,1)S(1)}, u32[]{:S(2)}, u32[]{:S(2)}) collective-permute-start(bf16[296,128]{1,0:T(8,128)(2,1)S(1)} %pad.11.refs_0_), channel_id=1, source_target_pairs={{0,24},{1,25},{2,26},{3,27},{4,28},{5,29},{6,30},{7,31},{8,16},{9,... | collective-permute-start | bytes 227336 | tf_op jit(solution)/shard_map/ppermute | solution.py:75
  31.7 2.3 %collective-permute-done.4.refs_3_ = bf16[296,128]{1,0:T(8,128)(2,1)S(1)} collective-permute-done((bf16[296,128]{1,0:T(8,128)(2,1)S(1)}, bf16[296,128]{1,0:T(8,128)(2,1)S(1)}, u32[]{:S(2)}, u32[]{:S(2)}) %collective-permute-start.4) | collective-permute-done | bytes 75808 | tf_op jit(solution)/shard_map/ppermute | solution.py:75
  34.0 3.9 %collective-permute-done.3.refs_2_ = bf16[296,128]{1,0:T(8,128)(2,1)S(1)} collective-permute-done((bf16[296,128]{1,0:T(8,128)(2,1)S(1)}, bf16[296,128]{1,0:T(8,128)(2,1)S(1)}, u32[]{:S(2)}, u32[]{:S(2)}) %collective-permute-start.3) | collective-permute-done | bytes 75808 | tf_op jit(solution)/shard_map/ppermute | solution.py:75
  38.7 19.5 %all_to_all.30.mine_ref = bf16[4,4,296,128]{3,2,1,0:T(8,128)(2,1)S(1)} all-to-all(bf16[4,4,296,128]{3,2,1,0:T(8,128)(2,1)S(1)} %shard_map.93), channel_id=1, replica_groups={{0,2,4,6},{1,3,5,7},{8,10,12,14},{9,11,13,15},{16,18,20,22},{17,19,21,2..., dimensions={0} | all-to-all | bytes 2424832 | tf_op jit(solution)/shard_map/all_to_all | solution.py:92
  58.6 3.3 %collective-permute-done.5.other_ref = bf16[4,4,152,128]{3,2,1,0:T(8,128)(2,1)S(1)} collective-permute-done((bf16[4,4,152,128]{3,2,1,0:T(8,128)(2,1)S(1)}, bf16[4,4,152,128]{3,2,1,0:T(8,128)(2,1)S(1)}, u32[]{:S(2)}, u32[]{:S(2)}) %collective-permute-start.5) | collective-permute-done | bytes 622624 | tf_op jit(solution)/shard_map/ppermute | solution.py:79
  61.9 4.5 %shard_map.94 = (f32[416,384]{1,0:T(8,128)S(1)}, bf16[416,384]{1,0:T(8,128)(2,1)S(1)}, bf16[416,384]{1,0:T(8,128)(2,1)S(1)}, bf16[416,384]{1,0:T(8,128)(2,1)S(1)...) custom-call(s32[8]{0:T(128)S(1)} %stack.27.meta_ref, ...), custom_call_target="tpu_custom_call" | custom-call | flops 5000000000 | bytes 7310880 | tf_op jit(solution)/shard_map/pallas_call | solution.py:418
  68.8 7.5 %shard_map.95 = (bf16[480,384]{1,0:T(8,128)(2,1)S(1)}, f32[416,384]{1,0:T(8,128)S(1)}, bf16[4,4,296,128]{3,2,1,0:T(8,128)(2,1)S(1)}, bf16[4,4,296,128]{3,2,1,0:T(8,128)(2,1)S(1)}) custom-call(s32[8]{0:T(128)S(1)} %stack.27.meta_ref, f32[416,384]{1,0:T(8,128)S(1)} %get-tuple-element.50.middle_ref, bf16[416,384]{1,0:T(8,128)(2,1)S(1)} %get-tuple-element.51.cotangent_ref, ...), custom_call_target="tpu_custom_call" | custom-call | flops 8999999488 | bytes 6815776 | tf_op jit(solution)/shard_map/pallas_call | solution.py:418
  76.5 3.5 %shard_map.96 = (bf16[208,1152]{1,0:T(8,128)(2,1)S(1)}, f32[384,384]{1,0:T(8,128)S(1)}, f32[1,384]{1,0:T(1,128)S(1)}, f32[8,128]{1,0:T(8,128)S(1)}, bf16[416,384]{1,0:T(8,128)(2,1)S(1)}) custom-call(s32[8]{0:T(128)S(1)} %stack.27.meta_ref, f32[416,384]{1,0:T(8,128)S(1)} %get-tuple-element.54.grad_middle_ref, ...), custom_call_target="tpu_custom_call" | custom-call | flops 4000000000 | bytes 4750880 | tf_op jit(solution)/shard_map/pallas_call | solution.py:418
  80.1 1.4 %add_convert_fusion = bf16[4,4,296,128]{3,2,1,0:T(8,128)(2,1)} fusion(bf16[4,4,296,128]{3,2,1,0:T(8,128)(2,1)S(1)} %collective-permute-done.7, bf16[4,4,296,128]{3,2,1,0:T(8,128)(2,1)S(1)} %get-tuple-element.62), kind=kLoop, calls=%fused_computation | loop fusion | flops 2424832 | bytes 3637248 | tf_op jit(solution)/shard_map/convert_element_type | solution.py:101
  81.5 3.7 %all-to-all-start.3 = ((bf16[4,4,296,128]{3,2,1,0:T(8,128)(2,1)}), bf16[4,4,296,128]{3,2,1,0:T(8,128)(2,1)S(1)}, u32[]{:S(2)}, u32[]{:S(2)}) async-start(bf16[4,4,296,128]{3,2,1,0:T(8,128)(2,1)} %add_convert_fusion), calls=%async_computation.3 | async-start | bytes 2424832 | tf_op jit(solution)/shard_map/all_to_all | solution.py:92
  85.2 1.3 copy-done.1
  93.8 5.3 %shard_map.97 = (f32[480,384]{1,0:T(8,128)S(1)}, bf16[4,4,152,128]{3,2,1,0:T(8,128)(2,1)S(1)}, bf16[4,4,152,128]{3,2,1,0:T(8,128)(2,1)S(1)}) custom-call(s32[8]{0:T(128)S(1)} %stack.27.meta_ref, f32[416,384]{1,0:T(8,128)S(1)} %copy-done.5, f32[8,128]{1,0:T(8,128)S(1)} %fusion.3.mask_ref, bf16[416,384]{1,0:T(8,128)(2,1)S(1)} %copy-done.15, ...), custom_call_target="tpu_custom_call" | custom-call | flops 8000000000 | bytes 7648288 | tf_op jit(solution)/shard_map/pallas_call | solution.py:418
  100.2 1.3 collective-permute-start.9
  101.5 3.0 %collective-permute-start.8 = (bf16[112,768]{1,0:T(8,128)(2,1)S(1)}, bf16[112,768]{1,0:T(8,128)(2,1)S(1)}, u32[]{:S(2)}, u32[]{:S(2)}) collective-permute-start(bf16[112,768]{1,0:T(8,128)(2,1)S(1)} %get-tuple-element.83), channel_id=1, source_target_pairs={{0,1},{1,2},{2,3},{3,4},{4,5},{5,6},{6,7},{7,8},{8,9},{9,10},{10,1... | collective-permute-start | bytes 516104 | tf_op jit(solution)/shard_map/ppermute | solution.py:572
  105.6 4.0 %all-to-all-start.4 = ((bf16[4,4,152,128]{3,2,1,0:T(8,128)(2,1)}), bf16[4,4,152,128]{3,2,1,0:T(8,128)(2,1)S(1)}, u32[]{:S(2)}, u32[]{:S(2)}) async-start(bf16[4,4,152,128]{3,2,1,0:T(8,128)(2,1)} %add_convert_fusion.1), calls=%async_computation.4 | async-start | bytes 1245184 | tf_op jit(solution)/shard_map/all_to_all | solution.py:92
  111.0 5.3 %collective-permute-start.11 = (bf16[296,128]{1,0:T(8,128)(2,1)S(1)}, bf16[296,128]{1,0:T(8,128)(2,1)S(1)}, u32[]{:S(2)}, u32[]{:S(2)}) collective-permute-start(bf16[296,128]{1,0:T(8,128)(2,1)S(1)} %get-tuple-element.79), channel_id=1, source_target_pairs={{0,8},{1,9},{2,10},{3,11},{4,12},{5,13},{6,14},{7,15},{8,0},{9,1},... | collective-permute-start | bytes 227336 | tf_op jit(solution)/shard_map/ppermute | solution.py:75
  116.4 2.3 %collective-permute-start.13 = (bf16[296,128]{1,0:T(8,128)(2,1)S(1)}, bf16[296,128]{1,0:T(8,128)(2,1)S(1)}, u32[]{:S(2)}, u32[]{:S(2)}) collective-permute-start(bf16[296,128]{1,0:T(8,128)(2,1)S(1)} %get-tuple-element.81), channel_id=1, source_target_pairs={{0,24},{1,25},{2,26},{3,27},{4,28},{5,29},{6,30},{7,31},{8,16},{9,... | collective-permute-start | bytes 227336 | tf_op jit(solution)/shard_map/ppermute | solution.py:75
  120.2 4.4 %all-to-all-start.5 = ((bf16[4,152,128]{2,1,0:T(8,128)(2,1)}), bf16[4,152,128]{2,1,0:T(8,128)(2,1)S(1)}, u32[]{:S(2)}, u32[]{:S(2)}) async-start(bf16[4,152,128]{2,1,0:T(8,128)(2,1)} %reduce_sum.31), calls=%async_computation.5 | async-start | bytes 311296 | tf_op jit(solution)/shard_map/all_to_all | solution.py:92
  125.5 5.6 %all-to-all-done.5 = bf16[4,152,128]{2,1,0:T(8,128)(2,1)S(1)} async-done(((bf16[4,152,128]{2,1,0:T(8,128)(2,1)}), bf16[4,152,128]{2,1,0:T(8,128)(2,1)S(1)}, u32[]{:S(2)}, u32[]{:S(2)}) %all-to-all-start.5) | async-done | bytes 155680 | tf_op jit(solution)/shard_map/all_to_all | solution.py:92
  (90 shorter events, 24.2 us)
Async XLA Ops:
  1.7 13.3 %copy-start.19 = (s32[256]{0:T(256)S(1)}, s32[256]{0:T(256)}, u32[]{:S(2)}) copy-start(s32[256]{0:T(256)} %param.9) | copy-start | bytes 3076
  1.7 18.4 %copy-start.18 = (bf16[1,36992]{1,0:T(2,128)(2,1)S(1)}, bf16[1,36992]{1,0:T(2,128)(2,1)}, u32[]{:S(2)}) copy-start(bf16[1,36992]{1,0:T(2,128)(2,1)} %param.8) | copy-start | bytes 221956
  2.4 18.3 %all-to-all-start = ((bf16[4,152,128]{2,1,0:T(8,128)(2,1)}), bf16[4,152,128]{2,1,0:T(8,128)(2,1)S(1)}, u32[]{:S(2)}, u32[]{:S(2)}) async-start(bf16[4,152,128]{2,1,0:T(8,128)(2,1)} %broadcast_in_dim.4), calls=%async_computation | async-start | bytes 311296 | tf_op jit(solution)/shard_map/all_to_all | solution.py:92
  10.7 10.0 %collective-permute-start.1 = (bf16[112,896]{1,0:T(8,128)(2,1)S(1)}, bf16[112,896]{1,0:T(8,128)(2,1)S(1)}, u32[]{:S(2)}, u32[]{:S(2)}) collective-permute-start(bf16[112,896]{1,0:T(8,128)(2,1)S(1)} %get-tuple-element.84), channel_id=1, source_target_pairs={{1,0},{2,1},{3,2},{4,3},{5,4},{6,5},{7,6},{8,7},{9,8},{10,9},{11,1... | collective-permute-start | bytes 602120 | tf_op jit(solution)/shard_map/ppermute | solution.py:476
  12.0 8.7 %collective-permute-start = (bf16[112,896]{1,0:T(8,128)(2,1)S(1)}, bf16[112,896]{1,0:T(8,128)(2,1)S(1)}, u32[]{:S(2)}, u32[]{:S(2)}) collective-permute-start(bf16[112,896]{1,0:T(8,128)(2,1)S(1)} %get-tuple-element.85), channel_id=1, source_target_pairs={{0,1},{1,2},{2,3},{3,4},{4,5},{5,6},{6,7},{7,8},{8,9},{9,10},{10,1... | collective-permute-start | bytes 602120 | tf_op jit(solution)/shard_map/ppermute | solution.py:475
  21.6 17.0 %all-to-all-start.1 = ((bf16[4,4,152,128]{3,2,1,0:T(8,128)(2,1)}), bf16[4,4,152,128]{3,2,1,0:T(8,128)(2,1)S(1)}, u32[]{:S(2)}, u32[]{:S(2)}) async-start(bf16[4,4,152,128]{3,2,1,0:T(8,128)(2,1)} %broadcast_in_dim.5), calls=%async_computation.1 | async-start | bytes 1245184 | tf_op jit(solution)/shard_map/all_to_all | solution.py:92
  25.3 8.6 %collective-permute-start.4 = (bf16[296,128]{1,0:T(8,128)(2,1)S(1)}, bf16[296,128]{1,0:T(8,128)(2,1)S(1)}, u32[]{:S(2)}, u32[]{:S(2)}) collective-permute-start(bf16[296,128]{1,0:T(8,128)(2,1)S(1)} %pad.11.refs_0_), channel_id=1, source_target_pairs={{0,24},{1,25},{2,26},{3,27},{4,28},{5,29},{6,30},{7,31},{8,16},{9,... | collective-permute-start | bytes 227336 | tf_op jit(solution)/shard_map/ppermute | solution.py:75
  31.0 6.9 %collective-permute-start.3 = (bf16[296,128]{1,0:T(8,128)(2,1)S(1)}, bf16[296,128]{1,0:T(8,128)(2,1)S(1)}, u32[]{:S(2)}, u32[]{:S(2)}) collective-permute-start(bf16[296,128]{1,0:T(8,128)(2,1)S(1)} %pad.11.refs_0_), channel_id=1, source_target_pairs={{0,16},{1,17},{2,18},{3,19},{4,20},{5,21},{6,22},{7,23},{8,24},{9,... | collective-permute-start | bytes 227336 | tf_op jit(solution)/shard_map/ppermute | solution.py:75
  31.0 6.9 %collective-permute-start.2 = (bf16[296,128]{1,0:T(8,128)(2,1)S(1)}, bf16[296,128]{1,0:T(8,128)(2,1)S(1)}, u32[]{:S(2)}, u32[]{:S(2)}) collective-permute-start(bf16[296,128]{1,0:T(8,128)(2,1)S(1)} %pad.11.refs_0_), channel_id=1, source_target_pairs={{0,8},{1,9},{2,10},{3,11},{4,12},{5,13},{6,14},{7,15},{8,0},{9,1},... | collective-permute-start | bytes 227336 | tf_op jit(solution)/shard_map/ppermute | solution.py:75
  58.1 10.6 %collective-permute-start.6 = (bf16[4,4,296,128]{3,2,1,0:T(8,128)(2,1)S(1)}, bf16[4,4,296,128]{3,2,1,0:T(8,128)(2,1)S(1)}, u32[]{:S(2)}, u32[]{:S(2)}) collective-permute-start(bf16[4,4,296,128]{3,2,1,0:T(8,128)(2,1)S(1)} %all_to_all.30.mine_ref), channel_id=1, source_target_pairs={{0,1},{1,0},{2,3},{3,2},{4,5},{5,4},{6,7},{7,6},{8,9},{9,8},{10,11... | collective-permute-start | bytes 3637256 | tf_op jit(solution)/shard_map/ppermute | solution.py:79
  58.1 3.8 %collective-permute-start.5 = (bf16[4,4,152,128]{3,2,1,0:T(8,128)(2,1)S(1)}, bf16[4,4,152,128]{3,2,1,0:T(8,128)(2,1)S(1)}, u32[]{:S(2)}, u32[]{:S(2)}) collective-permute-start(bf16[4,4,152,128]{3,2,1,0:T(8,128)(2,1)S(1)} %all-to-all-done.1.mine_ref), channel_id=1, source_target_pairs={{0,1},{1,0},{2,3},{3,2},{4,5},{5,4},{6,7},{7,6},{8,9},{9,8},{10,11... | collective-permute-start | bytes 1867784 | tf_op jit(solution)/shard_map/ppermute | solution.py:79
  68.7 7.7 %copy-start = (bf16[12,208,208]{2,1,0:T(8,128)(2,1)}, bf16[12,208,208]{2,1,0:T(8,128)(2,1)S(1)}, u32[]{:S(2)}) copy-start(bf16[12,208,208]{2,1,0:T(8,128)(2,1)S(1)} %get-tuple-element.58.probability_ref) | copy-start | bytes 3115012
  68.7 7.7 %copy-start.2 = (bf16[416,1152]{1,0:T(8,128)(2,1)}, bf16[416,1152]{1,0:T(8,128)(2,1)S(1)}, u32[]{:S(2)}) copy-start(bf16[416,1152]{1,0:T(8,128)(2,1)S(1)} %get-tuple-element.57.qkv_ref) | copy-start | bytes 2875396
  76.3 3.8 %copy-start.4 = (f32[416,384]{1,0:T(8,128)}, f32[416,384]{1,0:T(8,128)S(1)}, u32[]{:S(2)}) copy-start(f32[416,384]{1,0:T(8,128)S(1)} %get-tuple-element.54.grad_middle_ref) | copy-start | bytes 1916932
  76.3 3.8 %collective-permute-start.7 = (bf16[4,4,296,128]{3,2,1,0:T(8,128)(2,1)S(1)}, bf16[4,4,296,128]{3,2,1,0:T(8,128)(2,1)S(1)}, u32[]{:S(2)}, u32[]{:S(2)}) collective-permute-start(bf16[4,4,296,128]{3,2,1,0:T(8,128)(2,1)S(1)} %get-tuple-element.63), channel_id=1, source_target_pairs={{0,1},{1,0},{2,3},{3,2},{4,5},{5,4},{6,7},{7,6},{8,9},{9,8},{10,11... | collective-permute-start | bytes 3637256 | tf_op jit(solution)/shard_map/ppermute | solution.py:79
  81.5 24.1 %all-to-all-start.3 = ((bf16[4,4,296,128]{3,2,1,0:T(8,128)(2,1)}), bf16[4,4,296,128]{3,2,1,0:T(8,128)(2,1)S(1)}, u32[]{:S(2)}, u32[]{:S(2)}) async-start(bf16[4,4,296,128]{3,2,1,0:T(8,128)(2,1)} %add_convert_fusion), calls=%async_computation.3 | async-start | bytes 2424832 | tf_op jit(solution)/shard_map/all_to_all | solution.py:92
  99.0 5.5 %collective-permute-start.10 = (bf16[4,4,152,128]{3,2,1,0:T(8,128)(2,1)S(1)}, bf16[4,4,152,128]{3,2,1,0:T(8,128)(2,1)S(1)}, u32[]{:S(2)}, u32[]{:S(2)}) collective-permute-start(bf16[4,4,152,128]{3,2,1,0:T(8,128)(2,1)S(1)} %get-tuple-element.74), channel_id=1, source_target_pairs={{0,1},{1,0},{2,3},{3,2},{4,5},{5,4},{6,7},{7,6},{8,9},{9,8},{10,11... | collective-permute-start | bytes 1867784 | tf_op jit(solution)/shard_map/ppermute | solution.py:79
  100.2 9.3 %collective-permute-start.9 = (bf16[112,768]{1,0:T(8,128)(2,1)}, bf16[112,768]{1,0:T(8,128)(2,1)S(1)}, u32[]{:S(2)}, u32[]{:S(2)}) collective-permute-start(bf16[112,768]{1,0:T(8,128)(2,1)} %get-tuple-element.82), channel_id=1, source_target_pairs={{1,0},{2,1},{3,2},{4,3},{5,4},{6,5},{7,6},{8,7},{9,8},{10,9},{11,1... | collective-permute-start | bytes 516104 | tf_op jit(solution)/shard_map/ppermute | solution.py:571
  101.5 8.0 %collective-permute-start.8 = (bf16[112,768]{1,0:T(8,128)(2,1)S(1)}, bf16[112,768]{1,0:T(8,128)(2,1)S(1)}, u32[]{:S(2)}, u32[]{:S(2)}) collective-permute-start(bf16[112,768]{1,0:T(8,128)(2,1)S(1)} %get-tuple-element.83), channel_id=1, source_target_pairs={{0,1},{1,2},{2,3},{3,4},{4,5},{5,6},{6,7},{7,8},{8,9},{9,10},{10,1... | collective-permute-start | bytes 516104 | tf_op jit(solution)/shard_map/ppermute | solution.py:572
  105.6 13.9 %all-to-all-start.4 = ((bf16[4,4,152,128]{3,2,1,0:T(8,128)(2,1)}), bf16[4,4,152,128]{3,2,1,0:T(8,128)(2,1)S(1)}, u32[]{:S(2)}, u32[]{:S(2)}) async-start(bf16[4,4,152,128]{3,2,1,0:T(8,128)(2,1)} %add_convert_fusion.1), calls=%async_computation.4 | async-start | bytes 1245184 | tf_op jit(solution)/shard_map/all_to_all | solution.py:92
  111.0 13.6 %collective-permute-start.11 = (bf16[296,128]{1,0:T(8,128)(2,1)S(1)}, bf16[296,128]{1,0:T(8,128)(2,1)S(1)}, u32[]{:S(2)}, u32[]{:S(2)}) collective-permute-start(bf16[296,128]{1,0:T(8,128)(2,1)S(1)} %get-tuple-element.79), channel_id=1, source_target_pairs={{0,8},{1,9},{2,10},{3,11},{4,12},{5,13},{6,14},{7,15},{8,0},{9,1},... | collective-permute-start | bytes 227336 | tf_op jit(solution)/shard_map/ppermute | solution.py:75
  116.3 8.3 %collective-permute-start.12 = (bf16[296,128]{1,0:T(8,128)(2,1)S(1)}, bf16[296,128]{1,0:T(8,128)(2,1)S(1)}, u32[]{:S(2)}, u32[]{:S(2)}) collective-permute-start(bf16[296,128]{1,0:T(8,128)(2,1)S(1)} %get-tuple-element.80), channel_id=1, source_target_pairs={{0,16},{1,17},{2,18},{3,19},{4,20},{5,21},{6,22},{7,23},{8,24},{9,... | collective-permute-start | bytes 227336 | tf_op jit(solution)/shard_map/ppermute | solution.py:75
  116.4 8.2 %collective-permute-start.13 = (bf16[296,128]{1,0:T(8,128)(2,1)S(1)}, bf16[296,128]{1,0:T(8,128)(2,1)S(1)}, u32[]{:S(2)}, u32[]{:S(2)}) collective-permute-start(bf16[296,128]{1,0:T(8,128)(2,1)S(1)} %get-tuple-element.81), channel_id=1, source_target_pairs={{0,24},{1,25},{2,26},{3,27},{4,28},{5,29},{6,30},{7,31},{8,16},{9,... | collective-permute-start | bytes 227336 | tf_op jit(solution)/shard_map/ppermute | solution.py:75
  120.2 10.9 %all-to-all-start.5 = ((bf16[4,152,128]{2,1,0:T(8,128)(2,1)}), bf16[4,152,128]{2,1,0:T(8,128)(2,1)S(1)}, u32[]{:S(2)}, u32[]{:S(2)}) async-start(bf16[4,152,128]{2,1,0:T(8,128)(2,1)} %reduce_sum.31), calls=%async_computation.5 | async-start | bytes 311296 | tf_op jit(solution)/shard_map/all_to_all | solution.py:92
  (15 other events, 19.0 us)

commit v3 on v2

--- a/solution.py
+++ b/solution.py
@@ -59,24 +59,20 @@
     return lax.dot_general(left, right, (((1,), (1,)), ((), ())), preferred_element_type=f32)
 
 
-def groups_of(devices):
-    inner = CORES * SQUARE
-    chips = [
-        [base + CORES * spot + core for spot in range(SQUARE)]
-        for base in range(0, devices, inner)
-        for core in range(CORES)
-    ]
-    columns = [[base + inner * spot for spot in range(devices // inner)] for base in range(inner)]
-    return (chips, columns)
-
-
-def pass_column(value, step, devices):
-    inner = CORES * SQUARE
-    return lax.ppermute(value, "fsdp", [(i, i ^ (step * inner)) for i in range(devices)])
-
-
-def swap_cores(value, devices):
-    return lax.ppermute(value, "fsdp", [(i, i ^ 1) for i in range(devices)])
+def pass_on(value, step, devices):
+    return lax.ppermute(value, "fsdp", [(i, i ^ step) for i in range(devices)])
+
+
+def pass_cores(value, devices):
+    return pass_on(value, 1, devices)
+
+
+def pass_chips(parts, devices):
+    return [pass_on(part, q * CORES, devices) for q, part in enumerate(parts) if q]
+
+
+def pass_layers(parts, devices):
+    return [pass_on(part, k * CORES * SQUARE, devices) for k, part in enumerate(parts) if k]
 
 
 def rounded(amount, step):
@@ -88,66 +84,53 @@
     return jnp.pad(block.reshape(rows, LANES), ((0, rounded(rows, 8) - rows), (0, 0)))
 
 
-def exchange(part, groups):
-    return lax.all_to_all(part, "fsdp", 0, 0, axis_index_groups=groups, tiled=True)
-
-
-def gather_exchange(block, groups):
-    return exchange(jnp.broadcast_to(block[None], (len(groups[0]),) + block.shape), groups)
-
-
-def add_cores(keep, send, devices):
-    other = swap_cores(send, devices)
-    return (keep.astype(f32) + other.astype(f32)).astype(bf16)
-
-
-def sum_exchange(part, groups):
-    return jnp.sum(exchange(part, groups).astype(f32), axis=0)
-
-
 def as_block(part, like):
     width = like.shape[1]
     return part.astype(f32)[: width // LANES].reshape(1, width)
 
 
-def lay_out_blocks(core, mine_ref, other_ref, flat_ref):
-    spots, depth, padded, lanes = mine_ref.shape
-    rows = flat_ref.shape[0] // (CORES * spots * depth)
-    for layer in range(depth):
-        for spot in range(spots):
-            base = (layer * spots + spot) * CORES * rows
-            mine = mine_ref[spot, layer].astype(f32)[:rows]
-            other = other_ref[spot, layer].astype(f32)[:rows]
-            flat_ref[base : base + rows] = jnp.where(core == 0, mine, other)
-            flat_ref[base + rows : base + 2 * rows] = jnp.where(core == 0, other, mine)
-
-
-def cut_blocks(core, flat_ref, keep_ref, send_ref):
+def block_row(meta_ref, step, spot, layer, rows):
+    where = (meta_ref[5] ^ layer) * SQUARE + (meta_ref[6] ^ spot)
+    return (where * CORES + (meta_ref[4] ^ step)) * rows
+
+
+def lay_out_blocks(meta_ref, block_refs, flat_ref):
+    depth, padded, lanes = block_refs[0].shape
+    rows = flat_ref.shape[0] // (CORES * SQUARE * depth)
+    for index, block_ref in enumerate(block_refs):
+        step, spot = divmod(index, SQUARE)
+        for layer in range(depth):
+            base = block_row(meta_ref, step, spot, layer, rows)
+            flat_ref[pl.ds(base, rows), :] = block_ref[layer].astype(f32)[:rows]
+
+
+def cut_blocks(meta_ref, flat_ref, keep_ref, send_ref):
     spots, depth, padded, lanes = keep_ref.shape
     rows = flat_ref.shape[0] // (CORES * spots * depth)
-    for layer in range(depth):
+    for step, out_ref in enumerate((keep_ref, send_ref)):
         for spot in range(spots):
-            base = (layer * spots + spot) * CORES * rows
-            first = flat_ref[base : base + padded]
-            second = flat_ref[base + rows : base + rows + padded]
-            keep_ref[spot, layer] = jnp.where(core == 0, first, second).astype(bf16)
-            send_ref[spot, layer] = jnp.where(core == 0, second, first).astype(bf16)
-
-
-def spread_kernel(meta_ref, *refs):
-    spread_ref = refs[-1]
-    for step, part_ref in enumerate(refs[:-1]):
-        block = part_ref[...]
-        for spot in range(SQUARE):
-            spread_ref[spot, meta_ref[5] ^ step] = block
-
-
-def sum_chips_kernel(meta_ref, parts_ref, *out_refs):
-    for step, out_ref in enumerate(out_refs):
-        layer = meta_ref[5] ^ step
-        total = parts_ref[0, layer].astype(f32)
-        for spot in range(1, SQUARE):
-            total = total + parts_ref[spot, layer].astype(f32)
+            for layer in range(depth):
+                base = block_row(meta_ref, step, spot, layer, rows)
+                out_ref[spot, layer] = flat_ref[pl.ds(base, padded), :].astype(bf16)
+
+
+def pack_kernel(*refs):
+    for layer, part_ref in enumerate(refs[:-1]):
+        refs[-1][layer] = part_ref[...]
+
+
+def add_cores_kernel(keep_ref, other_ref, *out_refs):
+    for spot, out_ref in enumerate(out_refs):
+        total = keep_ref[spot].astype(f32) + other_ref[spot].astype(f32)
+        out_ref[...] = total.astype(bf16)
+
+
+def add_chips_kernel(*refs):
+    parts = refs[:SQUARE]
+    for layer, out_ref in enumerate(refs[SQUARE:]):
+        total = parts[0][layer].astype(f32)
+        for part_ref in parts[1:]:
+            total = total + part_ref[layer].astype(f32)
         out_ref[...] = total.astype(bf16)
 
 
@@ -196,14 +179,15 @@
 
 
 def attend_kernel(
-    meta_ref, before_ref, own_ref, after_ref, mask_ref, mine_ref, other_ref,
+    meta_ref, before_ref, own_ref, after_ref, mask_ref,
+    mine_0, mine_1, mine_2, mine_3, other_0, other_1, other_2, other_3,
     middle_ref, cotangent_ref, inputs_ref, normed_ref, qkv_ref, probability_ref,
     context_ref, classes_ref, w_qkv_ref, w_out_ref, gain_ref,
     flat_ref, window_ref,
 ):
-    core = meta_ref[4]
     window = window_ref.shape[0]
-    lay_out_blocks(core, mine_ref, other_ref, flat_ref)
+    block_refs = (mine_0, mine_1, mine_2, mine_3, other_0, other_1, other_2, other_3)
+    lay_out_blocks(meta_ref, block_refs, flat_ref)
     read_matrix(flat_ref, W_QKV_AT, D, QKV_ROWS, w_qkv_ref)
     read_matrix(flat_ref, W_OUT_AT, D, D_ROWS, w_out_ref)
     gain = read_vector(flat_ref, GAIN_AT, D_ROWS)
@@ -258,13 +242,14 @@
 
 
 def feed_kernel(
-    meta_ref, middle_ref, cotangent_ref, mine_ref, other_ref,
+    meta_ref, middle_ref, cotangent_ref,
+    mine_0, mine_1, mine_2, mine_3, other_0, other_1, other_2, other_3,
     output_ref, grad_middle_ref, keep_ref, send_ref,
     flat_ref, w_up_ref, w_down_ref, normed_ref,
 ):
-    core = meta_ref[4]
     window = output_ref.shape[0]
-    lay_out_blocks(core, mine_ref, other_ref, flat_ref)
+    block_refs = (mine_0, mine_1, mine_2, mine_3, other_0, other_1, other_2, other_3)
+    lay_out_blocks(meta_ref, block_refs, flat_ref)
     read_matrix(flat_ref, W_UP_AT, D, FF_ROWS, w_up_ref)
     read_matrix(flat_ref, W_DOWN_AT, FF, D_ROWS, w_down_ref)
     gain = read_vector(flat_ref, GAIN_AT, D_ROWS)
@@ -313,7 +298,7 @@
     write_vector(flat_ref, BIAS_DOWN_AT, D_ROWS, jnp.sum(grad_output, axis=0, keepdims=True))
     flat_ref[FEED_END:] = jnp.zeros((flat_ref.shape[0] - FEED_END, LANES), f32)
     grad_middle_ref[...] = grad_output + norm_back(grad, unit, inverse, gain)
-    cut_blocks(core, flat_ref, keep_ref, send_ref)
+    cut_blocks(meta_ref, flat_ref, keep_ref, send_ref)
 
 
 def slot_back(
@@ -373,7 +358,6 @@
     grad_inputs_ref, keep_ref, send_ref,
     flat_ref, grad_second_ref, grad_qkv_ref,
 ):
-    core = meta_ref[4]
     window = grad_inputs_ref.shape[0]
     grad_table = grad_table_ref[...] + slot_back(
         1, qkv_ref, probability_ref, classes_ref, grad_context_ref, grad_second_ref
@@ -408,12 +392,13 @@
     low_part = (grad_inputs - high.astype(f32)).astype(bf16)
     back = slot_mask(meta_ref, window, True)
     grad_inputs_ref[...] = dot(back, high) + dot(back, low_part)
-    cut_blocks(core, flat_ref, keep_ref, send_ref)
+    cut_blocks(meta_ref, flat_ref, keep_ref, send_ref)
 
 
 def call_kernel(kernel, out_shapes, scratch, flops, operands):
     vmem = pl.BlockSpec(memory_space=pltpu.VMEM)
-    specs = [pl.BlockSpec(memory_space=pltpu.SMEM)] + [vmem] * (len(operands) - 1)
+    smem = pl.BlockSpec(memory_space=pltpu.SMEM)
+    specs = [smem if operand.dtype == jnp.int32 else vmem for operand in operands]
     moved = sum(math.prod(o.shape) * o.dtype.itemsize for o in list(operands) + list(out_shapes))
     return pl.pallas_call(
         kernel,
@@ -442,19 +427,39 @@
     return jnp.stack(
         [
             start + HALO, stop_one - start, stop_one + HALO, stop_two - stop_one,
-            device % CORES, device // (CORES * SQUARE), zero, zero,
+            device % CORES, device // (CORES * SQUARE), (device // CORES) % SQUARE, zero,
         ]
     ).astype(jnp.int32)
 
 
 def struct(shape, kind):
     return jax.ShapeDtypeStruct(shape, kind)
+
+
+def gather_columns(rows, devices):
+    depth = devices // (CORES * SQUARE)
+    parts = [rows] + pass_layers([rows] * depth, devices)
+    return call_kernel(pack_kernel, [struct((depth,) + rows.shape, bf16)], [], 10**6, parts)[0]
+
+
+def gather_planes(column, devices):
+    return [column] + pass_chips([column] * SQUARE, devices)
+
+
+def add_cores(keep, send, devices):
+    parts = [struct(keep.shape[1:], bf16)] * SQUARE
+    return call_kernel(add_cores_kernel, parts, [], 10**6, [keep, pass_cores(send, devices)])
+
+
+def add_chips(parts, passed):
+    depth, padded, lanes = parts[0].shape
+    sums = [struct((padded, lanes), bf16)] * depth
+    return call_kernel(add_chips_kernel, sums, [], 10**6, [parts[0]] + passed)
 
 
 def shards(inputs, attn_blocks, mlp_blocks, image_id, bias_id, out_grad):
     token_rows = inputs.shape[0]
     devices = lax.axis_size("fsdp")
-    chips, columns = groups_of(devices)
     depth = devices // (CORES * SQUARE)
     window = token_rows + 2 * HALO
     attn_flat = devices * attn_blocks.shape[1] // LANES
@@ -471,23 +476,19 @@
     head_mask = ((lane % HEADS)[None, :] == head[:, None]) & (lane < NB * HEADS)[None, :]
     head_mask = head_mask.astype(f32)
 
-    attn_column = gather_exchange(as_rows(attn_blocks), columns)
+    attn_rows = as_rows(attn_blocks)
+    mlp_rows = as_rows(mlp_blocks)
+    attn_column = gather_columns(attn_rows, devices)
     before = lax.ppermute(tokens[token_rows - HALO :], "fsdp", up)
     after = lax.ppermute(tokens[:HALO], "fsdp", down)
-    mlp_rows = as_rows(mlp_blocks)
-    attn_column, before, after, meta, head_mask, mlp_rows = barrier(
-        (attn_column, before, after, meta, head_mask, mlp_rows)
-    )
-    attn_mine = gather_exchange(attn_column, chips)
-    mlp_parts = [mlp_rows] + [pass_column(mlp_rows, k, devices) for k in range(1, depth)]
-    (mlp_spread,) = call_kernel(
-        spread_kernel, [struct((SQUARE, depth) + mlp_rows.shape, bf16)], [], 10**6,
-        [meta] + mlp_parts,
-    )
-    mlp_spread, attn_mine = barrier((mlp_spread, attn_mine))
-    mlp_mine = exchange(mlp_spread, chips)
-    attn_other = swap_cores(attn_mine, devices)
-    mlp_other = swap_cores(mlp_mine, devices)
+    mlp_column = gather_columns(mlp_rows, devices)
+    attn_mine = gather_planes(attn_column, devices)
+    mlp_column, attn_mine, before, after, meta, head_mask = barrier(
+        (mlp_column, attn_mine, before, after, meta, head_mask)
+    )
+    mlp_mine = gather_planes(mlp_column, devices)
+    attn_other = [pass_cores(part, devices) for part in attn_mine]
+    mlp_other = [pass_cores(part, devices) for part in mlp_mine]
 
     (
         middle, cotangent, inputs_span, normed, qkv, probability, context, classes_span,
@@ -507,24 +508,24 @@
             struct((D, D), bf16),
             struct((1, D), f32),
         ],
-        [pltpu.VMEM((attn_flat, LANES), f32), pltpu.VMEM((window, WIDE), bf16)],
+        [pltpu.VMEM((attn_flat + 16, LANES), f32), pltpu.VMEM((window, WIDE), bf16)],
         5 * 10**9,
-        [meta, before, tokens, after, head_mask, attn_mine, attn_other],
-    )
-    feed_blocks = struct((SQUARE, depth, mlp_rows.shape[0], LANES), bf16)
+        [meta, before, tokens, after, head_mask] + attn_mine + attn_other,
+    )
+    feed_blocks = struct((SQUARE,) + mlp_column.shape, bf16)
     output, grad_middle, feed_keep, feed_send = call_kernel(
         feed_kernel,
         [struct((window, D), bf16), struct((SPAN, D), f32), feed_blocks, feed_blocks],
         [
-            pltpu.VMEM((mlp_flat + 8, LANES), f32),
+            pltpu.VMEM((mlp_flat + 16, LANES), f32),
             pltpu.VMEM((D, FF), bf16),
             pltpu.VMEM((FF, D), bf16),
             pltpu.VMEM((SPAN, D), bf16),
         ],
         9 * 10**9,
-        [meta, middle, cotangent, mlp_mine, mlp_other],
-    )
-    feed_part = add_cores(feed_keep, feed_send, devices)
+        [meta, middle, cotangent] + mlp_mine + mlp_other,
+    )
+    feed_parts = add_cores(feed_keep, feed_send, devices)
     grad_first, grad_w_out, grad_bias_out, grad_table, grad_context = call_kernel(
         attend_back_kernel,
         [
@@ -538,14 +539,14 @@
         4 * 10**9,
         [meta, grad_middle, qkv, probability, context, classes_span, w_out],
     )
-    feed_part, grad_first = barrier((feed_part, grad_first))
-    feed_part = exchange(feed_part, chips)
-    attn_blocks_out = struct((SQUARE, depth, attn_column.shape[1], LANES), bf16)
+    feed_parts, grad_first = barrier((feed_parts, grad_first))
+    feed_passed = pass_chips(feed_parts, devices)
+    attn_blocks_out = struct((SQUARE,) + attn_column.shape, bf16)
     grad_inputs, attn_keep, attn_send = call_kernel(
         inputs_back_kernel,
         [struct((window, D), f32), attn_blocks_out, attn_blocks_out],
         [
-            pltpu.VMEM((attn_flat + 8, LANES), f32),
+            pltpu.VMEM((attn_flat + 16, LANES), f32),
             pltpu.VMEM((SLOT, 3 * D), bf16),
             pltpu.VMEM((SPAN, 3 * D), bf16),
         ],
@@ -555,18 +556,14 @@
             w_qkv, gain, grad_first, grad_w_out, grad_bias_out, grad_table, grad_context,
         ],
     )
-    attn_part = add_cores(attn_keep, attn_send, devices)
-    attn_part, feed_part = barrier((attn_part, feed_part))
-    feed_sums = call_kernel(
-        sum_chips_kernel, [struct(mlp_rows.shape, bf16)] * depth, [], 10**6, [meta, feed_part]
-    )
-    attn_part = exchange(attn_part, chips)
-    feed_parts = [feed_sums[0]] + [
-        pass_column(feed_sums[k], k, devices) for k in range(1, depth)
-    ]
-    feed_sum = sum(part.astype(f32) for part in feed_parts)
-    attn_part = jnp.sum(attn_part.astype(f32), axis=0).astype(bf16)
-    attn_sum = sum_exchange(attn_part, columns)
+    attn_parts = add_cores(attn_keep, attn_send, devices)
+    attn_passed = pass_chips(attn_parts, devices)
+    feed_sums = add_chips(feed_parts, feed_passed)
+    feed_layers = [feed_sums[0]] + pass_layers(feed_sums, devices)
+    attn_sums = add_chips(attn_parts, attn_passed)
+    attn_layers = [attn_sums[0]] + pass_layers(attn_sums, devices)
+    feed_sum = sum(part.astype(f32) for part in feed_layers)
+    attn_sum = sum(part.astype(f32) for part in attn_layers)
     edges = jnp.concatenate([output, grad_inputs.astype(bf16)], axis=1)
     from_next = lax.ppermute(edges[:HALO], "fsdp", down)
     from_last = lax.ppermute(edges[window - HALO :], "fsdp", up)

time: 133 us -> 126 us (0.947)
  waiting for transfers between devices: 15.2 us -> 44.3 us
  blocking collectives: 19.5 us -> 0 us
  local copies, waits for them, and re-layouts: 14.7 us -> 2.86 us
  other arithmetic: 10.2 us -> 7.22 us
    ppermute x10 -> x34, waiting for transfers between devices: 9.54 us -> 44.3 us  [pass_on(): return lax.ppermute(value, 'fsdp', [(i, i ^ step) for i in range(devices)])]
    all_to_all x5 -> x0, starting transfers between devices: 22.1 us -> none  [exchange(): lax.all_to_all(part, 'fsdp', 0, 0, axis_index_groups=groups, tiled=True)]
    ppermute x10 -> x34, starting transfers between devices: 15.2 us -> 36.7 us  [pass_on(): return lax.ppermute(value, 'fsdp', [(i, i ^ step) for i in range(devices)])]
    all_to_all x1 -> x0, blocking collectives: 19.5 us -> none  [exchange(): lax.all_to_all(part, 'fsdp', 0, 0, axis_index_groups=groups, tiled=True)]
    unnamed x43 -> x4, local copies, waits for them, and re-layouts: 12.5 us -> 1.53 us
    all_to_all x5 -> x0, waiting for transfers between devices: 5.65 us -> none  [exchange(): lax.all_to_all(part, 'fsdp', 0, 0, axis_index_groups=groups, tiled=True)]
    convert_element_type x2 -> x0, other arithmetic: 2.41 us -> none  [add_cores(): return (keep.astype(f32) + other.astype(f32)).astype(bf16)]
    broadcast_in_dim x2 -> x0, local copies, waits for them, and re-layouts: 1.59 us -> none  [gather_exchange(): jnp.broadcast_to(block[None], (len(groups[0]),) + block.shape)]
  transfers between devices with their start and end apart: 19 -> 38, of which waited for: 4 -> 13; matrix products, arithmetic and copies ran while one was open for 7% -> 7% of each run, Pallas kernels for 11% -> 7%
where the time goes in v3:
time: 126 us; the launch traced here: 125 us
  starting transfers between devices  45.3 us (36%)
  waiting for transfers between devices  44.3 us (35%)
  Pallas kernels  21.3 us (17%)
  other arithmetic  7.22 us (6%)
  between operations  4.15 us (3%)
  local copies, waits for them, and re-layouts  2.86 us (2%)
    ppermute x34, waiting for transfers between devices, pass_on(): return lax.ppermute(value, 'fsdp', [(i, i ^ step) for i in range(devices)])  44.3 us
    ppermute x34, starting transfers between devices, pass_on(): return lax.ppermute(value, 'fsdp', [(i, i ^ step) for i in range(devices)])  36.7 us
    pallas_call x10, Pallas kernels, call_kernel(): pl.pallas_call(kernel, out_shape=out_shapes, in_specs=specs, out_specs=[v...  21.3 us
    ppermute x1, starting transfers between devices, shards(): before = lax.ppermute(tokens[token_rows - HALO:], 'fsdp', up)  3.04 us
    ppermute x1, starting transfers between devices, shards(): from_last = lax.ppermute(edges[window - HALO:], 'fsdp', up)  3.04 us
  transfers between devices with their start and end apart: 38, of which 13 were waited for; matrix products, arithmetic and copies ran while one was open for 7% of the time, Pallas kernels for 7%

profile of v3, /device:TPU:0, one launch (start us, length us, event | category | flops | bytes accessed | tf_op | source)
XLA Modules:
  0.0 125.2 jit_solution(2600770060547528718)
XLA Ops:
  1.7 5.1 %collective-permute-start.5 = (bf16[152,128]{1,0:T(8,128)(2,1)S(1)}, bf16[152,128]{1,0:T(8,128)(2,1)S(1)}, u32[]{:S(2)}, u32[]{:S(2)}) collective-permute-start(bf16[152,128]{1,0:T(8,128)(2,1)S(1)} %pad.11.refs_0_), channel_id=1, source_target_pairs={{0,24},{1,25},{2,26},{3,27},{4,28},{5,29},{6,30},{7,31},{8,16},{9,... | collective-permute-start | bytes 116744 | tf_op jit(solution)/shard_map/ppermute | solution.py:63
  8.8 3.8 %collective-permute-start.2 = (bf16[296,128]{1,0:T(8,128)(2,1)S(1)}, bf16[296,128]{1,0:T(8,128)(2,1)S(1)}, u32[]{:S(2)}, u32[]{:S(2)}) collective-permute-start(bf16[296,128]{1,0:T(8,128)(2,1)S(1)} %pad.10.refs_0_), channel_id=1, source_target_pairs={{0,24},{1,25},{2,26},{3,27},{4,28},{5,29},{6,30},{7,31},{8,16},{9,... | collective-permute-start | bytes 227336 | tf_op jit(solution)/shard_map/ppermute | solution.py:63
  22.4 3.0 %collective-permute-start.9 = (bf16[112,896]{1,0:T(8,128)(2,1)S(1)}, bf16[112,896]{1,0:T(8,128)(2,1)S(1)}, u32[]{:S(2)}, u32[]{:S(2)}) collective-permute-start(bf16[112,896]{1,0:T(8,128)(2,1)S(1)} %get-tuple-element.113), channel_id=1, source_target_pairs={{0,1},{1,2},{2,3},{3,4},{4,5},{5,6},{6,7},{7,8},{8,9},{9,10},{10,1... | collective-permute-start | bytes 602120 | tf_op jit(solution)/shard_map/ppermute | solution.py:482
  25.5 2.6 %collective-permute-start.8 = (bf16[4,152,128]{2,1,0:T(8,128)(2,1)S(1)}, bf16[4,152,128]{2,1,0:T(8,128)(2,1)S(1)}, u32[]{:S(2)}, u32[]{:S(2)}) collective-permute-start(bf16[4,152,128]{2,1,0:T(8,128)(2,1)S(1)} %shard_map.94.mine_0), channel_id=1, source_target_pairs={{0,6},{1,7},{2,4},{3,5},{4,2},{5,3},{6,0},{7,1},{8,14},{9,15},{10,... | collective-permute-start | bytes 466952 | tf_op jit(solution)/shard_map/ppermute | solution.py:63
  29.1 4.1 %collective-permute-done.8.mine_3 = bf16[4,152,128]{2,1,0:T(8,128)(2,1)S(1)} collective-permute-done((bf16[4,152,128]{2,1,0:T(8,128)(2,1)S(1)}, bf16[4,152,128]{2,1,0:T(8,128)(2,1)S(1)}, u32[]{:S(2)}, u32[]{:S(2)}) %collective-permute-start.8) | collective-permute-done | bytes 155680 | tf_op jit(solution)/shard_map/ppermute | solution.py:63
  33.1 3.7 %collective-permute-done.7.mine_2 = bf16[4,152,128]{2,1,0:T(8,128)(2,1)S(1)} collective-permute-done((bf16[4,152,128]{2,1,0:T(8,128)(2,1)S(1)}, bf16[4,152,128]{2,1,0:T(8,128)(2,1)S(1)}, u32[]{:S(2)}, u32[]{:S(2)}) %collective-permute-start.7) | collective-permute-done | bytes 155680 | tf_op jit(solution)/shard_map/ppermute | solution.py:63
  37.8 1.5 %collective-permute-start.17 = (bf16[4,296,128]{2,1,0:T(8,128)(2,1)S(1)}, bf16[4,296,128]{2,1,0:T(8,128)(2,1)S(1)}, u32[]{:S(2)}, u32[]{:S(2)}) collective-permute-start(bf16[4,296,128]{2,1,0:T(8,128)(2,1)S(1)} %shard_map.93.mine_0), channel_id=1, source_target_pairs={{0,6},{1,7},{2,4},{3,5},{4,2},{5,3},{6,0},{7,1},{8,14},{9,15},{10,... | collective-permute-start | bytes 909320 | tf_op jit(solution)/shard_map/ppermute | solution.py:63
  42.9 5.8 %collective-permute-done.17.mine_3 = bf16[4,296,128]{2,1,0:T(8,128)(2,1)S(1)} collective-permute-done((bf16[4,296,128]{2,1,0:T(8,128)(2,1)S(1)}, bf16[4,296,128]{2,1,0:T(8,128)(2,1)S(1)}, u32[]{:S(2)}, u32[]{:S(2)}) %collective-permute-start.17) | collective-permute-done | bytes 303136 | tf_op jit(solution)/shard_map/ppermute | solution.py:63
  48.7 6.0 %collective-permute-done.16.mine_2 = bf16[4,296,128]{2,1,0:T(8,128)(2,1)S(1)} collective-permute-done((bf16[4,296,128]{2,1,0:T(8,128)(2,1)S(1)}, bf16[4,296,128]{2,1,0:T(8,128)(2,1)S(1)}, u32[]{:S(2)}, u32[]{:S(2)}) %collective-permute-start.16) | collective-permute-done | bytes 303136 | tf_op jit(solution)/shard_map/ppermute | solution.py:63
  55.2 4.3 %shard_map.95 = (f32[416,384]{1,0:T(8,128)S(1)}, bf16[416,384]{1,0:T(8,128)(2,1)S(1)}, bf16[416,384]{1,0:T(8,128)(2,1)S(1)}, bf16[416,384]{1,0:T(8,128)(2,1)S(1)...) custom-call(s32[8]{0:T(128)S(1)} %stack.31.meta_ref, ...), custom_call_target="tpu_custom_call" | custom-call | flops 5000000000 | bytes 7310880 | tf_op jit(solution)/shard_map/pallas_call | solution.py:403
  59.6 7.5 %shard_map.96 = (bf16[480,384]{1,0:T(8,128)(2,1)S(1)}, f32[416,384]{1,0:T(8,128)S(1)}, bf16[4,4,296,128]{3,2,1,0:T(8,128)(2,1)S(1)}, bf16[4,4,296,128]{3,2,1,0:T(8,128)(2,1)S(1)}) custom-call(s32[8]{0:T(128)S(1)} %stack.31.meta_ref, f32[416,384]{1,0:T(8,128)S(1)} %get-tuple-element.65.middle_ref, bf16[416,384]{1,0:T(8,128)(2,1)S(1)} %get-tuple-element.66.cotangent_ref, ...), custom_call_target="tpu_custom_call" | custom-call | flops 8999999488 | bytes 6815776 | tf_op jit(solution)/shard_map/pallas_call | solution.py:403
  67.5 3.5 %shard_map.98 = (bf16[208,1152]{1,0:T(8,128)(2,1)S(1)}, f32[384,384]{1,0:T(8,128)S(1)}, f32[1,384]{1,0:T(1,128)S(1)}, f32[8,128]{1,0:T(8,128)S(1)}, bf16[416,384]{1,0:T(8,128)(2,1)S(1)}) custom-call(s32[8]{0:T(128)S(1)} %stack.31.meta_ref, f32[416,384]{1,0:T(8,128)S(1)} %get-tuple-element.69.grad_middle_ref, ...), custom_call_target="tpu_custom_call" | custom-call | flops 4000000000 | bytes 4750880 | tf_op jit(solution)/shard_map/pallas_call | solution.py:403
  71.3 5.3 %shard_map.99 = (f32[480,384]{1,0:T(8,128)S(1)}, bf16[4,4,152,128]{3,2,1,0:T(8,128)(2,1)S(1)}, bf16[4,4,152,128]{3,2,1,0:T(8,128)(2,1)S(1)}) custom-call(s32[8]{0:T(128)S(1)} %stack.31.meta_ref, f32[416,384]{1,0:T(8,128)S(1)} %get-tuple-element.69.grad_middle_ref, f32[8,128]{1,0:T(8,128)S(1)} %fusion.3.mask_ref, ...), custom_call_target="tpu_custom_call" | custom-call | flops 8000000000 | bytes 7648288 | tf_op jit(solution)/shard_map/pallas_call | solution.py:403
  78.2 3.0 %collective-permute-start.23 = (bf16[112,768]{1,0:T(8,128)(2,1)S(1)}, bf16[112,768]{1,0:T(8,128)(2,1)S(1)}, u32[]{:S(2)}, u32[]{:S(2)}) collective-permute-start(bf16[112,768]{1,0:T(8,128)(2,1)S(1)} %get-tuple-element.111), channel_id=1, source_target_pairs={{0,1},{1,2},{2,3},{3,4},{4,5},{5,6},{6,7},{7,8},{8,9},{9,10},{10,1... | collective-permute-start | bytes 516104 | tf_op jit(solution)/shard_map/ppermute | solution.py:569
  81.2 1.6 %collective-permute-start.32 = (bf16[4,296,128]{2,1,0:T(8,128)(2,1)S(1)}, bf16[4,296,128]{2,1,0:T(8,128)(2,1)S(1)}, u32[]{:S(2)}, u32[]{:S(2)}) collective-permute-start(bf16[4,296,128]{2,1,0:T(8,128)(2,1)S(1)} %get-tuple-element.103), channel_id=1, source_target_pairs={{0,2},{1,3},{2,0},{3,1},{4,6},{5,7},{6,4},{7,5},{8,10},{9,11},{10,... | collective-permute-start | bytes 909320 | tf_op jit(solution)/shard_map/ppermute | solution.py:63
  84.9 1.6 %collective-permute-start.26 = (bf16[4,152,128]{2,1,0:T(8,128)(2,1)S(1)}, bf16[4,152,128]{2,1,0:T(8,128)(2,1)S(1)}, u32[]{:S(2)}, u32[]{:S(2)}) collective-permute-start(bf16[4,152,128]{2,1,0:T(8,128)(2,1)S(1)} %get-tuple-element.95), channel_id=1, source_target_pairs={{0,2},{1,3},{2,0},{3,1},{4,6},{5,7},{6,4},{7,5},{8,10},{9,11},{10,... | collective-permute-start | bytes 466952 | tf_op jit(solution)/shard_map/ppermute | solution.py:63
  87.3 3.7 %collective-permute-done.32.refs_1_ = bf16[4,296,128]{2,1,0:T(8,128)(2,1)S(1)} collective-permute-done((bf16[4,296,128]{2,1,0:T(8,128)(2,1)S(1)}, bf16[4,296,128]{2,1,0:T(8,128)(2,1)S(1)}, u32[]{:S(2)}, u32[]{:S(2)}) %collective-permute-start.32) | collective-permute-done | bytes 303136 | tf_op jit(solution)/shard_map/ppermute | solution.py:63
  91.0 2.8 %collective-permute-done.33.refs_2_ = bf16[4,296,128]{2,1,0:T(8,128)(2,1)S(1)} collective-permute-done((bf16[4,296,128]{2,1,0:T(8,128)(2,1)S(1)}, bf16[4,296,128]{2,1,0:T(8,128)(2,1)S(1)}, u32[]{:S(2)}, u32[]{:S(2)}) %collective-permute-start.33) | collective-permute-done | bytes 303136 | tf_op jit(solution)/shard_map/ppermute | solution.py:63
  93.8 4.5 %collective-permute-done.34.refs_3_ = bf16[4,296,128]{2,1,0:T(8,128)(2,1)S(1)} collective-permute-done((bf16[4,296,128]{2,1,0:T(8,128)(2,1)S(1)}, bf16[4,296,128]{2,1,0:T(8,128)(2,1)S(1)}, u32[]{:S(2)}, u32[]{:S(2)}) %collective-permute-start.34) | collective-permute-done | bytes 303136 | tf_op jit(solution)/shard_map/ppermute | solution.py:63
  98.5 3.4 %collective-permute-start.35 = (bf16[296,128]{1,0:T(8,128)(2,1)S(1)}, bf16[296,128]{1,0:T(8,128)(2,1)S(1)}, u32[]{:S(2)}, u32[]{:S(2)}) collective-permute-start(bf16[296,128]{1,0:T(8,128)(2,1)S(1)} %get-tuple-element.107), channel_id=1, source_target_pairs={{0,8},{1,9},{2,10},{3,11},{4,12},{5,13},{6,14},{7,15},{8,0},{9,1},... | collective-permute-start | bytes 227336 | tf_op jit(solution)/shard_map/ppermute | solution.py:63
  101.9 3.5 %collective-permute-start.36 = (bf16[296,128]{1,0:T(8,128)(2,1)S(1)}, bf16[296,128]{1,0:T(8,128)(2,1)S(1)}, u32[]{:S(2)}, u32[]{:S(2)}) collective-permute-start(bf16[296,128]{1,0:T(8,128)(2,1)S(1)} %get-tuple-element.108), channel_id=1, source_target_pairs={{0,16},{1,17},{2,18},{3,19},{4,20},{5,21},{6,22},{7,23},{8,24},{9,... | collective-permute-start | bytes 227336 | tf_op jit(solution)/shard_map/ppermute | solution.py:63
  106.7 7.7 %collective-permute-done.27.refs_2_ = bf16[4,152,128]{2,1,0:T(8,128)(2,1)S(1)} collective-permute-done((bf16[4,152,128]{2,1,0:T(8,128)(2,1)S(1)}, bf16[4,152,128]{2,1,0:T(8,128)(2,1)S(1)}, u32[]{:S(2)}, u32[]{:S(2)}) %collective-permute-start.27) | collective-permute-done | bytes 155680 | tf_op jit(solution)/shard_map/ppermute | solution.py:63
  115.1 3.5 %collective-permute-start.30 = (bf16[152,128]{1,0:T(8,128)(2,1)S(1)}, bf16[152,128]{1,0:T(8,128)(2,1)S(1)}, u32[]{:S(2)}, u32[]{:S(2)}) collective-permute-start(bf16[152,128]{1,0:T(8,128)(2,1)S(1)} %get-tuple-element.100), channel_id=1, source_target_pairs={{0,16},{1,17},{2,18},{3,19},{4,20},{5,21},{6,22},{7,23},{8,24},{9,... | collective-permute-start | bytes 116744 | tf_op jit(solution)/shard_map/ppermute | solution.py:63
  121.0 3.4 %collective-permute-done.31 = bf16[152,128]{1,0:T(8,128)(2,1)S(1)} collective-permute-done((bf16[152,128]{1,0:T(8,128)(2,1)S(1)}, bf16[152,128]{1,0:T(8,128)(2,1)S(1)}, u32[]{:S(2)}, u32[]{:S(2)}) %collective-permute-start.31) | collective-permute-done | bytes 38944 | tf_op jit(solution)/shard_map/ppermute | solution.py:63
  (86 shorter events, 26.0 us)
Async XLA Ops:
  1.7 15.3 %collective-permute-start.5 = (bf16[152,128]{1,0:T(8,128)(2,1)S(1)}, bf16[152,128]{1,0:T(8,128)(2,1)S(1)}, u32[]{:S(2)}, u32[]{:S(2)}) collective-permute-start(bf16[152,128]{1,0:T(8,128)(2,1)S(1)} %pad.11.refs_0_), channel_id=1, source_target_pairs={{0,24},{1,25},{2,26},{3,27},{4,28},{5,29},{6,30},{7,31},{8,16},{9,... | collective-permute-start | bytes 116744 | tf_op jit(solution)/shard_map/ppermute | solution.py:63
  6.9 14.2 %collective-permute-start.4 = (bf16[152,128]{1,0:T(8,128)(2,1)S(1)}, bf16[152,128]{1,0:T(8,128)(2,1)S(1)}, u32[]{:S(2)}, u32[]{:S(2)}) collective-permute-start(bf16[152,128]{1,0:T(8,128)(2,1)S(1)} %pad.11.refs_0_), channel_id=1, source_target_pairs={{0,16},{1,17},{2,18},{3,19},{4,20},{5,21},{6,22},{7,23},{8,24},{9,... | collective-permute-start | bytes 116744 | tf_op jit(solution)/shard_map/ppermute | solution.py:63
  6.9 15.5 %collective-permute-start.3 = (bf16[152,128]{1,0:T(8,128)(2,1)S(1)}, bf16[152,128]{1,0:T(8,128)(2,1)S(1)}, u32[]{:S(2)}, u32[]{:S(2)}) collective-permute-start(bf16[152,128]{1,0:T(8,128)(2,1)S(1)} %pad.11.refs_0_), channel_id=1, source_target_pairs={{0,8},{1,9},{2,10},{3,11},{4,12},{5,13},{6,14},{7,15},{8,0},{9,1},... | collective-permute-start | bytes 116744 | tf_op jit(solution)/shard_map/ppermute | solution.py:63
  8.8 16.6 %collective-permute-start.2 = (bf16[296,128]{1,0:T(8,128)(2,1)S(1)}, bf16[296,128]{1,0:T(8,128)(2,1)S(1)}, u32[]{:S(2)}, u32[]{:S(2)}) collective-permute-start(bf16[296,128]{1,0:T(8,128)(2,1)S(1)} %pad.10.refs_0_), channel_id=1, source_target_pairs={{0,24},{1,25},{2,26},{3,27},{4,28},{5,29},{6,30},{7,31},{8,16},{9,... | collective-permute-start | bytes 227336 | tf_op jit(solution)/shard_map/ppermute | solution.py:63
  12.7 15.5 %collective-permute-start.1 = (bf16[296,128]{1,0:T(8,128)(2,1)S(1)}, bf16[296,128]{1,0:T(8,128)(2,1)S(1)}, u32[]{:S(2)}, u32[]{:S(2)}) collective-permute-start(bf16[296,128]{1,0:T(8,128)(2,1)S(1)} %pad.10.refs_0_), channel_id=1, source_target_pairs={{0,16},{1,17},{2,18},{3,19},{4,20},{5,21},{6,22},{7,23},{8,24},{9,... | collective-permute-start | bytes 227336 | tf_op jit(solution)/shard_map/ppermute | solution.py:63
  17.1 11.6 %collective-permute-start = (bf16[296,128]{1,0:T(8,128)(2,1)S(1)}, bf16[296,128]{1,0:T(8,128)(2,1)S(1)}, u32[]{:S(2)}, u32[]{:S(2)}) collective-permute-start(bf16[296,128]{1,0:T(8,128)(2,1)S(1)} %pad.10.refs_0_), channel_id=1, source_target_pairs={{0,8},{1,9},{2,10},{3,11},{4,12},{5,13},{6,14},{7,15},{8,0},{9,1},... | collective-permute-start | bytes 227336 | tf_op jit(solution)/shard_map/ppermute | solution.py:63
  21.1 15.9 %collective-permute-start.10 = (bf16[112,896]{1,0:T(8,128)(2,1)S(1)}, bf16[112,896]{1,0:T(8,128)(2,1)S(1)}, u32[]{:S(2)}, u32[]{:S(2)}) collective-permute-start(bf16[112,896]{1,0:T(8,128)(2,1)S(1)} %get-tuple-element.112), channel_id=1, source_target_pairs={{1,0},{2,1},{3,2},{4,3},{5,4},{6,5},{7,6},{8,7},{9,8},{10,9},{11,1... | collective-permute-start | bytes 602120 | tf_op jit(solution)/shard_map/ppermute | solution.py:483
  22.4 14.5 %collective-permute-start.9 = (bf16[112,896]{1,0:T(8,128)(2,1)S(1)}, bf16[112,896]{1,0:T(8,128)(2,1)S(1)}, u32[]{:S(2)}, u32[]{:S(2)}) collective-permute-start(bf16[112,896]{1,0:T(8,128)(2,1)S(1)} %get-tuple-element.113), channel_id=1, source_target_pairs={{0,1},{1,2},{2,3},{3,4},{4,5},{5,6},{6,7},{7,8},{8,9},{9,10},{10,1... | collective-permute-start | bytes 602120 | tf_op jit(solution)/shard_map/ppermute | solution.py:482
  28.1 8.7 %collective-permute-start.7 = (bf16[4,152,128]{2,1,0:T(8,128)(2,1)S(1)}, bf16[4,152,128]{2,1,0:T(8,128)(2,1)S(1)}, u32[]{:S(2)}, u32[]{:S(2)}) collective-permute-start(bf16[4,152,128]{2,1,0:T(8,128)(2,1)S(1)} %shard_map.94.mine_0), channel_id=1, source_target_pairs={{0,4},{1,5},{2,6},{3,7},{4,0},{5,1},{6,2},{7,3},{8,12},{9,13},{10,... | collective-permute-start | bytes 466952 | tf_op jit(solution)/shard_map/ppermute | solution.py:63
  37.8 10.9 %collective-permute-start.17 = (bf16[4,296,128]{2,1,0:T(8,128)(2,1)S(1)}, bf16[4,296,128]{2,1,0:T(8,128)(2,1)S(1)}, u32[]{:S(2)}, u32[]{:S(2)}) collective-permute-start(bf16[4,296,128]{2,1,0:T(8,128)(2,1)S(1)} %shard_map.93.mine_0), channel_id=1, source_target_pairs={{0,6},{1,7},{2,4},{3,5},{4,2},{5,3},{6,0},{7,1},{8,14},{9,15},{10,... | collective-permute-start | bytes 909320 | tf_op jit(solution)/shard_map/ppermute | solution.py:63
  39.3 15.4 %collective-permute-start.16 = (bf16[4,296,128]{2,1,0:T(8,128)(2,1)S(1)}, bf16[4,296,128]{2,1,0:T(8,128)(2,1)S(1)}, u32[]{:S(2)}, u32[]{:S(2)}) collective-permute-start(bf16[4,296,128]{2,1,0:T(8,128)(2,1)S(1)} %shard_map.93.mine_0), channel_id=1, source_target_pairs={{0,4},{1,5},{2,6},{3,7},{4,0},{5,1},{6,2},{7,3},{8,12},{9,13},{10,... | collective-permute-start | bytes 909320 | tf_op jit(solution)/shard_map/ppermute | solution.py:63
  40.6 14.5 %collective-permute-start.15 = (bf16[4,296,128]{2,1,0:T(8,128)(2,1)S(1)}, bf16[4,296,128]{2,1,0:T(8,128)(2,1)S(1)}, u32[]{:S(2)}, u32[]{:S(2)}) collective-permute-start(bf16[4,296,128]{2,1,0:T(8,128)(2,1)S(1)} %shard_map.93.mine_0), channel_id=1, source_target_pairs={{0,2},{1,3},{2,0},{3,1},{4,6},{5,7},{6,4},{7,5},{8,10},{9,11},{10,... | collective-permute-start | bytes 909320 | tf_op jit(solution)/shard_map/ppermute | solution.py:63
  41.3 13.9 %collective-permute-start.14 = (bf16[4,152,128]{2,1,0:T(8,128)(2,1)S(1)}, bf16[4,152,128]{2,1,0:T(8,128)(2,1)S(1)}, u32[]{:S(2)}, u32[]{:S(2)}) collective-permute-start(bf16[4,152,128]{2,1,0:T(8,128)(2,1)S(1)} %collective-permute-done.8.mine_3), channel_id=1, source_target_pairs={{0,1},{1,0},{2,3},{3,2},{4,5},{5,4},{6,7},{7,6},{8,9},{9,8},{10,11... | collective-permute-start | bytes 466952 | tf_op jit(solution)/shard_map/ppermute | solution.py:63
  42.7 16.8 %collective-permute-start.18 = (bf16[4,296,128]{2,1,0:T(8,128)(2,1)S(1)}, bf16[4,296,128]{2,1,0:T(8,128)(2,1)S(1)}, u32[]{:S(2)}, u32[]{:S(2)}) collective-permute-start(bf16[4,296,128]{2,1,0:T(8,128)(2,1)S(1)} %shard_map.93.mine_0), channel_id=1, source_target_pairs={{0,1},{1,0},{2,3},{3,2},{4,5},{5,4},{6,7},{7,6},{8,9},{9,8},{10,11... | collective-permute-start | bytes 909320 | tf_op jit(solution)/shard_map/ppermute | solution.py:63
  48.7 10.8 %collective-permute-start.21 = (bf16[4,296,128]{2,1,0:T(8,128)(2,1)S(1)}, bf16[4,296,128]{2,1,0:T(8,128)(2,1)S(1)}, u32[]{:S(2)}, u32[]{:S(2)}) collective-permute-start(bf16[4,296,128]{2,1,0:T(8,128)(2,1)S(1)} %collective-permute-done.17.mine_3), channel_id=1, source_target_pairs={{0,1},{1,0},{2,3},{3,2},{4,5},{5,4},{6,7},{7,6},{8,9},{9,8},{10,11... | collective-permute-start | bytes 909320 | tf_op jit(solution)/shard_map/ppermute | solution.py:63
  81.2 9.8 %collective-permute-start.32 = (bf16[4,296,128]{2,1,0:T(8,128)(2,1)S(1)}, bf16[4,296,128]{2,1,0:T(8,128)(2,1)S(1)}, u32[]{:S(2)}, u32[]{:S(2)}) collective-permute-start(bf16[4,296,128]{2,1,0:T(8,128)(2,1)S(1)} %get-tuple-element.103), channel_id=1, source_target_pairs={{0,2},{1,3},{2,0},{3,1},{4,6},{5,7},{6,4},{7,5},{8,10},{9,11},{10,... | collective-permute-start | bytes 909320 | tf_op jit(solution)/shard_map/ppermute | solution.py:63
  82.8 11.0 %collective-permute-start.33 = (bf16[4,296,128]{2,1,0:T(8,128)(2,1)S(1)}, bf16[4,296,128]{2,1,0:T(8,128)(2,1)S(1)}, u32[]{:S(2)}, u32[]{:S(2)}) collective-permute-start(bf16[4,296,128]{2,1,0:T(8,128)(2,1)S(1)} %get-tuple-element.104), channel_id=1, source_target_pairs={{0,4},{1,5},{2,6},{3,7},{4,0},{5,1},{6,2},{7,3},{8,12},{9,13},{10,... | collective-permute-start | bytes 909320 | tf_op jit(solution)/shard_map/ppermute | solution.py:63
  83.8 14.5 %collective-permute-start.34 = (bf16[4,296,128]{2,1,0:T(8,128)(2,1)S(1)}, bf16[4,296,128]{2,1,0:T(8,128)(2,1)S(1)}, u32[]{:S(2)}, u32[]{:S(2)}) collective-permute-start(bf16[4,296,128]{2,1,0:T(8,128)(2,1)S(1)} %get-tuple-element.105), channel_id=1, source_target_pairs={{0,6},{1,7},{2,4},{3,5},{4,2},{5,3},{6,0},{7,1},{8,14},{9,15},{10,... | collective-permute-start | bytes 909320 | tf_op jit(solution)/shard_map/ppermute | solution.py:63
  84.9 20.5 %collective-permute-start.26 = (bf16[4,152,128]{2,1,0:T(8,128)(2,1)S(1)}, bf16[4,152,128]{2,1,0:T(8,128)(2,1)S(1)}, u32[]{:S(2)}, u32[]{:S(2)}) collective-permute-start(bf16[4,152,128]{2,1,0:T(8,128)(2,1)S(1)} %get-tuple-element.95), channel_id=1, source_target_pairs={{0,2},{1,3},{2,0},{3,1},{4,6},{5,7},{6,4},{7,5},{8,10},{9,11},{10,... | collective-permute-start | bytes 466952 | tf_op jit(solution)/shard_map/ppermute | solution.py:63
  98.5 20.2 %collective-permute-start.35 = (bf16[296,128]{1,0:T(8,128)(2,1)S(1)}, bf16[296,128]{1,0:T(8,128)(2,1)S(1)}, u32[]{:S(2)}, u32[]{:S(2)}) collective-permute-start(bf16[296,128]{1,0:T(8,128)(2,1)S(1)} %get-tuple-element.107), channel_id=1, source_target_pairs={{0,8},{1,9},{2,10},{3,11},{4,12},{5,13},{6,14},{7,15},{8,0},{9,1},... | collective-permute-start | bytes 227336 | tf_op jit(solution)/shard_map/ppermute | solution.py:63
  101.9 17.0 %collective-permute-start.36 = (bf16[296,128]{1,0:T(8,128)(2,1)S(1)}, bf16[296,128]{1,0:T(8,128)(2,1)S(1)}, u32[]{:S(2)}, u32[]{:S(2)}) collective-permute-start(bf16[296,128]{1,0:T(8,128)(2,1)S(1)} %get-tuple-element.108), channel_id=1, source_target_pairs={{0,16},{1,17},{2,18},{3,19},{4,20},{5,21},{6,22},{7,23},{8,24},{9,... | collective-permute-start | bytes 227336 | tf_op jit(solution)/shard_map/ppermute | solution.py:63
  105.4 13.5 %collective-permute-start.37 = (bf16[296,128]{1,0:T(8,128)(2,1)S(1)}, bf16[296,128]{1,0:T(8,128)(2,1)S(1)}, u32[]{:S(2)}, u32[]{:S(2)}) collective-permute-start(bf16[296,128]{1,0:T(8,128)(2,1)S(1)} %get-tuple-element.109), channel_id=1, source_target_pairs={{0,24},{1,25},{2,26},{3,27},{4,28},{5,29},{6,30},{7,31},{8,16},{9,... | collective-permute-start | bytes 227336 | tf_op jit(solution)/shard_map/ppermute | solution.py:63
  105.4 9.0 %collective-permute-start.27 = (bf16[4,152,128]{2,1,0:T(8,128)(2,1)S(1)}, bf16[4,152,128]{2,1,0:T(8,128)(2,1)S(1)}, u32[]{:S(2)}, u32[]{:S(2)}) collective-permute-start(bf16[4,152,128]{2,1,0:T(8,128)(2,1)S(1)} %get-tuple-element.96), channel_id=1, source_target_pairs={{0,4},{1,5},{2,6},{3,7},{4,0},{5,1},{6,2},{7,3},{8,12},{9,13},{10,... | collective-permute-start | bytes 466952 | tf_op jit(solution)/shard_map/ppermute | solution.py:63
  105.5 9.0 %collective-permute-start.28 = (bf16[4,152,128]{2,1,0:T(8,128)(2,1)S(1)}, bf16[4,152,128]{2,1,0:T(8,128)(2,1)S(1)}, u32[]{:S(2)}, u32[]{:S(2)}) collective-permute-start(bf16[4,152,128]{2,1,0:T(8,128)(2,1)S(1)} %get-tuple-element.97), channel_id=1, source_target_pairs={{0,6},{1,7},{2,4},{3,5},{4,2},{5,3},{6,0},{7,1},{8,14},{9,15},{10,... | collective-permute-start | bytes 466952 | tf_op jit(solution)/shard_map/ppermute | solution.py:63
  (15 other events, 94.5 us)

commit v4 on v3

--- a/solution.py
+++ b/solution.py
@@ -94,14 +94,14 @@
     return (where * CORES + (meta_ref[4] ^ step)) * rows
 
 
-def lay_out_blocks(meta_ref, block_refs, flat_ref):
-    depth, padded, lanes = block_refs[0].shape
-    rows = flat_ref.shape[0] // (CORES * SQUARE * depth)
-    for index, block_ref in enumerate(block_refs):
-        step, spot = divmod(index, SQUARE)
-        for layer in range(depth):
-            base = block_row(meta_ref, step, spot, layer, rows)
-            flat_ref[pl.ds(base, rows), :] = block_ref[layer].astype(f32)[:rows]
+def lay_out_blocks(meta_ref, mine_ref, other_ref, flat_ref):
+    spots, depth, padded, lanes = mine_ref.shape
+    rows = flat_ref.shape[0] // (CORES * spots * depth)
+    for step, block_ref in enumerate((mine_ref, other_ref)):
+        for spot in range(spots):
+            for layer in range(depth):
+                base = block_row(meta_ref, step, spot, layer, rows)
+                flat_ref[pl.ds(base, rows), :] = block_ref[spot, layer].astype(f32)[:rows]
 
 
 def cut_blocks(meta_ref, flat_ref, keep_ref, send_ref):
@@ -180,14 +180,13 @@
 
 def attend_kernel(
     meta_ref, before_ref, own_ref, after_ref, mask_ref,
-    mine_0, mine_1, mine_2, mine_3, other_0, other_1, other_2, other_3,
+    mine_ref, other_ref,
     middle_ref, cotangent_ref, inputs_ref, normed_ref, qkv_ref, probability_ref,
     context_ref, classes_ref, w_qkv_ref, w_out_ref, gain_ref,
     flat_ref, window_ref,
 ):
     window = window_ref.shape[0]
-    block_refs = (mine_0, mine_1, mine_2, mine_3, other_0, other_1, other_2, other_3)
-    lay_out_blocks(meta_ref, block_refs, flat_ref)
+    lay_out_blocks(meta_ref, mine_ref, other_ref, flat_ref)
     read_matrix(flat_ref, W_QKV_AT, D, QKV_ROWS, w_qkv_ref)
     read_matrix(flat_ref, W_OUT_AT, D, D_ROWS, w_out_ref)
     gain = read_vector(flat_ref, GAIN_AT, D_ROWS)
@@ -243,13 +242,12 @@
 
 def feed_kernel(
     meta_ref, middle_ref, cotangent_ref,
-    mine_0, mine_1, mine_2, mine_3, other_0, other_1, other_2, other_3,
+    mine_ref, other_ref,
     output_ref, grad_middle_ref, keep_ref, send_ref,
     flat_ref, w_up_ref, w_down_ref, normed_ref,
 ):
     window = output_ref.shape[0]
-    block_refs = (mine_0, mine_1, mine_2, mine_3, other_0, other_1, other_2, other_3)
-    lay_out_blocks(meta_ref, block_refs, flat_ref)
+    lay_out_blocks(meta_ref, mine_ref, other_ref, flat_ref)
     read_matrix(flat_ref, W_UP_AT, D, FF_ROWS, w_up_ref)
     read_matrix(flat_ref, W_DOWN_AT, FF, D_ROWS, w_down_ref)
     gain = read_vector(flat_ref, GAIN_AT, D_ROWS)
@@ -399,7 +397,6 @@
     vmem = pl.BlockSpec(memory_space=pltpu.VMEM)
     smem = pl.BlockSpec(memory_space=pltpu.SMEM)
     specs = [smem if operand.dtype == jnp.int32 else vmem for operand in operands]
-    moved = sum(math.prod(o.shape) * o.dtype.itemsize for o in list(operands) + list(out_shapes))
     return pl.pallas_call(
         kernel,
         out_shape=out_shapes,
@@ -407,7 +404,7 @@
         out_specs=[vmem] * len(out_shapes),
         scratch_shapes=scratch,
         compiler_params=pltpu.CompilerParams(vmem_limit_bytes=32 * 1024 * 1024),
-        cost_estimate=pl.CostEstimate(flops=flops, bytes_accessed=moved, transcendentals=0),
+        cost_estimate=pl.CostEstimate(flops=flops, bytes_accessed=1, transcendentals=0),
     )(*operands)
 
 
@@ -436,25 +433,29 @@
     return jax.ShapeDtypeStruct(shape, kind)
 
 
+def pack(parts):
+    packed = struct((len(parts),) + parts[0].shape, bf16)
+    return call_kernel(pack_kernel, [packed], [], 1, parts)[0]
+
+
 def gather_columns(rows, devices):
     depth = devices // (CORES * SQUARE)
-    parts = [rows] + pass_layers([rows] * depth, devices)
-    return call_kernel(pack_kernel, [struct((depth,) + rows.shape, bf16)], [], 10**6, parts)[0]
+    return pack([rows] + pass_layers([rows] * depth, devices))
 
 
 def gather_planes(column, devices):
-    return [column] + pass_chips([column] * SQUARE, devices)
+    return pack([column] + pass_chips([column] * SQUARE, devices))
 
 
 def add_cores(keep, send, devices):
     parts = [struct(keep.shape[1:], bf16)] * SQUARE
-    return call_kernel(add_cores_kernel, parts, [], 10**6, [keep, pass_cores(send, devices)])
+    return call_kernel(add_cores_kernel, parts, [], 1, [keep, pass_cores(send, devices)])
 
 
 def add_chips(parts, passed):
     depth, padded, lanes = parts[0].shape
     sums = [struct((padded, lanes), bf16)] * depth
-    return call_kernel(add_chips_kernel, sums, [], 10**6, [parts[0]] + passed)
+    return call_kernel(add_chips_kernel, sums, [], 1, [parts[0]] + passed)
 
 
 def shards(inputs, attn_blocks, mlp_blocks, image_id, bias_id, out_grad):
@@ -479,16 +480,17 @@
     attn_rows = as_rows(attn_blocks)
     mlp_rows = as_rows(mlp_blocks)
     attn_column = gather_columns(attn_rows, devices)
+    mlp_parts = pass_layers([mlp_rows] * depth, devices)
+    attn_column, tokens = barrier((attn_column, tokens))
     before = lax.ppermute(tokens[token_rows - HALO :], "fsdp", up)
     after = lax.ppermute(tokens[:HALO], "fsdp", down)
-    mlp_column = gather_columns(mlp_rows, devices)
+    mlp_column = pack([mlp_rows] + mlp_parts)
     attn_mine = gather_planes(attn_column, devices)
     mlp_column, attn_mine, before, after, meta, head_mask = barrier(
         (mlp_column, attn_mine, before, after, meta, head_mask)
     )
-    mlp_mine = gather_planes(mlp_column, devices)
-    attn_other = [pass_cores(part, devices) for part in attn_mine]
-    mlp_other = [pass_cores(part, devices) for part in mlp_mine]
+    mlp_passed = pass_chips([mlp_column] * SQUARE, devices)
+    attn_other = pass_cores(attn_mine, devices)
 
     (
         middle, cotangent, inputs_span, normed, qkv, probability, context, classes_span,
@@ -509,9 +511,12 @@
             struct((1, D), f32),
         ],
         [pltpu.VMEM((attn_flat + 16, LANES), f32), pltpu.VMEM((window, WIDE), bf16)],
-        5 * 10**9,
-        [meta, before, tokens, after, head_mask] + attn_mine + attn_other,
-    )
+        1,
+        [meta, before, tokens, after, head_mask, attn_mine, attn_other],
+    )
+    mlp_passed, middle = barrier((mlp_passed, middle))
+    mlp_mine = pack([mlp_column] + mlp_passed)
+    mlp_other = pass_cores(mlp_mine, devices)
     feed_blocks = struct((SQUARE,) + mlp_column.shape, bf16)
     output, grad_middle, feed_keep, feed_send = call_kernel(
         feed_kernel,
@@ -522,8 +527,8 @@
             pltpu.VMEM((FF, D), bf16),
             pltpu.VMEM((SPAN, D), bf16),
         ],
-        9 * 10**9,
-        [meta, middle, cotangent] + mlp_mine + mlp_other,
+        1,
+        [meta, middle, cotangent, mlp_mine, mlp_other],
     )
     feed_parts = add_cores(feed_keep, feed_send, devices)
     grad_first, grad_w_out, grad_bias_out, grad_table, grad_context = call_kernel(
@@ -536,7 +541,7 @@
             struct((SPAN, D), bf16),
         ],
         [],
-        4 * 10**9,
+        1,
         [meta, grad_middle, qkv, probability, context, classes_span, w_out],
     )
     feed_parts, grad_first = barrier((feed_parts, grad_first))
@@ -550,23 +555,27 @@
             pltpu.VMEM((SLOT, 3 * D), bf16),
             pltpu.VMEM((SPAN, 3 * D), bf16),
         ],
-        8 * 10**9,
+        1,
         [
             meta, grad_middle, head_mask, inputs_span, normed, qkv, probability, classes_span,
             w_qkv, gain, grad_first, grad_w_out, grad_bias_out, grad_table, grad_context,
         ],
     )
-    attn_parts = add_cores(attn_keep, attn_send, devices)
-    attn_passed = pass_chips(attn_parts, devices)
+    edges = jnp.concatenate([output, grad_inputs.astype(bf16)], axis=1)
+    from_next = lax.ppermute(edges[:HALO], "fsdp", down)
+    from_last = lax.ppermute(edges[window - HALO :], "fsdp", up)
+    attn_send, feed_passed, from_next, from_last = barrier(
+        (attn_send, feed_passed, from_next, from_last)
+    )
+    attn_parts = list(add_cores(attn_keep, attn_send, devices))
     feed_sums = add_chips(feed_parts, feed_passed)
     feed_layers = [feed_sums[0]] + pass_layers(feed_sums, devices)
+    attn_parts[-1], feed_layers[1] = barrier((attn_parts[-1], feed_layers[1]))
+    attn_passed = pass_chips(attn_parts, devices)
     attn_sums = add_chips(attn_parts, attn_passed)
     attn_layers = [attn_sums[0]] + pass_layers(attn_sums, devices)
     feed_sum = sum(part.astype(f32) for part in feed_layers)
     attn_sum = sum(part.astype(f32) for part in attn_layers)
-    edges = jnp.concatenate([output, grad_inputs.astype(bf16)], axis=1)
-    from_next = lax.ppermute(edges[:HALO], "fsdp", down)
-    from_last = lax.ppermute(edges[window - HALO :], "fsdp", up)
     gap = jnp.zeros((token_rows - HALO, 2 * D), bf16)
     extra = jnp.concatenate([from_last, gap]) + jnp.concatenate([gap, from_next])
     own = slice(HALO, HALO + token_rows)

time: 126 us -> 114 us (0.905)
  waiting for transfers between devices: 44.3 us -> 29.1 us
  starting transfers between devices: 45.3 us -> 47.9 us
    ppermute x34 -> x28, waiting for transfers between devices: 44.3 us -> 26.2 us  [pass_on(): return lax.ppermute(value, 'fsdp', [(i, i ^ step) for i in range(devices)])]
    ppermute x34 -> x28, starting transfers between devices: 36.7 us -> 40.8 us  [pass_on(): return lax.ppermute(value, 'fsdp', [(i, i ^ step) for i in range(devices)])]
    ppermute x1, waiting for transfers between devices: 0.01 us -> 2.92 us  [shards(): from_next = lax.ppermute(edges[:HALO], 'fsdp', down)]
    ppermute x1, starting transfers between devices: 3.04 us -> 1.41 us  [shards(): from_last = lax.ppermute(edges[window - HALO:], 'fsdp', up)]
    pallas_call x10 -> x12, Pallas kernels: 21.3 us -> 21.4 us  [call_kernel(): pl.pallas_call(kernel, out_shape=out_shapes, in_specs=specs, out_specs=[v...]
  transfers between devices with their start and end apart: 38 -> 32, of which waited for: 13 -> 13; matrix products, arithmetic and copies ran while one was open for 7% -> 8% of each run, Pallas kernels for 7% -> 12%
where the time goes in v4:
time: 114 us; the launch traced here: 113 us
  starting transfers between devices  47.9 us (42%)
  waiting for transfers between devices  29.1 us (26%)
  Pallas kernels  21.4 us (19%)
  other arithmetic  7.9 us (7%)
  between operations  4.19 us (4%)
  local copies, waits for them, and re-layouts  2.86 us (3%)
    ppermute x28, starting transfers between devices, pass_on(): return lax.ppermute(value, 'fsdp', [(i, i ^ step) for i in range(devices)])  40.8 us
    ppermute x28, waiting for transfers between devices, pass_on(): return lax.ppermute(value, 'fsdp', [(i, i ^ step) for i in range(devices)])  26.2 us
    pallas_call x12, Pallas kernels, call_kernel(): pl.pallas_call(kernel, out_shape=out_shapes, in_specs=specs, out_specs=[v...  21.4 us
    ppermute x1, starting transfers between devices, shards(): before = lax.ppermute(tokens[token_rows - HALO:], 'fsdp', up)  3.04 us
    ppermute x1, waiting for transfers between devices, shards(): from_next = lax.ppermute(edges[:HALO], 'fsdp', down)  2.92 us
    unnamed x4, other arithmetic  2.48 us
  transfers between devices with their start and end apart: 32, of which 13 were waited for; matrix products, arithmetic and copies ran while one was open for 8% of the time, Pallas kernels for 12%

profile of v4, /device:TPU:0, one launch (start us, length us, event | category | flops | bytes accessed | tf_op | source)
XLA Modules:
  0.0 113.3 jit_solution(10394315315640305894)
XLA Ops:
  1.7 5.1 %collective-permute-start.5 = (bf16[152,128]{1,0:T(8,128)(2,1)S(1)}, bf16[152,128]{1,0:T(8,128)(2,1)S(1)}, u32[]{:S(2)}, u32[]{:S(2)}) collective-permute-start(bf16[152,128]{1,0:T(8,128)(2,1)S(1)} %pad.11.refs_0_), channel_id=1, source_target_pairs={{0,24},{1,25},{2,26},{3,27},{4,28},{5,29},{6,30},{7,31},{8,16},{9,... | collective-permute-start | bytes 116744 | tf_op jit(solution)/shard_map/ppermute | solution.py:63
  8.8 3.8 %collective-permute-start.2 = (bf16[296,128]{1,0:T(8,128)(2,1)S(1)}, bf16[296,128]{1,0:T(8,128)(2,1)S(1)}, u32[]{:S(2)}, u32[]{:S(2)}) collective-permute-start(bf16[296,128]{1,0:T(8,128)(2,1)S(1)} %pad.10.refs_0_), channel_id=1, source_target_pairs={{0,24},{1,25},{2,26},{3,27},{4,28},{5,29},{6,30},{7,31},{8,16},{9,... | collective-permute-start | bytes 227336 | tf_op jit(solution)/shard_map/ppermute | solution.py:63
  13.9 2.0 %fusion.4 = s32[]{:T(128)} fusion(s32[256]{0:T(256)} %param.9, s32[]{:T(128)} %bitcast), kind=kLoop, calls=%fused_computation.20 | loop fusion | flops 767 | bytes 1032 | tf_op jit(solution)/shard_map/reduce_sum | solution.py:414
  21.7 2.7 %collective-permute-start.8 = (bf16[4,152,128]{2,1,0:T(8,128)(2,1)S(1)}, bf16[4,152,128]{2,1,0:T(8,128)(2,1)S(1)}, u32[]{:S(2)}, u32[]{:S(2)}) collective-permute-start(bf16[4,152,128]{2,1,0:T(8,128)(2,1)S(1)} %shard_map.94.refs_0_), channel_id=1, source_target_pairs={{0,6},{1,7},{2,4},{3,5},{4,2},{5,3},{6,0},{7,1},{8,14},{9,15},{10,... | collective-permute-start | bytes 466952 | tf_op jit(solution)/shard_map/ppermute | solution.py:63
  26.7 3.0 %collective-permute-start.9 = (bf16[112,896]{1,0:T(8,128)(2,1)S(1)}, bf16[112,896]{1,0:T(8,128)(2,1)S(1)}, u32[]{:S(2)}, u32[]{:S(2)}) collective-permute-start(bf16[112,896]{1,0:T(8,128)(2,1)S(1)} %get-tuple-element.135), channel_id=1, source_target_pairs={{0,1},{1,2},{2,3},{3,4},{4,5},{5,6},{6,7},{7,8},{8,9},{9,10},{10,1... | collective-permute-start | bytes 602120 | tf_op jit(solution)/shard_map/ppermute | solution.py:485
  31.8 2.2 %collective-permute-start.14 = (bf16[4,4,152,128]{3,2,1,0:T(8,128)(2,1)S(1)}, bf16[4,4,152,128]{3,2,1,0:T(8,128)(2,1)S(1)}, u32[]{:S(2)}, u32[]{:S(2)}) collective-permute-start(bf16[4,4,152,128]{3,2,1,0:T(8,128)(2,1)S(1)} %shard_map.95.mine_ref), channel_id=1, source_target_pairs={{0,1},{1,0},{2,3},{3,2},{4,5},{5,4},{6,7},{7,6},{8,9},{9,8},{10,11... | collective-permute-start | bytes 1867784 | tf_op jit(solution)/shard_map/ppermute | solution.py:63
  34.0 3.0 %collective-permute-start.13 = (bf16[4,296,128]{2,1,0:T(8,128)(2,1)S(1)}, bf16[4,296,128]{2,1,0:T(8,128)(2,1)S(1)}, u32[]{:S(2)}, u32[]{:S(2)}) collective-permute-start(bf16[4,296,128]{2,1,0:T(8,128)(2,1)S(1)} %shard_map.93.refs_0_), channel_id=1, source_target_pairs={{0,6},{1,7},{2,4},{3,5},{4,2},{5,3},{6,0},{7,1},{8,14},{9,15},{10,... | collective-permute-start | bytes 909320 | tf_op jit(solution)/shard_map/ppermute | solution.py:63
  38.4 4.3 %shard_map.96 = (f32[416,384]{1,0:T(8,128)S(1)}, bf16[416,384]{1,0:T(8,128)(2,1)S(1)}, bf16[416,384]{1,0:T(8,128)(2,1)S(1)}, bf16[416,384]{1,0:T(8,128)(2,1)S(1)...) custom-call(s32[8]{0:T(128)S(1)} %stack.31.meta_ref, ...), custom_call_target="tpu_custom_call" | custom-call | flops 1 | bytes 1 | tf_op jit(solution)/shard_map/pallas_call | solution.py:400
  42.7 2.3 %collective-permute-done.13.refs_3_ = bf16[4,296,128]{2,1,0:T(8,128)(2,1)S(1)} collective-permute-done((bf16[4,296,128]{2,1,0:T(8,128)(2,1)S(1)}, bf16[4,296,128]{2,1,0:T(8,128)(2,1)S(1)}, u32[]{:S(2)}, u32[]{:S(2)}) %collective-permute-start.13) | collective-permute-done | bytes 303136 | tf_op jit(solution)/shard_map/ppermute | solution.py:63
  45.0 6.3 %collective-permute-done.12.refs_2_ = bf16[4,296,128]{2,1,0:T(8,128)(2,1)S(1)} collective-permute-done((bf16[4,296,128]{2,1,0:T(8,128)(2,1)S(1)}, bf16[4,296,128]{2,1,0:T(8,128)(2,1)S(1)}, u32[]{:S(2)}, u32[]{:S(2)}) %collective-permute-start.12) | collective-permute-done | bytes 303136 | tf_op jit(solution)/shard_map/ppermute | solution.py:63
  52.7 2.9 %collective-permute-done.15.other_ref = bf16[4,4,296,128]{3,2,1,0:T(8,128)(2,1)S(1)} collective-permute-done((bf16[4,4,296,128]{3,2,1,0:T(8,128)(2,1)S(1)}, bf16[4,4,296,128]{3,2,1,0:T(8,128)(2,1)S(1)}, u32[]{:S(2)}, u32[]{:S(2)}) %collective-permute-start.15) | collective-permute-done | bytes 1212448 | tf_op jit(solution)/shard_map/ppermute | solution.py:63
  55.5 7.5 %shard_map.98 = (bf16[480,384]{1,0:T(8,128)(2,1)S(1)}, f32[416,384]{1,0:T(8,128)S(1)}, bf16[4,4,296,128]{3,2,1,0:T(8,128)(2,1)S(1)}, bf16[4,4,296,128]{3,2,1,0:T(8,128)(2,1)S(1)}) custom-call(s32[8]{0:T(128)S(1)} %stack.31.meta_ref, f32[416,384]{1,0:T(8,128)S(1)} %get-tuple-element.77.middle_ref, bf16[416,384]{1,0:T(8,128)(2,1)S(1)} %get-tuple-element.78.cotangent_ref, ...), custom_call_target="tpu_custom_call" | custom-call | flops 1 | bytes 1 | tf_op jit(solution)/shard_map/pallas_call | solution.py:400
  63.2 3.5 %shard_map.100 = (bf16[208,1152]{1,0:T(8,128)(2,1)S(1)}, f32[384,384]{1,0:T(8,128)S(1)}, f32[1,384]{1,0:T(1,128)S(1)}, f32[8,128]{1,0:T(8,128)S(1)}, bf16[416,384]{1,0:T(8,128)(2,1)S(1)}) custom-call(s32[8]{0:T(128)S(1)} %stack.31.meta_ref, f32[416,384]{1,0:T(8,128)S(1)} %get-tuple-element.83.grad_middle_ref, ...), custom_call_target="tpu_custom_call" | custom-call | flops 1 | bytes 1 | tf_op jit(solution)/shard_map/pallas_call | solution.py:400
  69.1 1.5 %collective-permute-start.19 = (bf16[4,296,128]{2,1,0:T(8,128)(2,1)S(1)}, bf16[4,296,128]{2,1,0:T(8,128)(2,1)S(1)}, u32[]{:S(2)}, u32[]{:S(2)}) collective-permute-start(bf16[4,296,128]{2,1,0:T(8,128)(2,1)S(1)} %get-tuple-element.108), channel_id=1, source_target_pairs={{0,6},{1,7},{2,4},{3,5},{4,2},{5,3},{6,0},{7,1},{8,14},{9,15},{10,... | collective-permute-start | bytes 909320 | tf_op jit(solution)/shard_map/ppermute | solution.py:63
  70.6 5.3 %shard_map.101 = (f32[480,384]{1,0:T(8,128)S(1)}, bf16[4,4,152,128]{3,2,1,0:T(8,128)(2,1)S(1)}, bf16[4,4,152,128]{3,2,1,0:T(8,128)(2,1)S(1)}) custom-call(s32[8]{0:T(128)S(1)} %stack.31.meta_ref, f32[416,384]{1,0:T(8,128)S(1)} %get-tuple-element.83.grad_middle_ref, f32[8,128]{1,0:T(8,128)S(1)} %fusion.3.mask_ref, ...), custom_call_target="tpu_custom_call" | custom-call | flops 1 | bytes 1 | tf_op jit(solution)/shard_map/pallas_call | solution.py:400
  78.7 2.9 %collective-permute-done.20 = bf16[112,768]{1,0:T(8,128)(2,1)S(1)} collective-permute-done((bf16[112,768]{1,0:T(8,128)(2,1)S(1)}, bf16[112,768]{1,0:T(8,128)(2,1)S(1)}, u32[]{:S(2)}, u32[]{:S(2)}) %collective-permute-start.20) | collective-permute-done | bytes 172064 | tf_op jit(solution)/shard_map/ppermute | solution.py:565
  81.7 1.9 %collective-permute-done.19.refs_3_ = bf16[4,296,128]{2,1,0:T(8,128)(2,1)S(1)} collective-permute-done((bf16[4,296,128]{2,1,0:T(8,128)(2,1)S(1)}, bf16[4,296,128]{2,1,0:T(8,128)(2,1)S(1)}, u32[]{:S(2)}, u32[]{:S(2)}) %collective-permute-start.19) | collective-permute-done | bytes 303136 | tf_op jit(solution)/shard_map/ppermute | solution.py:63
  83.6 3.1 %collective-permute-start.22 = (bf16[4,4,152,128]{3,2,1,0:T(8,128)(2,1)S(1)}, bf16[4,4,152,128]{3,2,1,0:T(8,128)(2,1)S(1)}, u32[]{:S(2)}, u32[]{:S(2)}) collective-permute-start(bf16[4,4,152,128]{3,2,1,0:T(8,128)(2,1)S(1)} %get-tuple-element.113), channel_id=1, source_target_pairs={{0,1},{1,0},{2,3},{3,2},{4,5},{5,4},{6,7},{7,6},{8,9},{9,8},{10,11... | collective-permute-start | bytes 1867784 | tf_op jit(solution)/shard_map/ppermute | solution.py:63
  86.8 1.5 %collective-permute-start.25 = (bf16[296,128]{1,0:T(8,128)(2,1)S(1)}, bf16[296,128]{1,0:T(8,128)(2,1)S(1)}, u32[]{:S(2)}, u32[]{:S(2)}) collective-permute-start(bf16[296,128]{1,0:T(8,128)(2,1)S(1)} %get-tuple-element.122), channel_id=1, source_target_pairs={{0,8},{1,9},{2,10},{3,11},{4,12},{5,13},{6,14},{7,15},{8,0},{9,1},... | collective-permute-start | bytes 227336 | tf_op jit(solution)/shard_map/ppermute | solution.py:63
  88.4 2.9 %collective-permute-start.30 = (bf16[296,128]{1,0:T(8,128)(2,1)S(1)}, bf16[296,128]{1,0:T(8,128)(2,1)S(1)}, u32[]{:S(2)}, u32[]{:S(2)}) collective-permute-start(bf16[296,128]{1,0:T(8,128)(2,1)S(1)} %get-tuple-element.130), channel_id=1, source_target_pairs={{0,16},{1,17},{2,18},{3,19},{4,20},{5,21},{6,22},{7,23},{8,24},{9,... | collective-permute-start | bytes 227336 | tf_op jit(solution)/shard_map/ppermute | solution.py:63
  92.3 3.9 %collective-permute-start.26 = (bf16[4,152,128]{2,1,0:T(8,128)(2,1)S(1)}, bf16[4,152,128]{2,1,0:T(8,128)(2,1)S(1)}, u32[]{:S(2)}, u32[]{:S(2)}) collective-permute-start(bf16[4,152,128]{2,1,0:T(8,128)(2,1)S(1)} %get-tuple-element.123), channel_id=1, source_target_pairs={{0,6},{1,7},{2,4},{3,5},{4,2},{5,3},{6,0},{7,1},{8,14},{9,15},{10,... | collective-permute-start | bytes 466952 | tf_op jit(solution)/shard_map/ppermute | solution.py:63
  97.5 3.5 %collective-permute-done.26.refs_3_ = bf16[4,152,128]{2,1,0:T(8,128)(2,1)S(1)} collective-permute-done((bf16[4,152,128]{2,1,0:T(8,128)(2,1)S(1)}, bf16[4,152,128]{2,1,0:T(8,128)(2,1)S(1)}, u32[]{:S(2)}, u32[]{:S(2)}) %collective-permute-start.26) | collective-permute-done | bytes 155680 | tf_op jit(solution)/shard_map/ppermute | solution.py:63
  103.8 3.0 %collective-permute-start.28 = (bf16[152,128]{1,0:T(8,128)(2,1)S(1)}, bf16[152,128]{1,0:T(8,128)(2,1)S(1)}, u32[]{:S(2)}, u32[]{:S(2)}) collective-permute-start(bf16[152,128]{1,0:T(8,128)(2,1)S(1)} %get-tuple-element.126), channel_id=1, source_target_pairs={{0,16},{1,17},{2,18},{3,19},{4,20},{5,21},{6,22},{7,23},{8,24},{9,... | collective-permute-start | bytes 116744 | tf_op jit(solution)/shard_map/ppermute | solution.py:63
  108.8 3.8 %collective-permute-done.29 = bf16[152,128]{1,0:T(8,128)(2,1)S(1)} collective-permute-done((bf16[152,128]{1,0:T(8,128)(2,1)S(1)}, bf16[152,128]{1,0:T(8,128)(2,1)S(1)}, u32[]{:S(2)}, u32[]{:S(2)}) %collective-permute-start.29) | collective-permute-done | bytes 38944 | tf_op jit(solution)/shard_map/ppermute | solution.py:63
  (74 shorter events, 27.2 us)
Async XLA Ops:
  1.7 19.2 %collective-permute-start.5 = (bf16[152,128]{1,0:T(8,128)(2,1)S(1)}, bf16[152,128]{1,0:T(8,128)(2,1)S(1)}, u32[]{:S(2)}, u32[]{:S(2)}) collective-permute-start(bf16[152,128]{1,0:T(8,128)(2,1)S(1)} %pad.11.refs_0_), channel_id=1, source_target_pairs={{0,24},{1,25},{2,26},{3,27},{4,28},{5,29},{6,30},{7,31},{8,16},{9,... | collective-permute-start | bytes 116744 | tf_op jit(solution)/shard_map/ppermute | solution.py:63
  6.9 14.8 %collective-permute-start.4 = (bf16[152,128]{1,0:T(8,128)(2,1)S(1)}, bf16[152,128]{1,0:T(8,128)(2,1)S(1)}, u32[]{:S(2)}, u32[]{:S(2)}) collective-permute-start(bf16[152,128]{1,0:T(8,128)(2,1)S(1)} %pad.11.refs_0_), channel_id=1, source_target_pairs={{0,16},{1,17},{2,18},{3,19},{4,20},{5,21},{6,22},{7,23},{8,24},{9,... | collective-permute-start | bytes 116744 | tf_op jit(solution)/shard_map/ppermute | solution.py:63
  6.9 14.8 %collective-permute-start.3 = (bf16[152,128]{1,0:T(8,128)(2,1)S(1)}, bf16[152,128]{1,0:T(8,128)(2,1)S(1)}, u32[]{:S(2)}, u32[]{:S(2)}) collective-permute-start(bf16[152,128]{1,0:T(8,128)(2,1)S(1)} %pad.11.refs_0_), channel_id=1, source_target_pairs={{0,8},{1,9},{2,10},{3,11},{4,12},{5,13},{6,14},{7,15},{8,0},{9,1},... | collective-permute-start | bytes 116744 | tf_op jit(solution)/shard_map/ppermute | solution.py:63
  8.8 16.1 %collective-permute-start.2 = (bf16[296,128]{1,0:T(8,128)(2,1)S(1)}, bf16[296,128]{1,0:T(8,128)(2,1)S(1)}, u32[]{:S(2)}, u32[]{:S(2)}) collective-permute-start(bf16[296,128]{1,0:T(8,128)(2,1)S(1)} %pad.10.refs_0_), channel_id=1, source_target_pairs={{0,24},{1,25},{2,26},{3,27},{4,28},{5,29},{6,30},{7,31},{8,16},{9,... | collective-permute-start | bytes 227336 | tf_op jit(solution)/shard_map/ppermute | solution.py:63
  12.6 12.7 %collective-permute-start.1 = (bf16[296,128]{1,0:T(8,128)(2,1)S(1)}, bf16[296,128]{1,0:T(8,128)(2,1)S(1)}, u32[]{:S(2)}, u32[]{:S(2)}) collective-permute-start(bf16[296,128]{1,0:T(8,128)(2,1)S(1)} %pad.10.refs_0_), channel_id=1, source_target_pairs={{0,16},{1,17},{2,18},{3,19},{4,20},{5,21},{6,22},{7,23},{8,24},{9,... | collective-permute-start | bytes 227336 | tf_op jit(solution)/shard_map/ppermute | solution.py:63
  21.0 5.7 %collective-permute-start = (bf16[296,128]{1,0:T(8,128)(2,1)S(1)}, bf16[296,128]{1,0:T(8,128)(2,1)S(1)}, u32[]{:S(2)}, u32[]{:S(2)}) collective-permute-start(bf16[296,128]{1,0:T(8,128)(2,1)S(1)} %pad.10.refs_0_), channel_id=1, source_target_pairs={{0,8},{1,9},{2,10},{3,11},{4,12},{5,13},{6,14},{7,15},{8,0},{9,1},... | collective-permute-start | bytes 227336 | tf_op jit(solution)/shard_map/ppermute | solution.py:63
  21.7 8.2 %collective-permute-start.8 = (bf16[4,152,128]{2,1,0:T(8,128)(2,1)S(1)}, bf16[4,152,128]{2,1,0:T(8,128)(2,1)S(1)}, u32[]{:S(2)}, u32[]{:S(2)}) collective-permute-start(bf16[4,152,128]{2,1,0:T(8,128)(2,1)S(1)} %shard_map.94.refs_0_), channel_id=1, source_target_pairs={{0,6},{1,7},{2,4},{3,5},{4,2},{5,3},{6,0},{7,1},{8,14},{9,15},{10,... | collective-permute-start | bytes 466952 | tf_op jit(solution)/shard_map/ppermute | solution.py:63
  24.4 6.0 %collective-permute-start.7 = (bf16[4,152,128]{2,1,0:T(8,128)(2,1)S(1)}, bf16[4,152,128]{2,1,0:T(8,128)(2,1)S(1)}, u32[]{:S(2)}, u32[]{:S(2)}) collective-permute-start(bf16[4,152,128]{2,1,0:T(8,128)(2,1)S(1)} %shard_map.94.refs_0_), channel_id=1, source_target_pairs={{0,4},{1,5},{2,6},{3,7},{4,0},{5,1},{6,2},{7,3},{8,12},{9,13},{10,... | collective-permute-start | bytes 466952 | tf_op jit(solution)/shard_map/ppermute | solution.py:63
  24.9 6.8 %collective-permute-start.6 = (bf16[4,152,128]{2,1,0:T(8,128)(2,1)S(1)}, bf16[4,152,128]{2,1,0:T(8,128)(2,1)S(1)}, u32[]{:S(2)}, u32[]{:S(2)}) collective-permute-start(bf16[4,152,128]{2,1,0:T(8,128)(2,1)S(1)} %shard_map.94.refs_0_), channel_id=1, source_target_pairs={{0,2},{1,3},{2,0},{3,1},{4,6},{5,7},{6,4},{7,5},{8,10},{9,11},{10,... | collective-permute-start | bytes 466952 | tf_op jit(solution)/shard_map/ppermute | solution.py:63
  25.4 6.4 %collective-permute-start.10 = (bf16[112,896]{1,0:T(8,128)(2,1)S(1)}, bf16[112,896]{1,0:T(8,128)(2,1)S(1)}, u32[]{:S(2)}, u32[]{:S(2)}) collective-permute-start(bf16[112,896]{1,0:T(8,128)(2,1)S(1)} %get-tuple-element.134), channel_id=1, source_target_pairs={{1,0},{2,1},{3,2},{4,3},{5,4},{6,5},{7,6},{8,7},{9,8},{10,9},{11,1... | collective-permute-start | bytes 602120 | tf_op jit(solution)/shard_map/ppermute | solution.py:486
  31.8 6.6 %collective-permute-start.14 = (bf16[4,4,152,128]{3,2,1,0:T(8,128)(2,1)S(1)}, bf16[4,4,152,128]{3,2,1,0:T(8,128)(2,1)S(1)}, u32[]{:S(2)}, u32[]{:S(2)}) collective-permute-start(bf16[4,4,152,128]{3,2,1,0:T(8,128)(2,1)S(1)} %shard_map.95.mine_ref), channel_id=1, source_target_pairs={{0,1},{1,0},{2,3},{3,2},{4,5},{5,4},{6,7},{7,6},{8,9},{9,8},{10,11... | collective-permute-start | bytes 1867784 | tf_op jit(solution)/shard_map/ppermute | solution.py:63
  34.0 11.1 %collective-permute-start.13 = (bf16[4,296,128]{2,1,0:T(8,128)(2,1)S(1)}, bf16[4,296,128]{2,1,0:T(8,128)(2,1)S(1)}, u32[]{:S(2)}, u32[]{:S(2)}) collective-permute-start(bf16[4,296,128]{2,1,0:T(8,128)(2,1)S(1)} %shard_map.93.refs_0_), channel_id=1, source_target_pairs={{0,6},{1,7},{2,4},{3,5},{4,2},{5,3},{6,0},{7,1},{8,14},{9,15},{10,... | collective-permute-start | bytes 909320 | tf_op jit(solution)/shard_map/ppermute | solution.py:63
  36.9 14.3 %collective-permute-start.12 = (bf16[4,296,128]{2,1,0:T(8,128)(2,1)S(1)}, bf16[4,296,128]{2,1,0:T(8,128)(2,1)S(1)}, u32[]{:S(2)}, u32[]{:S(2)}) collective-permute-start(bf16[4,296,128]{2,1,0:T(8,128)(2,1)S(1)} %shard_map.93.refs_0_), channel_id=1, source_target_pairs={{0,4},{1,5},{2,6},{3,7},{4,0},{5,1},{6,2},{7,3},{8,12},{9,13},{10,... | collective-permute-start | bytes 909320 | tf_op jit(solution)/shard_map/ppermute | solution.py:63
  37.8 14.7 %collective-permute-start.11 = (bf16[4,296,128]{2,1,0:T(8,128)(2,1)S(1)}, bf16[4,296,128]{2,1,0:T(8,128)(2,1)S(1)}, u32[]{:S(2)}, u32[]{:S(2)}) collective-permute-start(bf16[4,296,128]{2,1,0:T(8,128)(2,1)S(1)} %shard_map.93.refs_0_), channel_id=1, source_target_pairs={{0,2},{1,3},{2,0},{3,1},{4,6},{5,7},{6,4},{7,5},{8,10},{9,11},{10,... | collective-permute-start | bytes 909320 | tf_op jit(solution)/shard_map/ppermute | solution.py:63
  67.0 14.6 %collective-permute-start.17 = (bf16[4,296,128]{2,1,0:T(8,128)(2,1)S(1)}, bf16[4,296,128]{2,1,0:T(8,128)(2,1)S(1)}, u32[]{:S(2)}, u32[]{:S(2)}) collective-permute-start(bf16[4,296,128]{2,1,0:T(8,128)(2,1)S(1)} %get-tuple-element.106), channel_id=1, source_target_pairs={{0,2},{1,3},{2,0},{3,1},{4,6},{5,7},{6,4},{7,5},{8,10},{9,11},{10,... | collective-permute-start | bytes 909320 | tf_op jit(solution)/shard_map/ppermute | solution.py:63
  67.9 13.7 %collective-permute-start.18 = (bf16[4,296,128]{2,1,0:T(8,128)(2,1)S(1)}, bf16[4,296,128]{2,1,0:T(8,128)(2,1)S(1)}, u32[]{:S(2)}, u32[]{:S(2)}) collective-permute-start(bf16[4,296,128]{2,1,0:T(8,128)(2,1)S(1)} %get-tuple-element.107), channel_id=1, source_target_pairs={{0,4},{1,5},{2,6},{3,7},{4,0},{5,1},{6,2},{7,3},{8,12},{9,13},{10,... | collective-permute-start | bytes 909320 | tf_op jit(solution)/shard_map/ppermute | solution.py:63
  69.1 14.5 %collective-permute-start.19 = (bf16[4,296,128]{2,1,0:T(8,128)(2,1)S(1)}, bf16[4,296,128]{2,1,0:T(8,128)(2,1)S(1)}, u32[]{:S(2)}, u32[]{:S(2)}) collective-permute-start(bf16[4,296,128]{2,1,0:T(8,128)(2,1)S(1)} %get-tuple-element.108), channel_id=1, source_target_pairs={{0,6},{1,7},{2,4},{3,5},{4,2},{5,3},{6,0},{7,1},{8,14},{9,15},{10,... | collective-permute-start | bytes 909320 | tf_op jit(solution)/shard_map/ppermute | solution.py:63
  83.6 8.5 %collective-permute-start.22 = (bf16[4,4,152,128]{3,2,1,0:T(8,128)(2,1)S(1)}, bf16[4,4,152,128]{3,2,1,0:T(8,128)(2,1)S(1)}, u32[]{:S(2)}, u32[]{:S(2)}) collective-permute-start(bf16[4,4,152,128]{3,2,1,0:T(8,128)(2,1)S(1)} %get-tuple-element.113), channel_id=1, source_target_pairs={{0,1},{1,0},{2,3},{3,2},{4,5},{5,4},{6,7},{7,6},{8,9},{9,8},{10,11... | collective-permute-start | bytes 1867784 | tf_op jit(solution)/shard_map/ppermute | solution.py:63
  88.4 19.3 %collective-permute-start.30 = (bf16[296,128]{1,0:T(8,128)(2,1)S(1)}, bf16[296,128]{1,0:T(8,128)(2,1)S(1)}, u32[]{:S(2)}, u32[]{:S(2)}) collective-permute-start(bf16[296,128]{1,0:T(8,128)(2,1)S(1)} %get-tuple-element.130), channel_id=1, source_target_pairs={{0,16},{1,17},{2,18},{3,19},{4,20},{5,21},{6,22},{7,23},{8,24},{9,... | collective-permute-start | bytes 227336 | tf_op jit(solution)/shard_map/ppermute | solution.py:63
  91.3 16.3 %collective-permute-start.31 = (bf16[296,128]{1,0:T(8,128)(2,1)S(1)}, bf16[296,128]{1,0:T(8,128)(2,1)S(1)}, u32[]{:S(2)}, u32[]{:S(2)}) collective-permute-start(bf16[296,128]{1,0:T(8,128)(2,1)S(1)} %get-tuple-element.131), channel_id=1, source_target_pairs={{0,24},{1,25},{2,26},{3,27},{4,28},{5,29},{6,30},{7,31},{8,16},{9,... | collective-permute-start | bytes 227336 | tf_op jit(solution)/shard_map/ppermute | solution.py:63
  92.3 8.8 %collective-permute-start.26 = (bf16[4,152,128]{2,1,0:T(8,128)(2,1)S(1)}, bf16[4,152,128]{2,1,0:T(8,128)(2,1)S(1)}, u32[]{:S(2)}, u32[]{:S(2)}) collective-permute-start(bf16[4,152,128]{2,1,0:T(8,128)(2,1)S(1)} %get-tuple-element.123), channel_id=1, source_target_pairs={{0,6},{1,7},{2,4},{3,5},{4,2},{5,3},{6,0},{7,1},{8,14},{9,15},{10,... | collective-permute-start | bytes 466952 | tf_op jit(solution)/shard_map/ppermute | solution.py:63
  96.1 6.2 %collective-permute-start.23 = (bf16[4,152,128]{2,1,0:T(8,128)(2,1)S(1)}, bf16[4,152,128]{2,1,0:T(8,128)(2,1)S(1)}, u32[]{:S(2)}, u32[]{:S(2)}) collective-permute-start(bf16[4,152,128]{2,1,0:T(8,128)(2,1)S(1)} %get-tuple-element.115), channel_id=1, source_target_pairs={{0,2},{1,3},{2,0},{3,1},{4,6},{5,7},{6,4},{7,5},{8,10},{9,11},{10,... | collective-permute-start | bytes 466952 | tf_op jit(solution)/shard_map/ppermute | solution.py:63
  96.1 7.0 %collective-permute-start.24 = (bf16[4,152,128]{2,1,0:T(8,128)(2,1)S(1)}, bf16[4,152,128]{2,1,0:T(8,128)(2,1)S(1)}, u32[]{:S(2)}, u32[]{:S(2)}) collective-permute-start(bf16[4,152,128]{2,1,0:T(8,128)(2,1)S(1)} %get-tuple-element.116), channel_id=1, source_target_pairs={{0,4},{1,5},{2,6},{3,7},{4,0},{5,1},{6,2},{7,3},{8,12},{9,13},{10,... | collective-permute-start | bytes 466952 | tf_op jit(solution)/shard_map/ppermute | solution.py:63
  106.8 5.8 %collective-permute-start.29 = (bf16[152,128]{1,0:T(8,128)(2,1)S(1)}, bf16[152,128]{1,0:T(8,128)(2,1)S(1)}, u32[]{:S(2)}, u32[]{:S(2)}) collective-permute-start(bf16[152,128]{1,0:T(8,128)(2,1)S(1)} %get-tuple-element.127), channel_id=1, source_target_pairs={{0,24},{1,25},{2,26},{3,27},{4,28},{5,29},{6,30},{7,31},{8,16},{9,... | collective-permute-start | bytes 116744 | tf_op jit(solution)/shard_map/ppermute | solution.py:63
  (8 other events, 34.4 us)

commit v5 on v4

--- a/solution.py
+++ b/solution.py
@@ -126,12 +126,68 @@
 
 
 def add_chips_kernel(*refs):
-    parts = refs[:SQUARE]
-    for layer, out_ref in enumerate(refs[SQUARE:]):
+    parts, (keep_ref, send_ref) = refs[:SQUARE], refs[SQUARE:]
+    half = keep_ref.shape[0]
+    for layer in range(2 * half):
         total = parts[0][layer].astype(f32)
         for part_ref in parts[1:]:
             total = total + part_ref[layer].astype(f32)
-        out_ref[...] = total.astype(bf16)
+        if layer < half:
+            keep_ref[layer] = total.astype(bf16)
+        else:
+            send_ref[layer - half] = total.astype(bf16)
+
+
+def add_layers_kernel(keep_ref, other_ref, near_ref, send_ref):
+    half = near_ref.shape[0]
+    near_ref[...] = (keep_ref[:half].astype(f32) + other_ref[:half].astype(f32)).astype(bf16)
+    send_ref[...] = (keep_ref[half:].astype(f32) + other_ref[half:].astype(f32)).astype(bf16)
+
+
+def sixth(index):
+    return (index * 43) >> 8
+
+
+def head_mask():
+    lane = lax.broadcasted_iota(jnp.int32, (8, LANES), 1)
+    head = lax.broadcasted_iota(jnp.int32, (8, LANES), 0)
+    inside = (lane - HEADS * sixth(lane) == head) & (lane < NB * HEADS)
+    return jnp.where(inside, 1.0, 0.0)
+
+
+def prepare_kernel(
+    last_device, device_ref, image_ref, bias_ref, inputs_ref, out_grad_ref,
+    tokens_ref, first_ref, last_ref, meta_ref,
+):
+    token_rows = inputs_ref.shape[0]
+    tokens_ref[:, :D] = inputs_ref[...]
+    tokens_ref[:, D : 2 * D] = out_grad_ref[...]
+    entry = sixth(lax.broadcasted_iota(jnp.int32, (LANES, LANES), 0))
+    inside = entry < NB
+    for step in range(token_rows // LANES):
+        same = inside & (entry == bias_ref[step : step + 1])
+        classes = jnp.transpose(jnp.where(same, 1.0, 0.0))
+        tokens_ref[step * LANES : (step + 1) * LANES, 2 * D :] = classes.astype(bf16)
+    first_ref[...] = tokens_ref[:HALO]
+    last_ref[...] = tokens_ref[token_rows - HALO :]
+    images = image_ref[...]
+    ends = jnp.sum(jnp.where(images == images[0:1, 0:1], 1, 0))
+    device = device_ref[0]
+    first, last = device == 0, device == last_device
+    holds = first | (ends >= IMG // 2 + 1)
+    start = jnp.where(first, 0, jnp.where(holds, ends - IMG, ends))
+    stop = jnp.where(last, token_rows, token_rows + IMG)
+    stop_one = jnp.where(holds, ends, jnp.minimum(ends + IMG, stop))
+    has_next = (stop_one < stop) & (last | (stop_one + IMG // 2 < token_rows))
+    stop_two = jnp.where(has_next, jnp.minimum(stop_one + IMG, stop), stop_one)
+    meta_ref[0] = start + HALO
+    meta_ref[1] = stop_one - start
+    meta_ref[2] = stop_one + HALO
+    meta_ref[3] = stop_two - stop_one
+    meta_ref[4] = device & (CORES - 1)
+    meta_ref[5] = device >> 3
+    meta_ref[6] = (device >> 1) & (SQUARE - 1)
+    meta_ref[7] = 0
 
 
 def read_vector(flat_ref, at, amount):
@@ -179,7 +235,7 @@
 
 
 def attend_kernel(
-    meta_ref, before_ref, own_ref, after_ref, mask_ref,
+    meta_ref, before_ref, own_ref, after_ref,
     mine_ref, other_ref,
     middle_ref, cotangent_ref, inputs_ref, normed_ref, qkv_ref, probability_ref,
     context_ref, classes_ref, w_qkv_ref, w_out_ref, gain_ref,
@@ -195,7 +251,7 @@
     bias_query = read_vector(flat_ref, BIAS_QUERY_AT, D_ROWS)
     bias_value = read_vector(flat_ref, BIAS_VALUE_AT, D_ROWS)
     bias_out = read_vector(flat_ref, BIAS_OUT_AT, D_ROWS)
-    table = (mask_ref[...] * flat_ref[TABLE_AT : TABLE_AT + 1]).astype(bf16)
+    table = (head_mask() * flat_ref[TABLE_AT : TABLE_AT + 1]).astype(bf16)
 
     halo = before_ref.shape[0]
     own = own_ref.shape[0]
@@ -350,7 +406,7 @@
 
 
 def inputs_back_kernel(
-    meta_ref, grad_middle_ref, mask_ref, inputs_ref, normed_ref, qkv_ref, probability_ref,
+    meta_ref, grad_middle_ref, inputs_ref, normed_ref, qkv_ref, probability_ref,
     classes_ref, w_qkv_ref, gain_ref,
     grad_first_ref, grad_w_out_ref, grad_bias_out_ref, grad_table_ref, grad_context_ref,
     grad_inputs_ref, keep_ref, send_ref,
@@ -363,7 +419,7 @@
     grad_qkv_ref[:SLOT] = grad_first_ref[...]
     grad_qkv_ref[SLOT:] = grad_second_ref[...]
     flat_ref[TABLE_AT:] = jnp.zeros((flat_ref.shape[0] - TABLE_AT, LANES), f32)
-    flat_ref[TABLE_AT : TABLE_AT + 1] = jnp.sum(grad_table * mask_ref[...], axis=0, keepdims=True)
+    flat_ref[TABLE_AT : TABLE_AT + 1] = jnp.sum(grad_table * head_mask(), axis=0, keepdims=True)
     write_vector(flat_ref, BIAS_OUT_AT, D_ROWS, grad_bias_out_ref[...])
     for i in range(D_ROWS):
         flat_ref[pl.ds(W_OUT_AT + i, D, stride=D_ROWS), :] = grad_w_out_ref[
@@ -396,39 +452,18 @@
 def call_kernel(kernel, out_shapes, scratch, flops, operands):
     vmem = pl.BlockSpec(memory_space=pltpu.VMEM)
     smem = pl.BlockSpec(memory_space=pltpu.SMEM)
-    specs = [smem if operand.dtype == jnp.int32 else vmem for operand in operands]
+    specs = [smem if operand.dtype == jnp.int32 and operand.ndim == 1 else vmem for operand in operands]
     return pl.pallas_call(
         kernel,
         out_shape=out_shapes,
         in_specs=specs,
-        out_specs=[vmem] * len(out_shapes),
+        out_specs=[smem if shape.dtype == jnp.int32 else vmem for shape in out_shapes],
         scratch_shapes=scratch,
         compiler_params=pltpu.CompilerParams(vmem_limit_bytes=32 * 1024 * 1024),
         cost_estimate=pl.CostEstimate(flops=flops, bytes_accessed=1, transcendentals=0),
     )(*operands)
 
 
-def plan_slots(image_id, devices):
-    token_rows = image_id.shape[0]
-    device = lax.axis_index("fsdp")
-    ends = jnp.sum((image_id == image_id[0]).astype(jnp.int32))
-    first, last = device == 0, device == devices - 1
-    holds = first | (ends >= IMG // 2 + 1)
-    start = jnp.where(first, 0, jnp.where(holds, ends - IMG, ends))
-    stop = jnp.where(last, token_rows, token_rows + IMG)
-    stop_one = jnp.where(holds, ends, jnp.minimum(ends + IMG, stop))
-    next_centre = stop_one + IMG // 2
-    has_next = (stop_one < stop) & (last | (next_centre < token_rows))
-    stop_two = jnp.where(has_next, jnp.minimum(stop_one + IMG, stop), stop_one)
-    zero = jnp.zeros((), jnp.int32)
-    return jnp.stack(
-        [
-            start + HALO, stop_one - start, stop_one + HALO, stop_two - stop_one,
-            device % CORES, device // (CORES * SQUARE), (device // CORES) % SQUARE, zero,
-        ]
-    ).astype(jnp.int32)
-
-
 def struct(shape, kind):
     return jax.ShapeDtypeStruct(shape, kind)
 
@@ -454,8 +489,19 @@
 
 def add_chips(parts, passed):
     depth, padded, lanes = parts[0].shape
-    sums = [struct((padded, lanes), bf16)] * depth
-    return call_kernel(add_chips_kernel, sums, [], 1, [parts[0]] + passed)
+    halves = [struct((depth // 2, padded, lanes), bf16)] * 2
+    return call_kernel(add_chips_kernel, halves, [], 1, [parts[0]] + passed)
+
+
+def add_layers(keep, send, devices):
+    half, padded, lanes = keep.shape
+    while half > 1:
+        other = pass_on(send, half * CORES * SQUARE, devices)
+        half //= 2
+        halves = [struct((half, padded, lanes), bf16)] * 2
+        keep, send = call_kernel(add_layers_kernel, halves, [], 1, [keep, other])
+    other = pass_on(send, CORES * SQUARE, devices)
+    return keep[0].astype(f32) + other[0].astype(f32)
 
 
 def shards(inputs, attn_blocks, mlp_blocks, image_id, bias_id, out_grad):
@@ -467,28 +513,36 @@
     mlp_flat = devices * mlp_blocks.shape[1] // LANES
     barrier = lax.optimization_barrier
 
-    lane = jnp.arange(LANES, dtype=jnp.int32)
-    classes = ((lane // HEADS)[None, :] == bias_id[:, None]) & (lane < NB * HEADS)[None, :]
-    tokens = jnp.concatenate([inputs, out_grad, classes.astype(bf16)], axis=1)
     up = [(i, i + 1) for i in range(devices - 1)]
     down = [(i + 1, i) for i in range(devices - 1)]
-    meta = plan_slots(image_id, devices)
-    head = jnp.arange(8, dtype=jnp.int32)
-    head_mask = ((lane % HEADS)[None, :] == head[:, None]) & (lane < NB * HEADS)[None, :]
-    head_mask = head_mask.astype(f32)
-
+    tokens, first_rows, last_rows, meta = call_kernel(
+        functools.partial(prepare_kernel, devices - 1),
+        [
+            struct((token_rows, WIDE), bf16),
+            struct((HALO, WIDE), bf16),
+            struct((HALO, WIDE), bf16),
+            struct((8,), jnp.int32),
+        ],
+        [],
+        1,
+        [
+            lax.axis_index("fsdp").astype(jnp.int32).reshape(1),
+            image_id.reshape(-1, LANES),
+            bias_id.reshape(-1, LANES),
+            inputs,
+            out_grad,
+        ],
+    )
     attn_rows = as_rows(attn_blocks)
     mlp_rows = as_rows(mlp_blocks)
     attn_column = gather_columns(attn_rows, devices)
     mlp_parts = pass_layers([mlp_rows] * depth, devices)
-    attn_column, tokens = barrier((attn_column, tokens))
-    before = lax.ppermute(tokens[token_rows - HALO :], "fsdp", up)
-    after = lax.ppermute(tokens[:HALO], "fsdp", down)
+    attn_column, first_rows, last_rows = barrier((attn_column, first_rows, last_rows))
+    before = lax.ppermute(last_rows, "fsdp", up)
+    after = lax.ppermute(first_rows, "fsdp", down)
     mlp_column = pack([mlp_rows] + mlp_parts)
     attn_mine = gather_planes(attn_column, devices)
-    mlp_column, attn_mine, before, after, meta, head_mask = barrier(
-        (mlp_column, attn_mine, before, after, meta, head_mask)
-    )
+    mlp_column, attn_mine = barrier((mlp_column, attn_mine))
     mlp_passed = pass_chips([mlp_column] * SQUARE, devices)
     attn_other = pass_cores(attn_mine, devices)
 
@@ -512,7 +566,7 @@
         ],
         [pltpu.VMEM((attn_flat + 16, LANES), f32), pltpu.VMEM((window, WIDE), bf16)],
         1,
-        [meta, before, tokens, after, head_mask, attn_mine, attn_other],
+        [meta, before, tokens, after, attn_mine, attn_other],
     )
     mlp_passed, middle = barrier((mlp_passed, middle))
     mlp_mine = pack([mlp_column] + mlp_passed)
@@ -557,7 +611,7 @@
         ],
         1,
         [
-            meta, grad_middle, head_mask, inputs_span, normed, qkv, probability, classes_span,
+            meta, grad_middle, inputs_span, normed, qkv, probability, classes_span,
             w_qkv, gain, grad_first, grad_w_out, grad_bias_out, grad_table, grad_context,
         ],
     )
@@ -568,14 +622,9 @@
         (attn_send, feed_passed, from_next, from_last)
     )
     attn_parts = list(add_cores(attn_keep, attn_send, devices))
-    feed_sums = add_chips(feed_parts, feed_passed)
-    feed_layers = [feed_sums[0]] + pass_layers(feed_sums, devices)
-    attn_parts[-1], feed_layers[1] = barrier((attn_parts[-1], feed_layers[1]))
+    feed_sum = add_layers(*add_chips(feed_parts, feed_passed), devices)
     attn_passed = pass_chips(attn_parts, devices)
-    attn_sums = add_chips(attn_parts, attn_passed)
-    attn_layers = [attn_sums[0]] + pass_layers(attn_sums, devices)
-    feed_sum = sum(part.astype(f32) for part in feed_layers)
-    attn_sum = sum(part.astype(f32) for part in attn_layers)
+    attn_sum = add_layers(*add_chips(attn_parts, attn_passed), devices)
     gap = jnp.zeros((token_rows - HALO, 2 * D), bf16)
     extra = jnp.concatenate([from_last, gap]) + jnp.concatenate([gap, from_next])
     own = slice(HALO, HALO + token_rows)

time: 114 us -> 115 us (level)
  waiting for transfers between devices: 29.1 us -> 34.6 us
  other arithmetic: 7.9 us -> 4.03 us
  between operations: 4.19 us -> 0.87 us
  local copies, waits for them, and re-layouts: 2.86 us -> 4.75 us
    unnamed x2 -> x10, local copies, waits for them, and re-layouts: 1.52 us -> 4.73 us
    ppermute x28 -> x26, waiting for transfers between devices: 26.2 us -> 28.9 us  [pass_on(): return lax.ppermute(value, 'fsdp', [(i, i ^ step) for i in range(devices)])]
    ppermute x2, waiting for transfers between devices: 0.01 us -> 2.04 us  [the longest x1 2.04 us: shards(): after = lax.ppermute(first_rows, 'fsdp', down)]
    reduce_sum x1 -> x0, other arithmetic: 1.96 us -> none  [plan_slots(): ends = jnp.sum((image_id == image_id[0]).astype(jnp.int32))]
    slice x2 -> x0, local copies, waits for them, and re-layouts: 1.22 us -> none  [the longest x1 1.19 us: plan_slots(): ends = jnp.sum((image_id == image_id[0]).astype(jnp.int32))]
    pallas_call x12 -> x15, Pallas kernels: 21.4 us -> 22.3 us  [call_kernel(): pl.pallas_call(kernel, out_shape=out_shapes, in_specs=specs, out_specs=[s...]
    ppermute x28 -> x26, starting transfers between devices: 40.8 us -> 41.7 us  [pass_on(): return lax.ppermute(value, 'fsdp', [(i, i ^ step) for i in range(devices)])]
  transfers between devices with their start and end apart: 32 -> 30, of which waited for: 13 -> 14; matrix products, arithmetic and copies ran while one was open for 8% -> 3% of each run, Pallas kernels for 12% -> 13%
where the time goes in v5:
time: 115 us
  starting transfers between devices  48 us (42%)
  waiting for transfers between devices  34.6 us (30%)
  Pallas kernels  22.3 us (19%)
  local copies, waits for them, and re-layouts  4.75 us (4%)
  other arithmetic  4.03 us (4%)
    ppermute x26, starting transfers between devices, pass_on(): return lax.ppermute(value, 'fsdp', [(i, i ^ step) for i in range(devices)])  41.7 us
    ppermute x26, waiting for transfers between devices, pass_on(): return lax.ppermute(value, 'fsdp', [(i, i ^ step) for i in range(devices)])  28.9 us
    pallas_call x15, Pallas kernels, call_kernel(): pl.pallas_call(kernel, out_shape=out_shapes, in_specs=specs, out_specs=[s...  22.3 us
    unnamed x10, local copies, waits for them, and re-layouts  4.73 us
    ppermute x1, waiting for transfers between devices, shards(): from_next = lax.ppermute(edges[:HALO], 'fsdp', down)  3.7 us
    unnamed x4, other arithmetic  2.44 us
    ppermute x1, starting transfers between devices, shards(): before = lax.ppermute(last_rows, 'fsdp', up)  2.4 us
  transfers between devices with their start and end apart: 30, of which 14 were waited for; matrix products, arithmetic and copies ran while one was open for 3% of the time, Pallas kernels for 13%

profile of v5, /device:TPU:0, one launch (start us, length us, event | category | flops | bytes accessed | tf_op | source)
XLA Modules:
  0.0 114.6 jit_solution(4158664887826045511)
XLA Ops:
  1.7 5.1 %collective-permute-start.5 = (bf16[152,128]{1,0:T(8,128)(2,1)S(1)}, bf16[152,128]{1,0:T(8,128)(2,1)S(1)}, u32[]{:S(2)}, u32[]{:S(2)}) collective-permute-start(bf16[152,128]{1,0:T(8,128)(2,1)S(1)} %pad.11.refs_0_), channel_id=1, source_target_pairs={{0,24},{1,25},{2,26},{3,27},{4,28},{5,29},{6,30},{7,31},{8,16},{9,... | collective-permute-start | bytes 116744 | tf_op jit(solution)/shard_map/ppermute | solution.py:63
  11.8 2.5 %collective-permute-start.8 = (bf16[4,152,128]{2,1,0:T(8,128)(2,1)S(1)}, bf16[4,152,128]{2,1,0:T(8,128)(2,1)S(1)}, u32[]{:S(2)}, u32[]{:S(2)}) collective-permute-start(bf16[4,152,128]{2,1,0:T(8,128)(2,1)S(1)} %shard_map.95.refs_0_), channel_id=1, source_target_pairs={{0,6},{1,7},{2,4},{3,5},{4,2},{5,3},{6,0},{7,1},{8,14},{9,15},{10,... | collective-permute-start | bytes 466952 | tf_op jit(solution)/shard_map/ppermute | solution.py:63
  16.6 3.7 %collective-permute-start.2 = (bf16[296,128]{1,0:T(8,128)(2,1)S(1)}, bf16[296,128]{1,0:T(8,128)(2,1)S(1)}, u32[]{:S(2)}, u32[]{:S(2)}) collective-permute-start(bf16[296,128]{1,0:T(8,128)(2,1)S(1)} %pad.10.refs_0_), channel_id=1, source_target_pairs={{0,24},{1,25},{2,26},{3,27},{4,28},{5,29},{6,30},{7,31},{8,16},{9,... | collective-permute-start | bytes 227336 | tf_op jit(solution)/shard_map/ppermute | solution.py:63
  20.3 2.7 %collective-permute-done.2.refs_3_ = bf16[296,128]{1,0:T(8,128)(2,1)S(1)} collective-permute-done((bf16[296,128]{1,0:T(8,128)(2,1)S(1)}, bf16[296,128]{1,0:T(8,128)(2,1)S(1)}, u32[]{:S(2)}, u32[]{:S(2)}) %collective-permute-start.2) | collective-permute-done | bytes 75808 | tf_op jit(solution)/shard_map/ppermute | solution.py:63
  27.6 2.4 %collective-permute-start.12 = (bf16[112,896]{1,0:T(8,128)(2,1)S(1)}, bf16[112,896]{1,0:T(8,128)(2,1)S(1)}, u32[]{:S(2)}, u32[]{:S(2)}) collective-permute-start(bf16[112,896]{1,0:T(8,128)(2,1)S(1)} %get-tuple-element.72), channel_id=1, source_target_pairs={{0,1},{1,2},{2,3},{3,4},{4,5},{5,6},{6,7},{7,8},{8,9},{9,10},{10,1... | collective-permute-start | bytes 602120 | tf_op jit(solution)/shard_map/ppermute | solution.py:541
  30.0 2.5 %collective-permute-start.11 = (bf16[4,296,128]{2,1,0:T(8,128)(2,1)S(1)}, bf16[4,296,128]{2,1,0:T(8,128)(2,1)S(1)}, u32[]{:S(2)}, u32[]{:S(2)}) collective-permute-start(bf16[4,296,128]{2,1,0:T(8,128)(2,1)S(1)} %shard_map.94.refs_0_), channel_id=1, source_target_pairs={{0,6},{1,7},{2,4},{3,5},{4,2},{5,3},{6,0},{7,1},{8,14},{9,15},{10,... | collective-permute-start | bytes 909320 | tf_op jit(solution)/shard_map/ppermute | solution.py:63
  34.8 2.0 %collective-permute-done.13.after_ref = bf16[112,896]{1,0:T(8,128)(2,1)S(1)} collective-permute-done((bf16[112,896]{1,0:T(8,128)(2,1)S(1)}, bf16[112,896]{1,0:T(8,128)(2,1)S(1)}, u32[]{:S(2)}, u32[]{:S(2)}) %collective-permute-start.13) | collective-permute-done | bytes 200736 | tf_op jit(solution)/shard_map/ppermute | solution.py:542
  36.9 4.3 %shard_map.97 = (f32[416,384]{1,0:T(8,128)S(1)}, bf16[416,384]{1,0:T(8,128)(2,1)S(1)}, bf16[416,384]{1,0:T(8,128)(2,1)S(1)}, bf16[416,384]{1,0:T(8,128)(2,1)S(1)...) custom-call(s32[8]{0:T(128)S(1)} %get-tuple-element.67.meta_ref, ...), custom_call_target="tpu_custom_call" | custom-call | flops 1 | bytes 1 | tf_op jit(solution)/shard_map/pallas_call | solution.py:456
  41.3 6.3 %collective-permute-done.10.refs_2_ = bf16[4,296,128]{2,1,0:T(8,128)(2,1)S(1)} collective-permute-done((bf16[4,296,128]{2,1,0:T(8,128)(2,1)S(1)}, bf16[4,296,128]{2,1,0:T(8,128)(2,1)S(1)}, u32[]{:S(2)}, u32[]{:S(2)}) %collective-permute-start.10) | collective-permute-done | bytes 303136 | tf_op jit(solution)/shard_map/ppermute | solution.py:63
  48.6 6.5 %collective-permute-start.15 = (bf16[4,4,296,128]{3,2,1,0:T(8,128)(2,1)S(1)}, bf16[4,4,296,128]{3,2,1,0:T(8,128)(2,1)S(1)}, u32[]{:S(2)}, u32[]{:S(2)}) collective-permute-start(bf16[4,4,296,128]{3,2,1,0:T(8,128)(2,1)S(1)} %shard_map.98.mine_ref), channel_id=1, source_target_pairs={{0,1},{1,0},{2,3},{3,2},{4,5},{5,4},{6,7},{7,6},{8,9},{9,8},{10,11... | collective-permute-start | bytes 3637256 | tf_op jit(solution)/shard_map/ppermute | solution.py:63
  55.1 2.5 %collective-permute-done.15.other_ref = bf16[4,4,296,128]{3,2,1,0:T(8,128)(2,1)S(1)} collective-permute-done((bf16[4,4,296,128]{3,2,1,0:T(8,128)(2,1)S(1)}, bf16[4,4,296,128]{3,2,1,0:T(8,128)(2,1)S(1)}, u32[]{:S(2)}, u32[]{:S(2)}) %collective-permute-start.15) | collective-permute-done | bytes 1212448 | tf_op jit(solution)/shard_map/ppermute | solution.py:63
  57.6 7.5 %shard_map.99 = (bf16[480,384]{1,0:T(8,128)(2,1)S(1)}, f32[416,384]{1,0:T(8,128)S(1)}, bf16[4,4,296,128]{3,2,1,0:T(8,128)(2,1)S(1)}, bf16[4,4,296,128]{3,2,1,0:T(8,128)(2,1)S(1)}) custom-call(s32[8]{0:T(128)S(1)} %get-tuple-element.67.meta_ref, f32[416,384]{1,0:T(8,128)S(1)} %get-tuple-element.77.middle_ref, ...), custom_call_target="tpu_custom_call" | custom-call | flops 1 | bytes 1 | tf_op jit(solution)/shard_map/pallas_call | solution.py:456
  65.6 3.5 %shard_map.101 = (bf16[208,1152]{1,0:T(8,128)(2,1)S(1)}, f32[384,384]{1,0:T(8,128)S(1)}, f32[1,384]{1,0:T(1,128)S(1)}, f32[8,128]{1,0:T(8,128)S(1)}, bf16[416,384]{1,0:T(8,128)(2,1)S(1)}) custom-call(s32[8]{0:T(128)S(1)} %get-tuple-element.67.meta_ref, f32[416,384]{1,0:T(8,128)S(1)} %get-tuple-element.83.grad_middle_ref, ...), custom_call_target="tpu_custom_call" | custom-call | flops 1 | bytes 1 | tf_op jit(solution)/shard_map/pallas_call | solution.py:456
  70.9 2.0 %collective-permute-start.19 = (bf16[4,296,128]{2,1,0:T(8,128)(2,1)S(1)}, bf16[4,296,128]{2,1,0:T(8,128)(2,1)S(1)}, u32[]{:S(2)}, u32[]{:S(2)}) collective-permute-start(bf16[4,296,128]{2,1,0:T(8,128)(2,1)S(1)} %get-tuple-element.108), channel_id=1, source_target_pairs={{0,6},{1,7},{2,4},{3,5},{4,2},{5,3},{6,0},{7,1},{8,14},{9,15},{10,... | collective-permute-start | bytes 909320 | tf_op jit(solution)/shard_map/ppermute | solution.py:63
  72.9 5.3 %shard_map.102 = (f32[480,384]{1,0:T(8,128)S(1)}, bf16[4,4,152,128]{3,2,1,0:T(8,128)(2,1)S(1)}, bf16[4,4,152,128]{3,2,1,0:T(8,128)(2,1)S(1)}) custom-call(s32[8]{0:T(128)S(1)} %get-tuple-element.67.meta_ref, f32[416,384]{1,0:T(8,128)S(1)} %get-tuple-element.83.grad_middle_ref, bf16[416,384]{1,0:T(8,128)(2,1)S(1)} %get-tuple-element.84.inputs_ref, ...), custom_call_target="tpu_custom_call" | custom-call | flops 1 | bytes 1 | tf_op jit(solution)/shard_map/pallas_call | solution.py:456
  80.9 3.7 %collective-permute-done.20 = bf16[112,768]{1,0:T(8,128)(2,1)S(1)} collective-permute-done((bf16[112,768]{1,0:T(8,128)(2,1)S(1)}, bf16[112,768]{1,0:T(8,128)(2,1)S(1)}, u32[]{:S(2)}, u32[]{:S(2)}) %collective-permute-start.20) | collective-permute-done | bytes 172064 | tf_op jit(solution)/shard_map/ppermute | solution.py:619
  86.4 2.4 %collective-permute-start.22 = (bf16[4,4,152,128]{3,2,1,0:T(8,128)(2,1)S(1)}, bf16[4,4,152,128]{3,2,1,0:T(8,128)(2,1)S(1)}, u32[]{:S(2)}, u32[]{:S(2)}) collective-permute-start(bf16[4,4,152,128]{3,2,1,0:T(8,128)(2,1)S(1)} %get-tuple-element.113), channel_id=1, source_target_pairs={{0,1},{1,0},{2,3},{3,2},{4,5},{5,4},{6,7},{7,6},{8,9},{9,8},{10,11... | collective-permute-start | bytes 1867784 | tf_op jit(solution)/shard_map/ppermute | solution.py:63
  88.9 2.2 %collective-permute-start.28 = (bf16[2,296,128]{2,1,0:T(8,128)(2,1)S(1)}, bf16[2,296,128]{2,1,0:T(8,128)(2,1)S(1)}, u32[]{:S(2)}, u32[]{:S(2)}) collective-permute-start(bf16[2,296,128]{2,1,0:T(8,128)(2,1)S(1)} %get-tuple-element.127), channel_id=1, source_target_pairs={{0,16},{1,17},{2,18},{3,19},{4,20},{5,21},{6,22},{7,23},{8,24},{9,... | collective-permute-start | bytes 454664 | tf_op jit(solution)/shard_map/ppermute | solution.py:63
  91.3 2.2 %collective-permute-start.23 = (bf16[4,152,128]{2,1,0:T(8,128)(2,1)S(1)}, bf16[4,152,128]{2,1,0:T(8,128)(2,1)S(1)}, u32[]{:S(2)}, u32[]{:S(2)}) collective-permute-start(bf16[4,152,128]{2,1,0:T(8,128)(2,1)S(1)} %get-tuple-element.115), channel_id=1, source_target_pairs={{0,2},{1,3},{2,0},{3,1},{4,6},{5,7},{6,4},{7,5},{8,10},{9,11},{10,... | collective-permute-start | bytes 466952 | tf_op jit(solution)/shard_map/ppermute | solution.py:63
  93.5 3.0 %collective-permute-start.24 = (bf16[4,152,128]{2,1,0:T(8,128)(2,1)S(1)}, bf16[4,152,128]{2,1,0:T(8,128)(2,1)S(1)}, u32[]{:S(2)}, u32[]{:S(2)}) collective-permute-start(bf16[4,152,128]{2,1,0:T(8,128)(2,1)S(1)} %get-tuple-element.116), channel_id=1, source_target_pairs={{0,4},{1,5},{2,6},{3,7},{4,0},{5,1},{6,2},{7,3},{8,12},{9,13},{10,... | collective-permute-start | bytes 466952 | tf_op jit(solution)/shard_map/ppermute | solution.py:63
  99.8 3.7 %collective-permute-done.24.refs_2_ = bf16[4,152,128]{2,1,0:T(8,128)(2,1)S(1)} collective-permute-done((bf16[4,152,128]{2,1,0:T(8,128)(2,1)S(1)}, bf16[4,152,128]{2,1,0:T(8,128)(2,1)S(1)}, u32[]{:S(2)}, u32[]{:S(2)}) %collective-permute-start.24) | collective-permute-done | bytes 155680 | tf_op jit(solution)/shard_map/ppermute | solution.py:63
  103.6 2.2 %collective-permute-start.26 = (bf16[2,152,128]{2,1,0:T(8,128)(2,1)S(1)}, bf16[2,152,128]{2,1,0:T(8,128)(2,1)S(1)}, u32[]{:S(2)}, u32[]{:S(2)}) collective-permute-start(bf16[2,152,128]{2,1,0:T(8,128)(2,1)S(1)} %get-tuple-element.119), channel_id=1, source_target_pairs={{0,16},{1,17},{2,18},{3,19},{4,20},{5,21},{6,22},{7,23},{8,24},{9,... | collective-permute-start | bytes 233480 | tf_op jit(solution)/shard_map/ppermute | solution.py:63
  106.5 3.3 %collective-permute-done.26.other_ref = bf16[2,152,128]{2,1,0:T(8,128)(2,1)S(1)} collective-permute-done((bf16[2,152,128]{2,1,0:T(8,128)(2,1)S(1)}, bf16[2,152,128]{2,1,0:T(8,128)(2,1)S(1)}, u32[]{:S(2)}, u32[]{:S(2)}) %collective-permute-start.26) | collective-permute-done | bytes 77856 | tf_op jit(solution)/shard_map/ppermute | solution.py:63
  110.8 3.1 %collective-permute-done.27 = bf16[1,152,128]{2,1,0:T(8,128)(2,1)S(1)} collective-permute-done((bf16[1,152,128]{2,1,0:T(8,128)(2,1)S(1)}, bf16[1,152,128]{2,1,0:T(8,128)(2,1)S(1)}, u32[]{:S(2)}, u32[]{:S(2)}) %collective-permute-start.27) | collective-permute-done | bytes 38944 | tf_op jit(solution)/shard_map/ppermute | solution.py:63
  (71 shorter events, 29.0 us)
Async XLA Ops:
  1.7 9.8 %collective-permute-start.5 = (bf16[152,128]{1,0:T(8,128)(2,1)S(1)}, bf16[152,128]{1,0:T(8,128)(2,1)S(1)}, u32[]{:S(2)}, u32[]{:S(2)}) collective-permute-start(bf16[152,128]{1,0:T(8,128)(2,1)S(1)} %pad.11.refs_0_), channel_id=1, source_target_pairs={{0,24},{1,25},{2,26},{3,27},{4,28},{5,29},{6,30},{7,31},{8,16},{9,... | collective-permute-start | bytes 116744 | tf_op jit(solution)/shard_map/ppermute | solution.py:63
  6.9 4.9 %collective-permute-start.4 = (bf16[152,128]{1,0:T(8,128)(2,1)S(1)}, bf16[152,128]{1,0:T(8,128)(2,1)S(1)}, u32[]{:S(2)}, u32[]{:S(2)}) collective-permute-start(bf16[152,128]{1,0:T(8,128)(2,1)S(1)} %pad.11.refs_0_), channel_id=1, source_target_pairs={{0,16},{1,17},{2,18},{3,19},{4,20},{5,21},{6,22},{7,23},{8,24},{9,... | collective-permute-start | bytes 116744 | tf_op jit(solution)/shard_map/ppermute | solution.py:63
  6.9 4.9 %collective-permute-start.3 = (bf16[152,128]{1,0:T(8,128)(2,1)S(1)}, bf16[152,128]{1,0:T(8,128)(2,1)S(1)}, u32[]{:S(2)}, u32[]{:S(2)}) collective-permute-start(bf16[152,128]{1,0:T(8,128)(2,1)S(1)} %pad.11.refs_0_), channel_id=1, source_target_pairs={{0,8},{1,9},{2,10},{3,11},{4,12},{5,13},{6,14},{7,15},{8,0},{9,1},... | collective-permute-start | bytes 116744 | tf_op jit(solution)/shard_map/ppermute | solution.py:63
  11.8 15.7 %collective-permute-start.8 = (bf16[4,152,128]{2,1,0:T(8,128)(2,1)S(1)}, bf16[4,152,128]{2,1,0:T(8,128)(2,1)S(1)}, u32[]{:S(2)}, u32[]{:S(2)}) collective-permute-start(bf16[4,152,128]{2,1,0:T(8,128)(2,1)S(1)} %shard_map.95.refs_0_), channel_id=1, source_target_pairs={{0,6},{1,7},{2,4},{3,5},{4,2},{5,3},{6,0},{7,1},{8,14},{9,15},{10,... | collective-permute-start | bytes 466952 | tf_op jit(solution)/shard_map/ppermute | solution.py:63
  14.3 13.2 %collective-permute-start.7 = (bf16[4,152,128]{2,1,0:T(8,128)(2,1)S(1)}, bf16[4,152,128]{2,1,0:T(8,128)(2,1)S(1)}, u32[]{:S(2)}, u32[]{:S(2)}) collective-permute-start(bf16[4,152,128]{2,1,0:T(8,128)(2,1)S(1)} %shard_map.95.refs_0_), channel_id=1, source_target_pairs={{0,4},{1,5},{2,6},{3,7},{4,0},{5,1},{6,2},{7,3},{8,12},{9,13},{10,... | collective-permute-start | bytes 466952 | tf_op jit(solution)/shard_map/ppermute | solution.py:63
  14.8 12.7 %collective-permute-start.6 = (bf16[4,152,128]{2,1,0:T(8,128)(2,1)S(1)}, bf16[4,152,128]{2,1,0:T(8,128)(2,1)S(1)}, u32[]{:S(2)}, u32[]{:S(2)}) collective-permute-start(bf16[4,152,128]{2,1,0:T(8,128)(2,1)S(1)} %shard_map.95.refs_0_), channel_id=1, source_target_pairs={{0,2},{1,3},{2,0},{3,1},{4,6},{5,7},{6,4},{7,5},{8,10},{9,11},{10,... | collective-permute-start | bytes 466952 | tf_op jit(solution)/shard_map/ppermute | solution.py:63
  16.6 6.4 %collective-permute-start.2 = (bf16[296,128]{1,0:T(8,128)(2,1)S(1)}, bf16[296,128]{1,0:T(8,128)(2,1)S(1)}, u32[]{:S(2)}, u32[]{:S(2)}) collective-permute-start(bf16[296,128]{1,0:T(8,128)(2,1)S(1)} %pad.10.refs_0_), channel_id=1, source_target_pairs={{0,24},{1,25},{2,26},{3,27},{4,28},{5,29},{6,30},{7,31},{8,16},{9,... | collective-permute-start | bytes 227336 | tf_op jit(solution)/shard_map/ppermute | solution.py:63
  20.3 5.3 %collective-permute-start.1 = (bf16[296,128]{1,0:T(8,128)(2,1)S(1)}, bf16[296,128]{1,0:T(8,128)(2,1)S(1)}, u32[]{:S(2)}, u32[]{:S(2)}) collective-permute-start(bf16[296,128]{1,0:T(8,128)(2,1)S(1)} %pad.10.refs_0_), channel_id=1, source_target_pairs={{0,16},{1,17},{2,18},{3,19},{4,20},{5,21},{6,22},{7,23},{8,24},{9,... | collective-permute-start | bytes 227336 | tf_op jit(solution)/shard_map/ppermute | solution.py:63
  27.5 9.4 %collective-permute-start.14 = (bf16[4,4,152,128]{3,2,1,0:T(8,128)(2,1)S(1)}, bf16[4,4,152,128]{3,2,1,0:T(8,128)(2,1)S(1)}, u32[]{:S(2)}, u32[]{:S(2)}) collective-permute-start(bf16[4,4,152,128]{3,2,1,0:T(8,128)(2,1)S(1)} %shard_map.96.mine_ref), channel_id=1, source_target_pairs={{0,1},{1,0},{2,3},{3,2},{4,5},{5,4},{6,7},{7,6},{8,9},{9,8},{10,11... | collective-permute-start | bytes 1867784 | tf_op jit(solution)/shard_map/ppermute | solution.py:63
  27.6 6.0 %collective-permute-start.12 = (bf16[112,896]{1,0:T(8,128)(2,1)S(1)}, bf16[112,896]{1,0:T(8,128)(2,1)S(1)}, u32[]{:S(2)}, u32[]{:S(2)}) collective-permute-start(bf16[112,896]{1,0:T(8,128)(2,1)S(1)} %get-tuple-element.72), channel_id=1, source_target_pairs={{0,1},{1,2},{2,3},{3,4},{4,5},{5,6},{6,7},{7,8},{8,9},{9,10},{10,1... | collective-permute-start | bytes 602120 | tf_op jit(solution)/shard_map/ppermute | solution.py:541
  30.0 11.2 %collective-permute-start.11 = (bf16[4,296,128]{2,1,0:T(8,128)(2,1)S(1)}, bf16[4,296,128]{2,1,0:T(8,128)(2,1)S(1)}, u32[]{:S(2)}, u32[]{:S(2)}) collective-permute-start(bf16[4,296,128]{2,1,0:T(8,128)(2,1)S(1)} %shard_map.94.refs_0_), channel_id=1, source_target_pairs={{0,6},{1,7},{2,4},{3,5},{4,2},{5,3},{6,0},{7,1},{8,14},{9,15},{10,... | collective-permute-start | bytes 909320 | tf_op jit(solution)/shard_map/ppermute | solution.py:63
  32.5 15.1 %collective-permute-start.10 = (bf16[4,296,128]{2,1,0:T(8,128)(2,1)S(1)}, bf16[4,296,128]{2,1,0:T(8,128)(2,1)S(1)}, u32[]{:S(2)}, u32[]{:S(2)}) collective-permute-start(bf16[4,296,128]{2,1,0:T(8,128)(2,1)S(1)} %shard_map.94.refs_0_), channel_id=1, source_target_pairs={{0,4},{1,5},{2,6},{3,7},{4,0},{5,1},{6,2},{7,3},{8,12},{9,13},{10,... | collective-permute-start | bytes 909320 | tf_op jit(solution)/shard_map/ppermute | solution.py:63
  33.0 15.5 %collective-permute-start.9 = (bf16[4,296,128]{2,1,0:T(8,128)(2,1)S(1)}, bf16[4,296,128]{2,1,0:T(8,128)(2,1)S(1)}, u32[]{:S(2)}, u32[]{:S(2)}) collective-permute-start(bf16[4,296,128]{2,1,0:T(8,128)(2,1)S(1)} %shard_map.94.refs_0_), channel_id=1, source_target_pairs={{0,2},{1,3},{2,0},{3,1},{4,6},{5,7},{6,4},{7,5},{8,10},{9,11},{10,... | collective-permute-start | bytes 909320 | tf_op jit(solution)/shard_map/ppermute | solution.py:63
  48.6 9.0 %collective-permute-start.15 = (bf16[4,4,296,128]{3,2,1,0:T(8,128)(2,1)S(1)}, bf16[4,4,296,128]{3,2,1,0:T(8,128)(2,1)S(1)}, u32[]{:S(2)}, u32[]{:S(2)}) collective-permute-start(bf16[4,4,296,128]{3,2,1,0:T(8,128)(2,1)S(1)} %shard_map.98.mine_ref), channel_id=1, source_target_pairs={{0,1},{1,0},{2,3},{3,2},{4,5},{5,4},{6,7},{7,6},{8,9},{9,8},{10,11... | collective-permute-start | bytes 3637256 | tf_op jit(solution)/shard_map/ppermute | solution.py:63
  69.4 15.3 %collective-permute-start.17 = (bf16[4,296,128]{2,1,0:T(8,128)(2,1)S(1)}, bf16[4,296,128]{2,1,0:T(8,128)(2,1)S(1)}, u32[]{:S(2)}, u32[]{:S(2)}) collective-permute-start(bf16[4,296,128]{2,1,0:T(8,128)(2,1)S(1)} %get-tuple-element.106), channel_id=1, source_target_pairs={{0,2},{1,3},{2,0},{3,1},{4,6},{5,7},{6,4},{7,5},{8,10},{9,11},{10,... | collective-permute-start | bytes 909320 | tf_op jit(solution)/shard_map/ppermute | solution.py:63
  70.9 15.4 %collective-permute-start.18 = (bf16[4,296,128]{2,1,0:T(8,128)(2,1)S(1)}, bf16[4,296,128]{2,1,0:T(8,128)(2,1)S(1)}, u32[]{:S(2)}, u32[]{:S(2)}) collective-permute-start(bf16[4,296,128]{2,1,0:T(8,128)(2,1)S(1)} %get-tuple-element.107), channel_id=1, source_target_pairs={{0,4},{1,5},{2,6},{3,7},{4,0},{5,1},{6,2},{7,3},{8,12},{9,13},{10,... | collective-permute-start | bytes 909320 | tf_op jit(solution)/shard_map/ppermute | solution.py:63
  70.9 15.4 %collective-permute-start.19 = (bf16[4,296,128]{2,1,0:T(8,128)(2,1)S(1)}, bf16[4,296,128]{2,1,0:T(8,128)(2,1)S(1)}, u32[]{:S(2)}, u32[]{:S(2)}) collective-permute-start(bf16[4,296,128]{2,1,0:T(8,128)(2,1)S(1)} %get-tuple-element.108), channel_id=1, source_target_pairs={{0,6},{1,7},{2,4},{3,5},{4,2},{5,3},{6,0},{7,1},{8,14},{9,15},{10,... | collective-permute-start | bytes 909320 | tf_op jit(solution)/shard_map/ppermute | solution.py:63
  79.6 5.0 %collective-permute-start.20 = (bf16[112,768]{1,0:T(8,128)(2,1)S(1)}, bf16[112,768]{1,0:T(8,128)(2,1)S(1)}, u32[]{:S(2)}, u32[]{:S(2)}) collective-permute-start(bf16[112,768]{1,0:T(8,128)(2,1)S(1)} %get-tuple-element.131), channel_id=1, source_target_pairs={{1,0},{2,1},{3,2},{4,3},{5,4},{6,5},{7,6},{8,7},{9,8},{10,9},{11,1... | collective-permute-start | bytes 516104 | tf_op jit(solution)/shard_map/ppermute | solution.py:619
  88.9 10.1 %collective-permute-start.28 = (bf16[2,296,128]{2,1,0:T(8,128)(2,1)S(1)}, bf16[2,296,128]{2,1,0:T(8,128)(2,1)S(1)}, u32[]{:S(2)}, u32[]{:S(2)}) collective-permute-start(bf16[2,296,128]{2,1,0:T(8,128)(2,1)S(1)} %get-tuple-element.127), channel_id=1, source_target_pairs={{0,16},{1,17},{2,18},{3,19},{4,20},{5,21},{6,22},{7,23},{8,24},{9,... | collective-permute-start | bytes 454664 | tf_op jit(solution)/shard_map/ppermute | solution.py:63
  91.3 8.5 %collective-permute-start.23 = (bf16[4,152,128]{2,1,0:T(8,128)(2,1)S(1)}, bf16[4,152,128]{2,1,0:T(8,128)(2,1)S(1)}, u32[]{:S(2)}, u32[]{:S(2)}) collective-permute-start(bf16[4,152,128]{2,1,0:T(8,128)(2,1)S(1)} %get-tuple-element.115), channel_id=1, source_target_pairs={{0,2},{1,3},{2,0},{3,1},{4,6},{5,7},{6,4},{7,5},{8,10},{9,11},{10,... | collective-permute-start | bytes 466952 | tf_op jit(solution)/shard_map/ppermute | solution.py:63
  93.5 10.0 %collective-permute-start.24 = (bf16[4,152,128]{2,1,0:T(8,128)(2,1)S(1)}, bf16[4,152,128]{2,1,0:T(8,128)(2,1)S(1)}, u32[]{:S(2)}, u32[]{:S(2)}) collective-permute-start(bf16[4,152,128]{2,1,0:T(8,128)(2,1)S(1)} %get-tuple-element.116), channel_id=1, source_target_pairs={{0,4},{1,5},{2,6},{3,7},{4,0},{5,1},{6,2},{7,3},{8,12},{9,13},{10,... | collective-permute-start | bytes 466952 | tf_op jit(solution)/shard_map/ppermute | solution.py:63
  96.5 7.0 %collective-permute-start.25 = (bf16[4,152,128]{2,1,0:T(8,128)(2,1)S(1)}, bf16[4,152,128]{2,1,0:T(8,128)(2,1)S(1)}, u32[]{:S(2)}, u32[]{:S(2)}) collective-permute-start(bf16[4,152,128]{2,1,0:T(8,128)(2,1)S(1)} %get-tuple-element.117), channel_id=1, source_target_pairs={{0,6},{1,7},{2,4},{3,5},{4,2},{5,3},{6,0},{7,1},{8,14},{9,15},{10,... | collective-permute-start | bytes 466952 | tf_op jit(solution)/shard_map/ppermute | solution.py:63
  99.0 10.9 %collective-permute-start.29 = (bf16[1,296,128]{2,1,0:T(8,128)(2,1)S(1)}, bf16[1,296,128]{2,1,0:T(8,128)(2,1)S(1)}, u32[]{:S(2)}, u32[]{:S(2)}) collective-permute-start(bf16[1,296,128]{2,1,0:T(8,128)(2,1)S(1)} %get-tuple-element.129), channel_id=1, source_target_pairs={{0,8},{1,9},{2,10},{3,11},{4,12},{5,13},{6,14},{7,15},{8,0},{9,1},... | collective-permute-start | bytes 227336 | tf_op jit(solution)/shard_map/ppermute | solution.py:63
  103.6 6.2 %collective-permute-start.26 = (bf16[2,152,128]{2,1,0:T(8,128)(2,1)S(1)}, bf16[2,152,128]{2,1,0:T(8,128)(2,1)S(1)}, u32[]{:S(2)}, u32[]{:S(2)}) collective-permute-start(bf16[2,152,128]{2,1,0:T(8,128)(2,1)S(1)} %get-tuple-element.119), channel_id=1, source_target_pairs={{0,16},{1,17},{2,18},{3,19},{4,20},{5,21},{6,22},{7,23},{8,24},{9,... | collective-permute-start | bytes 233480 | tf_op jit(solution)/shard_map/ppermute | solution.py:63
  (10 other events, 26.3 us)

commit v6 on v5

--- a/solution.py
+++ b/solution.py
@@ -119,6 +119,12 @@
         refs[-1][layer] = part_ref[...]
 
 
+def join_kernel(near_ref, far_ref, joined_ref):
+    half = near_ref.shape[0]
+    joined_ref[:half] = near_ref[...]
+    joined_ref[half:] = far_ref[...]
+
+
 def add_cores_kernel(keep_ref, other_ref, *out_refs):
     for spot, out_ref in enumerate(out_refs):
         total = keep_ref[spot].astype(f32) + other_ref[spot].astype(f32)
@@ -155,21 +161,37 @@
     return jnp.where(inside, 1.0, 0.0)
 
 
+def edge_rows(core, near_core, last):
+    return pl.ds(pl.multiple_of(jnp.where(core == near_core, last, 0), 16), HALO)
+
+
 def prepare_kernel(
-    last_device, device_ref, image_ref, bias_ref, inputs_ref, out_grad_ref,
-    tokens_ref, first_ref, last_ref, meta_ref,
+    last_device, device_ref, image_hbm, bias_hbm, inputs_hbm, out_grad_hbm,
+    tokens_ref, inner_ref, outer_ref, meta_ref,
+    image_ref, bias_ref, semaphores,
 ):
-    token_rows = inputs_ref.shape[0]
-    tokens_ref[:, :D] = inputs_ref[...]
-    tokens_ref[:, D : 2 * D] = out_grad_ref[...]
+    token_rows = tokens_ref.shape[0]
+    moves = [
+        pltpu.make_async_copy(source, target, semaphores.at[step])
+        for step, (source, target) in enumerate(
+            [
+                (bias_hbm, bias_ref),
+                (image_hbm, image_ref),
+                (inputs_hbm, tokens_ref.at[:, 0:D]),
+                (out_grad_hbm, tokens_ref.at[:, D : 2 * D]),
+            ]
+        )
+    ]
+    for move in moves:
+        move.start()
     entry = sixth(lax.broadcasted_iota(jnp.int32, (LANES, LANES), 0))
     inside = entry < NB
+    moves[0].wait()
     for step in range(token_rows // LANES):
         same = inside & (entry == bias_ref[step : step + 1])
         classes = jnp.transpose(jnp.where(same, 1.0, 0.0))
         tokens_ref[step * LANES : (step + 1) * LANES, 2 * D :] = classes.astype(bf16)
-    first_ref[...] = tokens_ref[:HALO]
-    last_ref[...] = tokens_ref[token_rows - HALO :]
+    moves[1].wait()
     images = image_ref[...]
     ends = jnp.sum(jnp.where(images == images[0:1, 0:1], 1, 0))
     device = device_ref[0]
@@ -188,6 +210,11 @@
     meta_ref[5] = device >> 3
     meta_ref[6] = (device >> 1) & (SQUARE - 1)
     meta_ref[7] = 0
+    moves[2].wait()
+    moves[3].wait()
+    core = device & (CORES - 1)
+    inner_ref[...] = tokens_ref[edge_rows(core, 0, token_rows - HALO)]
+    outer_ref[...] = tokens_ref[edge_rows(core, 1, token_rows - HALO)]
 
 
 def read_vector(flat_ref, at, amount):
@@ -235,7 +262,7 @@
 
 
 def attend_kernel(
-    meta_ref, before_ref, own_ref, after_ref,
+    meta_ref, inner_ref, own_ref, outer_ref,
     mine_ref, other_ref,
     middle_ref, cotangent_ref, inputs_ref, normed_ref, qkv_ref, probability_ref,
     context_ref, classes_ref, w_qkv_ref, w_out_ref, gain_ref,
@@ -253,11 +280,10 @@
     bias_out = read_vector(flat_ref, BIAS_OUT_AT, D_ROWS)
     table = (head_mask() * flat_ref[TABLE_AT : TABLE_AT + 1]).astype(bf16)
 
-    halo = before_ref.shape[0]
     own = own_ref.shape[0]
-    window_ref[0:halo] = before_ref[...]
-    window_ref[halo : halo + own] = own_ref[...]
-    window_ref[halo + own : window] = after_ref[...]
+    window_ref[edge_rows(meta_ref[4], 0, HALO + own)] = inner_ref[...]
+    window_ref[HALO : HALO + own] = own_ref[...]
+    window_ref[edge_rows(meta_ref[4], 1, HALO + own)] = outer_ref[...]
     picked = dot(slot_mask(meta_ref, window, False), window_ref[...])
     inputs = picked[:, :D]
     inputs_ref[...] = inputs.astype(bf16)
@@ -406,11 +432,11 @@
 
 
 def inputs_back_kernel(
-    meta_ref, grad_middle_ref, inputs_ref, normed_ref, qkv_ref, probability_ref,
+    meta_ref, grad_middle_ref, output_ref, inputs_ref, normed_ref, qkv_ref, probability_ref,
     classes_ref, w_qkv_ref, gain_ref,
     grad_first_ref, grad_w_out_ref, grad_bias_out_ref, grad_table_ref, grad_context_ref,
-    grad_inputs_ref, keep_ref, send_ref,
-    flat_ref, grad_second_ref, grad_qkv_ref,
+    own_output_ref, own_grad_ref, inner_ref, outer_ref, keep_ref, send_ref,
+    flat_ref, grad_second_ref, grad_qkv_ref, grad_inputs_ref,
 ):
     window = grad_inputs_ref.shape[0]
     grad_table = grad_table_ref[...] + slot_back(
@@ -446,20 +472,43 @@
     low_part = (grad_inputs - high.astype(f32)).astype(bf16)
     back = slot_mask(meta_ref, window, True)
     grad_inputs_ref[...] = dot(back, high) + dot(back, low_part)
+    own = slice(HALO, window - HALO)
+    own_output_ref[...] = output_ref[own]
+    own_grad_ref[...] = grad_inputs_ref[own]
+    for near_core, edge_ref in enumerate((inner_ref, outer_ref)):
+        edge = edge_rows(meta_ref[4], near_core, window - HALO)
+        edge_ref[:, :D] = output_ref[edge]
+        edge_ref[:, D:] = grad_inputs_ref[edge].astype(bf16)
     cut_blocks(meta_ref, flat_ref, keep_ref, send_ref)
 
 
-def call_kernel(kernel, out_shapes, scratch, flops, operands):
+def combine_kernel(
+    meta_ref, own_output_ref, own_grad_ref, inner_ref, outer_ref, output_ref, grad_inputs_ref
+):
+    last = output_ref.shape[0] - HALO
+    output_ref[HALO:last] = own_output_ref[HALO:last]
+    grad_inputs_ref[HALO:last] = own_grad_ref[HALO:last]
+    for near_core, edge_ref in enumerate((inner_ref, outer_ref)):
+        edge = edge_rows(meta_ref[4], near_core, last)
+        output_ref[edge] = (
+            own_output_ref[edge].astype(f32) + edge_ref[:, :D].astype(f32)
+        ).astype(bf16)
+        grad_inputs_ref[edge] = own_grad_ref[edge] + edge_ref[:, D:].astype(f32)
+
+
+def call_kernel(kernel, out_shapes, scratch, flops, operands, far=(), room=32 * 1024 * 1024):
     vmem = pl.BlockSpec(memory_space=pltpu.VMEM)
     smem = pl.BlockSpec(memory_space=pltpu.SMEM)
-    specs = [smem if operand.dtype == jnp.int32 and operand.ndim == 1 else vmem for operand in operands]
+    specs = [smem if operand.dtype == jnp.int32 else vmem for operand in operands]
+    for index in far:
+        specs[index] = pl.BlockSpec(memory_space=pltpu.HBM)
     return pl.pallas_call(
         kernel,
         out_shape=out_shapes,
         in_specs=specs,
         out_specs=[smem if shape.dtype == jnp.int32 else vmem for shape in out_shapes],
         scratch_shapes=scratch,
-        compiler_params=pltpu.CompilerParams(vmem_limit_bytes=32 * 1024 * 1024),
+        compiler_params=pltpu.CompilerParams(vmem_limit_bytes=room),
         cost_estimate=pl.CostEstimate(flops=flops, bytes_accessed=1, transcendentals=0),
     )(*operands)
 
@@ -478,19 +527,26 @@
     return pack([rows] + pass_layers([rows] * depth, devices))
 
 
+def double_column(column, devices):
+    half = column.shape[0]
+    far = pass_on(column, half * CORES * SQUARE, devices)
+    joined = struct((2 * half,) + column.shape[1:], bf16)
+    return call_kernel(join_kernel, [joined], [], 1, [column, far])[0]
+
+
 def gather_planes(column, devices):
     return pack([column] + pass_chips([column] * SQUARE, devices))
 
 
-def add_cores(keep, send, devices):
+def add_cores(keep, other):
     parts = [struct(keep.shape[1:], bf16)] * SQUARE
-    return call_kernel(add_cores_kernel, parts, [], 1, [keep, pass_cores(send, devices)])
-
-
-def add_chips(parts, passed):
+    return call_kernel(add_cores_kernel, parts, [], 1, [keep, other])
+
+
+def add_chips(parts, passed, flops=1):
     depth, padded, lanes = parts[0].shape
     halves = [struct((depth // 2, padded, lanes), bf16)] * 2
-    return call_kernel(add_chips_kernel, halves, [], 1, [parts[0]] + passed)
+    return call_kernel(add_chips_kernel, halves, [], flops, [parts[0]] + passed)
 
 
 def add_layers(keep, send, devices):
@@ -513,9 +569,9 @@
     mlp_flat = devices * mlp_blocks.shape[1] // LANES
     barrier = lax.optimization_barrier
 
-    up = [(i, i + 1) for i in range(devices - 1)]
-    down = [(i + 1, i) for i in range(devices - 1)]
-    tokens, first_rows, last_rows, meta = call_kernel(
+    outside = [(i, i + 1) for i in range(1, devices - 1, 2)]
+    outside = outside + [(b, a) for a, b in outside]
+    tokens, inner, outer, meta = call_kernel(
         functools.partial(prepare_kernel, devices - 1),
         [
             struct((token_rows, WIDE), bf16),
@@ -523,7 +579,11 @@
             struct((HALO, WIDE), bf16),
             struct((8,), jnp.int32),
         ],
-        [],
+        [
+            pltpu.VMEM((token_rows // LANES, LANES), jnp.int32),
+            pltpu.VMEM((token_rows // LANES, LANES), jnp.int32),
+            pltpu.SemaphoreType.DMA((4,)),
+        ],
         1,
         [
             lax.axis_index("fsdp").astype(jnp.int32).reshape(1),
@@ -532,17 +592,21 @@
             inputs,
             out_grad,
         ],
+        (1, 2, 3, 4),
+        60 * 1024 * 1024,
     )
     attn_rows = as_rows(attn_blocks)
     mlp_rows = as_rows(mlp_blocks)
     attn_column = gather_columns(attn_rows, devices)
-    mlp_parts = pass_layers([mlp_rows] * depth, devices)
-    attn_column, first_rows, last_rows = barrier((attn_column, first_rows, last_rows))
-    before = lax.ppermute(last_rows, "fsdp", up)
-    after = lax.ppermute(first_rows, "fsdp", down)
-    mlp_column = pack([mlp_rows] + mlp_parts)
+    mlp_column = double_column(mlp_rows[None], devices)
+    attn_column, mlp_column, inner, outer = barrier((attn_column, mlp_column, inner, outer))
+    inner = pass_cores(inner, devices)
+    outer = lax.ppermute(outer, "fsdp", outside)
+    mlp_column, inner = barrier((mlp_column, inner))
+    while mlp_column.shape[0] < depth:
+        mlp_column = double_column(mlp_column, devices)
     attn_mine = gather_planes(attn_column, devices)
-    mlp_column, attn_mine = barrier((mlp_column, attn_mine))
+    mlp_column, attn_mine, inner, outer = barrier((mlp_column, attn_mine, inner, outer))
     mlp_passed = pass_chips([mlp_column] * SQUARE, devices)
     attn_other = pass_cores(attn_mine, devices)
 
@@ -566,7 +630,7 @@
         ],
         [pltpu.VMEM((attn_flat + 16, LANES), f32), pltpu.VMEM((window, WIDE), bf16)],
         1,
-        [meta, before, tokens, after, attn_mine, attn_other],
+        [meta, inner, tokens, outer, attn_mine, attn_other],
     )
     mlp_passed, middle = barrier((mlp_passed, middle))
     mlp_mine = pack([mlp_column] + mlp_passed)
@@ -584,7 +648,7 @@
         1,
         [meta, middle, cotangent, mlp_mine, mlp_other],
     )
-    feed_parts = add_cores(feed_keep, feed_send, devices)
+    feed_parts = add_cores(feed_keep, pass_cores(feed_send, devices))
     grad_first, grad_w_out, grad_bias_out, grad_table, grad_context = call_kernel(
         attend_back_kernel,
         [
@@ -601,35 +665,46 @@
     feed_parts, grad_first = barrier((feed_parts, grad_first))
     feed_passed = pass_chips(feed_parts, devices)
     attn_blocks_out = struct((SQUARE,) + attn_column.shape, bf16)
-    grad_inputs, attn_keep, attn_send = call_kernel(
+    own_output, own_grad, inner, outer, attn_keep, attn_send = call_kernel(
         inputs_back_kernel,
-        [struct((window, D), f32), attn_blocks_out, attn_blocks_out],
+        [
+            struct((token_rows, D), bf16),
+            struct((token_rows, D), f32),
+            struct((HALO, 2 * D), bf16),
+            struct((HALO, 2 * D), bf16),
+            attn_blocks_out,
+            attn_blocks_out,
+        ],
         [
             pltpu.VMEM((attn_flat + 16, LANES), f32),
             pltpu.VMEM((SLOT, 3 * D), bf16),
             pltpu.VMEM((SPAN, 3 * D), bf16),
+            pltpu.VMEM((window, D), f32),
         ],
         1,
         [
-            meta, grad_middle, inputs_span, normed, qkv, probability, classes_span,
+            meta, grad_middle, output, inputs_span, normed, qkv, probability, classes_span,
             w_qkv, gain, grad_first, grad_w_out, grad_bias_out, grad_table, grad_context,
         ],
     )
-    edges = jnp.concatenate([output, grad_inputs.astype(bf16)], axis=1)
-    from_next = lax.ppermute(edges[:HALO], "fsdp", down)
-    from_last = lax.ppermute(edges[window - HALO :], "fsdp", up)
-    attn_send, feed_passed, from_next, from_last = barrier(
-        (attn_send, feed_passed, from_next, from_last)
-    )
-    attn_parts = list(add_cores(attn_keep, attn_send, devices))
-    feed_sum = add_layers(*add_chips(feed_parts, feed_passed), devices)
+    attn_other = pass_cores(attn_send, devices)
+    feed_keep, feed_send = add_chips(feed_parts, feed_passed, 10**10)
+    outer = lax.ppermute(outer, "fsdp", outside)
+    attn_other, feed_keep, feed_send, outer = barrier((attn_other, feed_keep, feed_send, outer))
+    attn_parts = list(add_cores(attn_keep, attn_other))
     attn_passed = pass_chips(attn_parts, devices)
-    attn_sum = add_layers(*add_chips(attn_parts, attn_passed), devices)
-    gap = jnp.zeros((token_rows - HALO, 2 * D), bf16)
-    extra = jnp.concatenate([from_last, gap]) + jnp.concatenate([gap, from_next])
-    own = slice(HALO, HALO + token_rows)
-    output = output[own] + extra[:, :D]
-    grad_inputs = grad_inputs[own] + extra[:, D:].astype(f32)
+    attn_keep, attn_send = add_chips(attn_parts, attn_passed)
+    attn_keep, inner = barrier((attn_keep, inner))
+    inner = pass_cores(inner, devices)
+    feed_sum = add_layers(feed_keep, feed_send, devices)
+    attn_sum = add_layers(attn_keep, attn_send, devices)
+    output, grad_inputs = call_kernel(
+        combine_kernel,
+        [struct((token_rows, D), bf16), struct((token_rows, D), f32)],
+        [],
+        1,
+        [meta, own_output, own_grad, inner, outer],
+    )
     return (output, grad_inputs, as_block(attn_sum, attn_blocks), as_block(feed_sum, mlp_blocks))
 
 

time: 115 us -> 105 us (0.913)
  starting transfers between devices: 48 us -> 37.8 us
  local copies, waits for them, and re-layouts: 4.75 us -> 1.55 us
  waiting for transfers between devices: 34.6 us -> 37.5 us
  Pallas kernels: 22.3 us -> 25 us
  other arithmetic: 4.03 us -> 2.44 us
    ppermute x26 -> x27, waiting for transfers between devices: 28.9 us -> 37.5 us  [pass_on(): return lax.ppermute(value, 'fsdp', [(i, i ^ step) for i in range(devices)])]
    ppermute x4 -> x2, waiting for transfers between devices: 5.75 us -> 0.01 us  [shards(): outer = lax.ppermute(outer, 'fsdp', outside)]
    ppermute x26 -> x27, starting transfers between devices: 41.7 us -> 36.5 us  [pass_on(): return lax.ppermute(value, 'fsdp', [(i, i ^ step) for i in range(devices)])]
    ppermute x4 -> x2, starting transfers between devices: 6.27 us -> 1.35 us  [shards(): outer = lax.ppermute(outer, 'fsdp', outside)]
    unnamed x10 -> x6, local copies, waits for them, and re-layouts: 4.73 us -> 1.53 us
    pallas_call x15 -> x17, Pallas kernels: 22.3 us -> 25 us  [call_kernel(): pl.pallas_call(kernel, out_shape=out_shapes, in_specs=specs, out_specs=[s...]
    add x2 -> x0, other arithmetic: 1.51 us -> none  [the longest x1 0.79 us: shards(): grad_inputs = grad_inputs[own] + extra[:, D:].astype(f32)]
  transfers between devices with their start and end apart: 30 -> 29, of which waited for: 14 -> 14; matrix products, arithmetic and copies ran while one was open for 3% -> 3% of each run, Pallas kernels for 13% -> 15%
where the time goes in v6:
time: 105 us
  starting transfers between devices  37.8 us (36%)
  waiting for transfers between devices  37.5 us (36%)
  Pallas kernels  25 us (24%)
  other arithmetic  2.44 us (2%)
  local copies, waits for them, and re-layouts  1.55 us (1%)
    ppermute x27, waiting for transfers between devices, pass_on(): return lax.ppermute(value, 'fsdp', [(i, i ^ step) for i in range(devices)])  37.5 us
    ppermute x27, starting transfers between devices, pass_on(): return lax.ppermute(value, 'fsdp', [(i, i ^ step) for i in range(devices)])  36.5 us
    pallas_call x17, Pallas kernels, call_kernel(): pl.pallas_call(kernel, out_shape=out_shapes, in_specs=specs, out_specs=[s...  25 us
    unnamed x4, other arithmetic  2.44 us
  transfers between devices with their start and end apart: 29, of which 14 were waited for; matrix products, arithmetic and copies ran while one was open for 3% of the time, Pallas kernels for 15%

profile of v6, /device:TPU:0, one launch (start us, length us, event | category | flops | bytes accessed | tf_op | source)
XLA Modules:
  0.0 105.2 jit_solution(2462034545320105245)
XLA Ops:
  2.0 3.1 %collective-permute-start.3 = (bf16[1,296,128]{2,1,0:T(8,128)(2,1)S(1)}, bf16[1,296,128]{2,1,0:T(8,128)(2,1)S(1)}, u32[]{:S(2)}, u32[]{:S(2)}) collective-permute-start(bf16[1,296,128]{2,1,0:T(8,128)(2,1)S(1)} %pad_bitcast_fusion.near_ref), channel_id=1, source_target_pairs={{0,8},{1,9},{2,10},{3,11},{4,12},{5,13},{6,14},{7,15},{8,0},{9,1},... | collective-permute-start | bytes 227336 | tf_op jit(solution)/shard_map/ppermute | solution.py:63
  6.2 2.5 %collective-permute-start.2 = (bf16[152,128]{1,0:T(8,128)(2,1)S(1)}, bf16[152,128]{1,0:T(8,128)(2,1)S(1)}, u32[]{:S(2)}, u32[]{:S(2)}) collective-permute-start(bf16[152,128]{1,0:T(8,128)(2,1)S(1)} %pad.8.refs_0_), channel_id=1, source_target_pairs={{0,24},{1,25},{2,26},{3,27},{4,28},{5,29},{6,30},{7,31},{8,16},{9,... | collective-permute-start | bytes 116744 | tf_op jit(solution)/shard_map/ppermute | solution.py:63
  8.9 1.7 %collective-permute-start = (bf16[152,128]{1,0:T(8,128)(2,1)S(1)}, bf16[152,128]{1,0:T(8,128)(2,1)S(1)}, u32[]{:S(2)}, u32[]{:S(2)}) collective-permute-start(bf16[152,128]{1,0:T(8,128)(2,1)S(1)} %pad.8.refs_0_), channel_id=1, source_target_pairs={{0,8},{1,9},{2,10},{3,11},{4,12},{5,13},{6,14},{7,15},{8,0},{9,1},... | collective-permute-start | bytes 116744 | tf_op jit(solution)/shard_map/ppermute | solution.py:63
  10.6 2.0 %shard_map.93 = (bf16[256,896]{1,0:T(8,128)(2,1)}, bf16[112,896]{1,0:T(8,128)(2,1)}, bf16[112,896]{1,0:T(8,128)(2,1)}, s32[8]{0:T(128)}) custom-call(s32[1]{0:T(128)} %bitcast.device_ref, s32[2,128]{1,0:T(2,128)} %bitcast.21, s32[2,128]{1,0:T(2,128)} %bitcast.22, bf16[256,384]{1,0:T(8,128)(2,1)} %inputs_hbm.1, bf16[256,384]{1,0:T(8,128)(2,1)} %out_grad_hbm.1), custom_call_target="tpu_custom_call" | custom-call | flops 1 | bytes 1 | tf_op jit(solution)/shard_map/pallas_call | solution.py:505
  14.8 4.4 %collective-permute-start.8 = (bf16[4,152,128]{2,1,0:T(8,128)(2,1)S(1)}, bf16[4,152,128]{2,1,0:T(8,128)(2,1)S(1)}, u32[]{:S(2)}, u32[]{:S(2)}) collective-permute-start(bf16[4,152,128]{2,1,0:T(8,128)(2,1)S(1)} %shard_map.94.refs_0_), channel_id=1, source_target_pairs={{0,6},{1,7},{2,4},{3,5},{4,2},{5,3},{6,0},{7,1},{8,14},{9,15},{10,... | collective-permute-start | bytes 466952 | tf_op jit(solution)/shard_map/ppermute | solution.py:63
  20.6 3.0 %collective-permute-start.5 = (bf16[2,296,128]{2,1,0:T(8,128)(2,1)S(1)}, bf16[2,296,128]{2,1,0:T(8,128)(2,1)S(1)}, u32[]{:S(2)}, u32[]{:S(2)}) collective-permute-start(bf16[2,296,128]{2,1,0:T(8,128)(2,1)S(1)} %shard_map.95.near_ref), channel_id=1, source_target_pairs={{0,16},{1,17},{2,18},{3,19},{4,20},{5,21},{6,22},{7,23},{8,24},{9,... | collective-permute-start | bytes 454664 | tf_op jit(solution)/shard_map/ppermute | solution.py:63
  23.6 4.4 %collective-permute-done.8.refs_3_ = bf16[4,152,128]{2,1,0:T(8,128)(2,1)S(1)} collective-permute-done((bf16[4,152,128]{2,1,0:T(8,128)(2,1)S(1)}, bf16[4,152,128]{2,1,0:T(8,128)(2,1)S(1)}, u32[]{:S(2)}, u32[]{:S(2)}) %collective-permute-start.8) | collective-permute-done | bytes 155680 | tf_op jit(solution)/shard_map/ppermute | solution.py:63
  28.7 1.9 %collective-permute-done.6.refs_1_ = bf16[4,152,128]{2,1,0:T(8,128)(2,1)S(1)} collective-permute-done((bf16[4,152,128]{2,1,0:T(8,128)(2,1)S(1)}, bf16[4,152,128]{2,1,0:T(8,128)(2,1)S(1)}, u32[]{:S(2)}, u32[]{:S(2)}) %collective-permute-start.6) | collective-permute-done | bytes 155680 | tf_op jit(solution)/shard_map/ppermute | solution.py:63
  30.9 2.0 %collective-permute-start.12 = (bf16[4,296,128]{2,1,0:T(8,128)(2,1)S(1)}, bf16[4,296,128]{2,1,0:T(8,128)(2,1)S(1)}, u32[]{:S(2)}, u32[]{:S(2)}) collective-permute-start(bf16[4,296,128]{2,1,0:T(8,128)(2,1)S(1)} %shard_map.96.refs_0_), channel_id=1, source_target_pairs={{0,6},{1,7},{2,4},{3,5},{4,2},{5,3},{6,0},{7,1},{8,14},{9,15},{10,... | collective-permute-start | bytes 909320 | tf_op jit(solution)/shard_map/ppermute | solution.py:63
  34.4 4.3 %shard_map.98 = (f32[416,384]{1,0:T(8,128)S(1)}, bf16[416,384]{1,0:T(8,128)(2,1)S(1)}, bf16[416,384]{1,0:T(8,128)(2,1)S(1)}, bf16[416,384]{1,0:T(8,128)(2,1)S(1)...) custom-call(s32[8]{0:T(128)S(1)} %copy-done.1, ...), custom_call_target="tpu_custom_call" | custom-call | flops 1 | bytes 1 | tf_op jit(solution)/shard_map/pallas_call | solution.py:505
  38.8 3.1 %collective-permute-done.12.refs_3_ = bf16[4,296,128]{2,1,0:T(8,128)(2,1)S(1)} collective-permute-done((bf16[4,296,128]{2,1,0:T(8,128)(2,1)S(1)}, bf16[4,296,128]{2,1,0:T(8,128)(2,1)S(1)}, u32[]{:S(2)}, u32[]{:S(2)}) %collective-permute-start.12) | collective-permute-done | bytes 303136 | tf_op jit(solution)/shard_map/ppermute | solution.py:63
  41.9 5.9 %collective-permute-done.11.refs_2_ = bf16[4,296,128]{2,1,0:T(8,128)(2,1)S(1)} collective-permute-done((bf16[4,296,128]{2,1,0:T(8,128)(2,1)S(1)}, bf16[4,296,128]{2,1,0:T(8,128)(2,1)S(1)}, u32[]{:S(2)}, u32[]{:S(2)}) %collective-permute-start.11) | collective-permute-done | bytes 303136 | tf_op jit(solution)/shard_map/ppermute | solution.py:63
  48.0 2.9 %collective-permute-done.14.other_ref = bf16[4,4,296,128]{3,2,1,0:T(8,128)(2,1)S(1)} collective-permute-done((bf16[4,4,296,128]{3,2,1,0:T(8,128)(2,1)S(1)}, bf16[4,4,296,128]{3,2,1,0:T(8,128)(2,1)S(1)}, u32[]{:S(2)}, u32[]{:S(2)}) %collective-permute-start.14) | collective-permute-done | bytes 1212448 | tf_op jit(solution)/shard_map/ppermute | solution.py:63
  50.8 7.5 %shard_map.100 = (bf16[480,384]{1,0:T(8,128)(2,1)S(1)}, f32[416,384]{1,0:T(8,128)S(1)}, bf16[4,4,296,128]{3,2,1,0:T(8,128)(2,1)S(1)}, bf16[4,4,296,128]{3,2,1,0:T(8,128)(2,1)S(1)}) custom-call(s32[8]{0:T(128)S(1)} %copy-done.1, f32[416,384]{1,0:T(8,128)S(1)} %get-tuple-element.92.middle_ref, bf16[416,384]{1,0:T(8,128)(2,1)S(1)} %get-tuple-element.93.cotangent_ref, ...), custom_call_target="tpu_custom_call" | custom-call | flops 1 | bytes 1 | tf_op jit(solution)/shard_map/pallas_call | solution.py:505
  58.5 3.5 %shard_map.102 = (bf16[208,1152]{1,0:T(8,128)(2,1)S(1)}, f32[384,384]{1,0:T(8,128)S(1)}, f32[1,384]{1,0:T(1,128)S(1)}, f32[8,128]{1,0:T(8,128)S(1)}, bf16[416,384]{1,0:T(8,128)(2,1)S(1)}) custom-call(s32[8]{0:T(128)S(1)} %copy-done.1, f32[416,384]{1,0:T(8,128)S(1)} %get-tuple-element.97.grad_middle_ref, bf16[416,1152]{1,0:T(8,128)(2,1)S(1)} %get-tuple-element.101.qkv_ref, ...), custom_call_target="tpu_custom_call" | custom-call | flops 1 | bytes 1 | tf_op jit(solution)/shard_map/pallas_call | solution.py:505
  65.9 5.4 %shard_map.103 = (bf16[256,384]{1,0:T(8,128)(2,1)S(1)}, f32[256,384]{1,0:T(8,128)S(1)}, bf16[112,768]{1,0:T(8,128)(2,1)S(1)}, bf16[112,768]{1,0:T(8,128)(2,1)S(1...) custom-call(s32[8]{0:T(128)S(1)} %copy-done.1, ...), custom_call_target="tpu_custom_call" | custom-call | flops 1 | bytes 1 | tf_op jit(solution)/shard_map/pallas_call | solution.py:505
  71.9 2.7 %collective-permute-start.16 = (bf16[4,4,152,128]{3,2,1,0:T(8,128)(2,1)S(1)}, bf16[4,4,152,128]{3,2,1,0:T(8,128)(2,1)S(1)}, u32[]{:S(2)}, u32[]{:S(2)}) collective-permute-start(bf16[4,4,152,128]{3,2,1,0:T(8,128)(2,1)S(1)} %get-tuple-element.123), channel_id=1, source_target_pairs={{0,1},{1,0},{2,3},{3,2},{4,5},{5,4},{6,7},{7,6},{8,9},{9,8},{10,11... | collective-permute-start | bytes 1867784 | tf_op jit(solution)/shard_map/ppermute | solution.py:63
  74.6 4.7 %collective-permute-done.18.refs_2_ = bf16[4,296,128]{2,1,0:T(8,128)(2,1)S(1)} collective-permute-done((bf16[4,296,128]{2,1,0:T(8,128)(2,1)S(1)}, bf16[4,296,128]{2,1,0:T(8,128)(2,1)S(1)}, u32[]{:S(2)}, u32[]{:S(2)}) %collective-permute-start.18) | collective-permute-done | bytes 303136 | tf_op jit(solution)/shard_map/ppermute | solution.py:63
  79.9 3.7 %collective-permute-start.21 = (bf16[4,152,128]{2,1,0:T(8,128)(2,1)S(1)}, bf16[4,152,128]{2,1,0:T(8,128)(2,1)S(1)}, u32[]{:S(2)}, u32[]{:S(2)}) collective-permute-start(bf16[4,152,128]{2,1,0:T(8,128)(2,1)S(1)} %get-tuple-element.133), channel_id=1, source_target_pairs={{0,2},{1,3},{2,0},{3,1},{4,6},{5,7},{6,4},{7,5},{8,10},{9,11},{10,... | collective-permute-start | bytes 466952 | tf_op jit(solution)/shard_map/ppermute | solution.py:63
  86.7 1.6 %collective-permute-done.21.refs_1_ = bf16[4,152,128]{2,1,0:T(8,128)(2,1)S(1)} collective-permute-done((bf16[4,152,128]{2,1,0:T(8,128)(2,1)S(1)}, bf16[4,152,128]{2,1,0:T(8,128)(2,1)S(1)}, u32[]{:S(2)}, u32[]{:S(2)}) %collective-permute-start.21) | collective-permute-done | bytes 155680 | tf_op jit(solution)/shard_map/ppermute | solution.py:63
  88.3 4.5 %collective-permute-done.22.refs_2_ = bf16[4,152,128]{2,1,0:T(8,128)(2,1)S(1)} collective-permute-done((bf16[4,152,128]{2,1,0:T(8,128)(2,1)S(1)}, bf16[4,152,128]{2,1,0:T(8,128)(2,1)S(1)}, u32[]{:S(2)}, u32[]{:S(2)}) %collective-permute-start.22) | collective-permute-done | bytes 155680 | tf_op jit(solution)/shard_map/ppermute | solution.py:63
  92.9 1.8 %collective-permute-start.25 = (bf16[2,152,128]{2,1,0:T(8,128)(2,1)S(1)}, bf16[2,152,128]{2,1,0:T(8,128)(2,1)S(1)}, u32[]{:S(2)}, u32[]{:S(2)}) collective-permute-start(bf16[2,152,128]{2,1,0:T(8,128)(2,1)S(1)} %get-tuple-element.143), channel_id=1, source_target_pairs={{0,16},{1,17},{2,18},{3,19},{4,20},{5,21},{6,22},{7,23},{8,24},{9,... | collective-permute-start | bytes 233480 | tf_op jit(solution)/shard_map/ppermute | solution.py:63
  95.3 3.7 %collective-permute-done.25.other_ref = bf16[2,152,128]{2,1,0:T(8,128)(2,1)S(1)} collective-permute-done((bf16[2,152,128]{2,1,0:T(8,128)(2,1)S(1)}, bf16[2,152,128]{2,1,0:T(8,128)(2,1)S(1)}, u32[]{:S(2)}, u32[]{:S(2)}) %collective-permute-start.25) | collective-permute-done | bytes 77856 | tf_op jit(solution)/shard_map/ppermute | solution.py:63
  100.7 2.4 %collective-permute-done.26 = bf16[1,152,128]{2,1,0:T(8,128)(2,1)S(1)} collective-permute-done((bf16[1,152,128]{2,1,0:T(8,128)(2,1)S(1)}, bf16[1,152,128]{2,1,0:T(8,128)(2,1)S(1)}, u32[]{:S(2)}, u32[]{:S(2)}) %collective-permute-start.26) | collective-permute-done | bytes 38944 | tf_op jit(solution)/shard_map/ppermute | solution.py:63
  (63 shorter events, 21.7 us)
Async XLA Ops:
  2.0 12.1 %collective-permute-start.3 = (bf16[1,296,128]{2,1,0:T(8,128)(2,1)S(1)}, bf16[1,296,128]{2,1,0:T(8,128)(2,1)S(1)}, u32[]{:S(2)}, u32[]{:S(2)}) collective-permute-start(bf16[1,296,128]{2,1,0:T(8,128)(2,1)S(1)} %pad_bitcast_fusion.near_ref), channel_id=1, source_target_pairs={{0,8},{1,9},{2,10},{3,11},{4,12},{5,13},{6,14},{7,15},{8,0},{9,1},... | collective-permute-start | bytes 227336 | tf_op jit(solution)/shard_map/ppermute | solution.py:63
  6.2 6.5 %collective-permute-start.2 = (bf16[152,128]{1,0:T(8,128)(2,1)S(1)}, bf16[152,128]{1,0:T(8,128)(2,1)S(1)}, u32[]{:S(2)}, u32[]{:S(2)}) collective-permute-start(bf16[152,128]{1,0:T(8,128)(2,1)S(1)} %pad.8.refs_0_), channel_id=1, source_target_pairs={{0,24},{1,25},{2,26},{3,27},{4,28},{5,29},{6,30},{7,31},{8,16},{9,... | collective-permute-start | bytes 116744 | tf_op jit(solution)/shard_map/ppermute | solution.py:63
  8.7 5.3 %collective-permute-start.1 = (bf16[152,128]{1,0:T(8,128)(2,1)S(1)}, bf16[152,128]{1,0:T(8,128)(2,1)S(1)}, u32[]{:S(2)}, u32[]{:S(2)}) collective-permute-start(bf16[152,128]{1,0:T(8,128)(2,1)S(1)} %pad.8.refs_0_), channel_id=1, source_target_pairs={{0,16},{1,17},{2,18},{3,19},{4,20},{5,21},{6,22},{7,23},{8,24},{9,... | collective-permute-start | bytes 116744 | tf_op jit(solution)/shard_map/ppermute | solution.py:63
  8.9 5.1 %collective-permute-start = (bf16[152,128]{1,0:T(8,128)(2,1)S(1)}, bf16[152,128]{1,0:T(8,128)(2,1)S(1)}, u32[]{:S(2)}, u32[]{:S(2)}) collective-permute-start(bf16[152,128]{1,0:T(8,128)(2,1)S(1)} %pad.8.refs_0_), channel_id=1, source_target_pairs={{0,8},{1,9},{2,10},{3,11},{4,12},{5,13},{6,14},{7,15},{8,0},{9,1},... | collective-permute-start | bytes 116744 | tf_op jit(solution)/shard_map/ppermute | solution.py:63
  14.1 6.6 %collective-permute-start.4 = (bf16[112,896]{1,0:T(8,128)(2,1)}, bf16[112,896]{1,0:T(8,128)(2,1)S(1)}, u32[]{:S(2)}, u32[]{:S(2)}) collective-permute-start(bf16[112,896]{1,0:T(8,128)(2,1)} %get-tuple-element.81), channel_id=1, source_target_pairs={{0,1},{1,0},{2,3},{3,2},{4,5},{5,4},{6,7},{7,6},{8,9},{9,8},{10,11... | collective-permute-start | bytes 602120 | tf_op jit(solution)/shard_map/ppermute | solution.py:63
  14.1 16.6 %collective-permute-start.9 = (bf16[112,896]{1,0:T(8,128)(2,1)}, bf16[112,896]{1,0:T(8,128)(2,1)S(1)}, u32[]{:S(2)}, u32[]{:S(2)}) collective-permute-start(bf16[112,896]{1,0:T(8,128)(2,1)} %get-tuple-element.85), channel_id=1, source_target_pairs={{1,2},{3,4},{5,6},{7,8},{9,10},{11,12},{13,14},{15,16},{17,18},{19... | collective-permute-start | bytes 602120 | tf_op jit(solution)/shard_map/ppermute | solution.py:604
  14.8 13.2 %collective-permute-start.8 = (bf16[4,152,128]{2,1,0:T(8,128)(2,1)S(1)}, bf16[4,152,128]{2,1,0:T(8,128)(2,1)S(1)}, u32[]{:S(2)}, u32[]{:S(2)}) collective-permute-start(bf16[4,152,128]{2,1,0:T(8,128)(2,1)S(1)} %shard_map.94.refs_0_), channel_id=1, source_target_pairs={{0,6},{1,7},{2,4},{3,5},{4,2},{5,3},{6,0},{7,1},{8,14},{9,15},{10,... | collective-permute-start | bytes 466952 | tf_op jit(solution)/shard_map/ppermute | solution.py:63
  19.2 9.5 %collective-permute-start.7 = (bf16[4,152,128]{2,1,0:T(8,128)(2,1)S(1)}, bf16[4,152,128]{2,1,0:T(8,128)(2,1)S(1)}, u32[]{:S(2)}, u32[]{:S(2)}) collective-permute-start(bf16[4,152,128]{2,1,0:T(8,128)(2,1)S(1)} %shard_map.94.refs_0_), channel_id=1, source_target_pairs={{0,4},{1,5},{2,6},{3,7},{4,0},{5,1},{6,2},{7,3},{8,12},{9,13},{10,... | collective-permute-start | bytes 466952 | tf_op jit(solution)/shard_map/ppermute | solution.py:63
  19.7 10.9 %collective-permute-start.6 = (bf16[4,152,128]{2,1,0:T(8,128)(2,1)S(1)}, bf16[4,152,128]{2,1,0:T(8,128)(2,1)S(1)}, u32[]{:S(2)}, u32[]{:S(2)}) collective-permute-start(bf16[4,152,128]{2,1,0:T(8,128)(2,1)S(1)} %shard_map.94.refs_0_), channel_id=1, source_target_pairs={{0,2},{1,3},{2,0},{3,1},{4,6},{5,7},{6,4},{7,5},{8,10},{9,11},{10,... | collective-permute-start | bytes 466952 | tf_op jit(solution)/shard_map/ppermute | solution.py:63
  20.6 10.0 %collective-permute-start.5 = (bf16[2,296,128]{2,1,0:T(8,128)(2,1)S(1)}, bf16[2,296,128]{2,1,0:T(8,128)(2,1)S(1)}, u32[]{:S(2)}, u32[]{:S(2)}) collective-permute-start(bf16[2,296,128]{2,1,0:T(8,128)(2,1)S(1)} %shard_map.95.near_ref), channel_id=1, source_target_pairs={{0,16},{1,17},{2,18},{3,19},{4,20},{5,21},{6,22},{7,23},{8,24},{9,... | collective-permute-start | bytes 454664 | tf_op jit(solution)/shard_map/ppermute | solution.py:63
  30.9 11.0 %collective-permute-start.12 = (bf16[4,296,128]{2,1,0:T(8,128)(2,1)S(1)}, bf16[4,296,128]{2,1,0:T(8,128)(2,1)S(1)}, u32[]{:S(2)}, u32[]{:S(2)}) collective-permute-start(bf16[4,296,128]{2,1,0:T(8,128)(2,1)S(1)} %shard_map.96.refs_0_), channel_id=1, source_target_pairs={{0,6},{1,7},{2,4},{3,5},{4,2},{5,3},{6,0},{7,1},{8,14},{9,15},{10,... | collective-permute-start | bytes 909320 | tf_op jit(solution)/shard_map/ppermute | solution.py:63
  32.9 14.8 %collective-permute-start.11 = (bf16[4,296,128]{2,1,0:T(8,128)(2,1)S(1)}, bf16[4,296,128]{2,1,0:T(8,128)(2,1)S(1)}, u32[]{:S(2)}, u32[]{:S(2)}) collective-permute-start(bf16[4,296,128]{2,1,0:T(8,128)(2,1)S(1)} %shard_map.96.refs_0_), channel_id=1, source_target_pairs={{0,4},{1,5},{2,6},{3,7},{4,0},{5,1},{6,2},{7,3},{8,12},{9,13},{10,... | collective-permute-start | bytes 909320 | tf_op jit(solution)/shard_map/ppermute | solution.py:63
  33.5 14.3 %collective-permute-start.10 = (bf16[4,296,128]{2,1,0:T(8,128)(2,1)S(1)}, bf16[4,296,128]{2,1,0:T(8,128)(2,1)S(1)}, u32[]{:S(2)}, u32[]{:S(2)}) collective-permute-start(bf16[4,296,128]{2,1,0:T(8,128)(2,1)S(1)} %shard_map.96.refs_0_), channel_id=1, source_target_pairs={{0,2},{1,3},{2,0},{3,1},{4,6},{5,7},{6,4},{7,5},{8,10},{9,11},{10,... | collective-permute-start | bytes 909320 | tf_op jit(solution)/shard_map/ppermute | solution.py:63
  62.3 12.3 %collective-permute-start.17 = (bf16[4,296,128]{2,1,0:T(8,128)(2,1)S(1)}, bf16[4,296,128]{2,1,0:T(8,128)(2,1)S(1)}, u32[]{:S(2)}, u32[]{:S(2)}) collective-permute-start(bf16[4,296,128]{2,1,0:T(8,128)(2,1)S(1)} %get-tuple-element.125), channel_id=1, source_target_pairs={{0,2},{1,3},{2,0},{3,1},{4,6},{5,7},{6,4},{7,5},{8,10},{9,11},{10,... | collective-permute-start | bytes 909320 | tf_op jit(solution)/shard_map/ppermute | solution.py:63
  63.6 15.7 %collective-permute-start.18 = (bf16[4,296,128]{2,1,0:T(8,128)(2,1)S(1)}, bf16[4,296,128]{2,1,0:T(8,128)(2,1)S(1)}, u32[]{:S(2)}, u32[]{:S(2)}) collective-permute-start(bf16[4,296,128]{2,1,0:T(8,128)(2,1)S(1)} %get-tuple-element.126), channel_id=1, source_target_pairs={{0,4},{1,5},{2,6},{3,7},{4,0},{5,1},{6,2},{7,3},{8,12},{9,13},{10,... | collective-permute-start | bytes 909320 | tf_op jit(solution)/shard_map/ppermute | solution.py:63
  64.7 14.8 %collective-permute-start.19 = (bf16[4,296,128]{2,1,0:T(8,128)(2,1)S(1)}, bf16[4,296,128]{2,1,0:T(8,128)(2,1)S(1)}, u32[]{:S(2)}, u32[]{:S(2)}) collective-permute-start(bf16[4,296,128]{2,1,0:T(8,128)(2,1)S(1)} %get-tuple-element.127), channel_id=1, source_target_pairs={{0,6},{1,7},{2,4},{3,5},{4,2},{5,3},{6,0},{7,1},{8,14},{9,15},{10,... | collective-permute-start | bytes 909320 | tf_op jit(solution)/shard_map/ppermute | solution.py:63
  71.2 8.5 %collective-permute-start.20 = (bf16[112,768]{1,0:T(8,128)(2,1)S(1)}, bf16[112,768]{1,0:T(8,128)(2,1)S(1)}, u32[]{:S(2)}, u32[]{:S(2)}) collective-permute-start(bf16[112,768]{1,0:T(8,128)(2,1)S(1)} %get-tuple-element.130), channel_id=1, source_target_pairs={{1,2},{3,4},{5,6},{7,8},{9,10},{11,12},{13,14},{15,16},{17,18},{19... | collective-permute-start | bytes 516104 | tf_op jit(solution)/shard_map/ppermute | solution.py:692
  71.9 7.8 %collective-permute-start.16 = (bf16[4,4,152,128]{3,2,1,0:T(8,128)(2,1)S(1)}, bf16[4,4,152,128]{3,2,1,0:T(8,128)(2,1)S(1)}, u32[]{:S(2)}, u32[]{:S(2)}) collective-permute-start(bf16[4,4,152,128]{3,2,1,0:T(8,128)(2,1)S(1)} %get-tuple-element.123), channel_id=1, source_target_pairs={{0,1},{1,0},{2,3},{3,2},{4,5},{5,4},{6,7},{7,6},{8,9},{9,8},{10,11... | collective-permute-start | bytes 1867784 | tf_op jit(solution)/shard_map/ppermute | solution.py:63
  79.9 8.5 %collective-permute-start.21 = (bf16[4,152,128]{2,1,0:T(8,128)(2,1)S(1)}, bf16[4,152,128]{2,1,0:T(8,128)(2,1)S(1)}, u32[]{:S(2)}, u32[]{:S(2)}) collective-permute-start(bf16[4,152,128]{2,1,0:T(8,128)(2,1)S(1)} %get-tuple-element.133), channel_id=1, source_target_pairs={{0,2},{1,3},{2,0},{3,1},{4,6},{5,7},{6,4},{7,5},{8,10},{9,11},{10,... | collective-permute-start | bytes 466952 | tf_op jit(solution)/shard_map/ppermute | solution.py:63
  83.5 9.3 %collective-permute-start.22 = (bf16[4,152,128]{2,1,0:T(8,128)(2,1)S(1)}, bf16[4,152,128]{2,1,0:T(8,128)(2,1)S(1)}, u32[]{:S(2)}, u32[]{:S(2)}) collective-permute-start(bf16[4,152,128]{2,1,0:T(8,128)(2,1)S(1)} %get-tuple-element.134), channel_id=1, source_target_pairs={{0,4},{1,5},{2,6},{3,7},{4,0},{5,1},{6,2},{7,3},{8,12},{9,13},{10,... | collective-permute-start | bytes 466952 | tf_op jit(solution)/shard_map/ppermute | solution.py:63
  84.0 8.8 %collective-permute-start.23 = (bf16[4,152,128]{2,1,0:T(8,128)(2,1)S(1)}, bf16[4,152,128]{2,1,0:T(8,128)(2,1)S(1)}, u32[]{:S(2)}, u32[]{:S(2)}) collective-permute-start(bf16[4,152,128]{2,1,0:T(8,128)(2,1)S(1)} %get-tuple-element.135), channel_id=1, source_target_pairs={{0,6},{1,7},{2,4},{3,5},{4,2},{5,3},{6,0},{7,1},{8,14},{9,15},{10,... | collective-permute-start | bytes 466952 | tf_op jit(solution)/shard_map/ppermute | solution.py:63
  85.1 9.7 %collective-permute-start.27 = (bf16[2,296,128]{2,1,0:T(8,128)(2,1)S(1)}, bf16[2,296,128]{2,1,0:T(8,128)(2,1)S(1)}, u32[]{:S(2)}, u32[]{:S(2)}) collective-permute-start(bf16[2,296,128]{2,1,0:T(8,128)(2,1)S(1)} %get-tuple-element.147), channel_id=1, source_target_pairs={{0,16},{1,17},{2,18},{3,19},{4,20},{5,21},{6,22},{7,23},{8,24},{9,... | collective-permute-start | bytes 454664 | tf_op jit(solution)/shard_map/ppermute | solution.py:63
  92.9 6.1 %collective-permute-start.25 = (bf16[2,152,128]{2,1,0:T(8,128)(2,1)S(1)}, bf16[2,152,128]{2,1,0:T(8,128)(2,1)S(1)}, u32[]{:S(2)}, u32[]{:S(2)}) collective-permute-start(bf16[2,152,128]{2,1,0:T(8,128)(2,1)S(1)} %get-tuple-element.143), channel_id=1, source_target_pairs={{0,16},{1,17},{2,18},{3,19},{4,20},{5,21},{6,22},{7,23},{8,24},{9,... | collective-permute-start | bytes 233480 | tf_op jit(solution)/shard_map/ppermute | solution.py:63
  95.2 8.5 %collective-permute-start.24 = (bf16[112,768]{1,0:T(8,128)(2,1)S(1)}, bf16[112,768]{1,0:T(8,128)(2,1)S(1)}, u32[]{:S(2)}, u32[]{:S(2)}) collective-permute-start(bf16[112,768]{1,0:T(8,128)(2,1)S(1)} %get-tuple-element.138), channel_id=1, source_target_pairs={{0,1},{1,0},{2,3},{3,2},{4,5},{5,4},{6,7},{7,6},{8,9},{9,8},{10,11... | collective-permute-start | bytes 516104 | tf_op jit(solution)/shard_map/ppermute | solution.py:63
  (7 other events, 62.9 us)

commit v7 on v6

--- a/solution.py
+++ b/solution.py
@@ -517,25 +517,23 @@
     return jax.ShapeDtypeStruct(shape, kind)
 
 
-def pack(parts):
+def pack(parts, flops=1):
     packed = struct((len(parts),) + parts[0].shape, bf16)
-    return call_kernel(pack_kernel, [packed], [], 1, parts)[0]
+    return call_kernel(pack_kernel, [packed], [], flops, parts)[0]
 
 
 def gather_columns(rows, devices):
     depth = devices // (CORES * SQUARE)
-    return pack([rows] + pass_layers([rows] * depth, devices))
-
-
-def double_column(column, devices):
-    half = column.shape[0]
-    far = pass_on(column, half * CORES * SQUARE, devices)
-    joined = struct((2 * half,) + column.shape[1:], bf16)
-    return call_kernel(join_kernel, [joined], [], 1, [column, far])[0]
-
-
-def gather_planes(column, devices):
-    return pack([column] + pass_chips([column] * SQUARE, devices))
+    return pack([rows] + pass_layers([rows] * depth, devices), 10**10)
+
+
+def pass_column(column, devices):
+    return pass_on(column, column.shape[0] * CORES * SQUARE, devices)
+
+
+def join(near, far):
+    joined = struct((2 * near.shape[0],) + near.shape[1:], bf16)
+    return call_kernel(join_kernel, [joined], [], 1, [near, far])[0]
 
 
 def add_cores(keep, other):
@@ -598,14 +596,18 @@
     attn_rows = as_rows(attn_blocks)
     mlp_rows = as_rows(mlp_blocks)
     attn_column = gather_columns(attn_rows, devices)
-    mlp_column = double_column(mlp_rows[None], devices)
+    mlp_column = join(mlp_rows[None], pass_column(mlp_rows[None], devices))
     attn_column, mlp_column, inner, outer = barrier((attn_column, mlp_column, inner, outer))
     inner = pass_cores(inner, devices)
+    inner, outer = barrier((inner, outer))
     outer = lax.ppermute(outer, "fsdp", outside)
-    mlp_column, inner = barrier((mlp_column, inner))
-    while mlp_column.shape[0] < depth:
-        mlp_column = double_column(mlp_column, devices)
-    attn_mine = gather_planes(attn_column, devices)
+    while 2 * mlp_column.shape[0] < depth:
+        mlp_column = join(mlp_column, pass_column(mlp_column, devices))
+    mlp_far = pass_column(mlp_column, devices)
+    attn_passed = pass_chips([attn_column] * SQUARE, devices)
+    attn_mine = pack([attn_column] + attn_passed, 10**10)
+    attn_mine, outer, mlp_far = barrier((attn_mine, outer, mlp_far))
+    mlp_column = join(mlp_column, mlp_far)
     mlp_column, attn_mine, inner, outer = barrier((mlp_column, attn_mine, inner, outer))
     mlp_passed = pass_chips([mlp_column] * SQUARE, devices)
     attn_other = pass_cores(attn_mine, devices)

time: 105 us -> 104 us (level)
  waiting for transfers between devices: 37.5 us -> 35.1 us
  starting transfers between devices: 37.8 us -> 39.2 us
    ppermute x27, waiting for transfers between devices: 37.5 us -> 35.1 us  [pass_on(): return lax.ppermute(value, 'fsdp', [(i, i ^ step) for i in range(devices)])]
    ppermute x27, starting transfers between devices: 36.5 us -> 37.8 us  [pass_on(): return lax.ppermute(value, 'fsdp', [(i, i ^ step) for i in range(devices)])]
  transfers between devices with their start and end apart: 29 -> 29, of which waited for: 14 -> 15; matrix products, arithmetic and copies ran while one was open for 3% -> 3% of each run, Pallas kernels for 15% -> 15%
where the time goes in v7:
time: 104 us
  starting transfers between devices  39.2 us (38%)
  waiting for transfers between devices  35.1 us (34%)
  Pallas kernels  25 us (24%)
  other arithmetic  2.44 us (2%)
  local copies, waits for them, and re-layouts  1.56 us (2%)
    ppermute x27, starting transfers between devices, pass_on(): return lax.ppermute(value, 'fsdp', [(i, i ^ step) for i in range(devices)])  37.8 us
    ppermute x27, waiting for transfers between devices, pass_on(): return lax.ppermute(value, 'fsdp', [(i, i ^ step) for i in range(devices)])  35.1 us
    pallas_call x17, Pallas kernels, call_kernel(): pl.pallas_call(kernel, out_shape=out_shapes, in_specs=specs, out_specs=[s...  25 us
    unnamed x4, other arithmetic  2.44 us
  transfers between devices with their start and end apart: 29, of which 15 were waited for; matrix products, arithmetic and copies ran while one was open for 3% of the time, Pallas kernels for 15%

profile of v7, /device:TPU:0, one launch (start us, length us, event | category | flops | bytes accessed | tf_op | source)
XLA Modules:
  0.0 104.2 jit_solution(11222796918026776740)
XLA Ops:
  1.7 5.1 %collective-permute-start.2 = (bf16[152,128]{1,0:T(8,128)(2,1)S(1)}, bf16[152,128]{1,0:T(8,128)(2,1)S(1)}, u32[]{:S(2)}, u32[]{:S(2)}) collective-permute-start(bf16[152,128]{1,0:T(8,128)(2,1)S(1)} %pad.8.refs_0_), channel_id=1, source_target_pairs={{0,24},{1,25},{2,26},{3,27},{4,28},{5,29},{6,30},{7,31},{8,16},{9,... | collective-permute-start | bytes 116744 | tf_op jit(solution)/shard_map/ppermute | solution.py:63
  8.8 1.5 %collective-permute-start.3 = (bf16[1,296,128]{2,1,0:T(8,128)(2,1)S(1)}, bf16[1,296,128]{2,1,0:T(8,128)(2,1)S(1)}, u32[]{:S(2)}, u32[]{:S(2)}) collective-permute-start(bf16[1,296,128]{2,1,0:T(8,128)(2,1)S(1)} %pad_bitcast_fusion.near_ref), channel_id=1, source_target_pairs={{0,8},{1,9},{2,10},{3,11},{4,12},{5,13},{6,14},{7,15},{8,0},{9,1},... | collective-permute-start | bytes 227336 | tf_op jit(solution)/shard_map/ppermute | solution.py:63
  10.3 2.0 %shard_map.93 = (bf16[256,896]{1,0:T(8,128)(2,1)}, bf16[112,896]{1,0:T(8,128)(2,1)}, bf16[112,896]{1,0:T(8,128)(2,1)}, s32[8]{0:T(128)}) custom-call(s32[1]{0:T(128)} %bitcast.device_ref, s32[2,128]{1,0:T(2,128)} %bitcast.21, s32[2,128]{1,0:T(2,128)} %bitcast.22, bf16[256,384]{1,0:T(8,128)(2,1)} %inputs_hbm.1, bf16[256,384]{1,0:T(8,128)(2,1)} %out_grad_hbm.1), custom_call_target="tpu_custom_call" | custom-call | flops 1 | bytes 1 | tf_op jit(solution)/shard_map/pallas_call | solution.py:505
  13.4 2.7 %collective-permute-start.6 = (bf16[4,152,128]{2,1,0:T(8,128)(2,1)S(1)}, bf16[4,152,128]{2,1,0:T(8,128)(2,1)S(1)}, u32[]{:S(2)}, u32[]{:S(2)}) collective-permute-start(bf16[4,152,128]{2,1,0:T(8,128)(2,1)S(1)} %shard_map.94.refs_0_), channel_id=1, source_target_pairs={{0,6},{1,7},{2,4},{3,5},{4,2},{5,3},{6,0},{7,1},{8,14},{9,15},{10,... | collective-permute-start | bytes 466952 | tf_op jit(solution)/shard_map/ppermute | solution.py:63
  17.0 2.7 %collective-permute-start.9 = (bf16[2,296,128]{2,1,0:T(8,128)(2,1)S(1)}, bf16[2,296,128]{2,1,0:T(8,128)(2,1)S(1)}, u32[]{:S(2)}, u32[]{:S(2)}) collective-permute-start(bf16[2,296,128]{2,1,0:T(8,128)(2,1)S(1)} %shard_map.95.near_ref), channel_id=1, source_target_pairs={{0,16},{1,17},{2,18},{3,19},{4,20},{5,21},{6,22},{7,23},{8,24},{9,... | collective-permute-start | bytes 454664 | tf_op jit(solution)/shard_map/ppermute | solution.py:63
  21.2 2.9 %collective-permute-done.5.refs_2_ = bf16[4,152,128]{2,1,0:T(8,128)(2,1)S(1)} collective-permute-done((bf16[4,152,128]{2,1,0:T(8,128)(2,1)S(1)}, bf16[4,152,128]{2,1,0:T(8,128)(2,1)S(1)}, u32[]{:S(2)}, u32[]{:S(2)}) %collective-permute-start.5) | collective-permute-done | bytes 155680 | tf_op jit(solution)/shard_map/ppermute | solution.py:63
  24.4 2.4 %collective-permute-done.9.far_ref = bf16[2,296,128]{2,1,0:T(8,128)(2,1)S(1)} collective-permute-done((bf16[2,296,128]{2,1,0:T(8,128)(2,1)S(1)}, bf16[2,296,128]{2,1,0:T(8,128)(2,1)S(1)}, u32[]{:S(2)}, u32[]{:S(2)}) %collective-permute-start.9) | collective-permute-done | bytes 151584 | tf_op jit(solution)/shard_map/ppermute | solution.py:63
  27.9 3.2 %collective-permute-start.12 = (bf16[4,296,128]{2,1,0:T(8,128)(2,1)S(1)}, bf16[4,296,128]{2,1,0:T(8,128)(2,1)S(1)}, u32[]{:S(2)}, u32[]{:S(2)}) collective-permute-start(bf16[4,296,128]{2,1,0:T(8,128)(2,1)S(1)} %shard_map.97.refs_0_), channel_id=1, source_target_pairs={{0,6},{1,7},{2,4},{3,5},{4,2},{5,3},{6,0},{7,1},{8,14},{9,15},{10,... | collective-permute-start | bytes 909320 | tf_op jit(solution)/shard_map/ppermute | solution.py:63
  32.0 4.3 %shard_map.98 = (f32[416,384]{1,0:T(8,128)S(1)}, bf16[416,384]{1,0:T(8,128)(2,1)S(1)}, bf16[416,384]{1,0:T(8,128)(2,1)S(1)}, bf16[416,384]{1,0:T(8,128)(2,1)S(1)...) custom-call(s32[8]{0:T(128)S(1)} %copy-done.1, ...), custom_call_target="tpu_custom_call" | custom-call | flops 1 | bytes 1 | tf_op jit(solution)/shard_map/pallas_call | solution.py:505
  36.4 2.8 %collective-permute-done.12.refs_3_ = bf16[4,296,128]{2,1,0:T(8,128)(2,1)S(1)} collective-permute-done((bf16[4,296,128]{2,1,0:T(8,128)(2,1)S(1)}, bf16[4,296,128]{2,1,0:T(8,128)(2,1)S(1)}, u32[]{:S(2)}, u32[]{:S(2)}) %collective-permute-start.12) | collective-permute-done | bytes 303136 | tf_op jit(solution)/shard_map/ppermute | solution.py:63
  39.1 6.1 %collective-permute-done.11.refs_2_ = bf16[4,296,128]{2,1,0:T(8,128)(2,1)S(1)} collective-permute-done((bf16[4,296,128]{2,1,0:T(8,128)(2,1)S(1)}, bf16[4,296,128]{2,1,0:T(8,128)(2,1)S(1)}, u32[]{:S(2)}, u32[]{:S(2)}) %collective-permute-start.11) | collective-permute-done | bytes 303136 | tf_op jit(solution)/shard_map/ppermute | solution.py:63
  46.2 2.9 %collective-permute-done.14.other_ref = bf16[4,4,296,128]{3,2,1,0:T(8,128)(2,1)S(1)} collective-permute-done((bf16[4,4,296,128]{3,2,1,0:T(8,128)(2,1)S(1)}, bf16[4,4,296,128]{3,2,1,0:T(8,128)(2,1)S(1)}, u32[]{:S(2)}, u32[]{:S(2)}) %collective-permute-start.14) | collective-permute-done | bytes 1212448 | tf_op jit(solution)/shard_map/ppermute | solution.py:63
  49.1 7.5 %shard_map.100 = (bf16[480,384]{1,0:T(8,128)(2,1)S(1)}, f32[416,384]{1,0:T(8,128)S(1)}, bf16[4,4,296,128]{3,2,1,0:T(8,128)(2,1)S(1)}, bf16[4,4,296,128]{3,2,1,0:T(8,128)(2,1)S(1)}) custom-call(s32[8]{0:T(128)S(1)} %copy-done.1, f32[416,384]{1,0:T(8,128)S(1)} %get-tuple-element.98.middle_ref, bf16[416,384]{1,0:T(8,128)(2,1)S(1)} %get-tuple-element.99.cotangent_ref, ...), custom_call_target="tpu_custom_call" | custom-call | flops 1 | bytes 1 | tf_op jit(solution)/shard_map/pallas_call | solution.py:505
  56.8 3.5 %shard_map.102 = (bf16[208,1152]{1,0:T(8,128)(2,1)S(1)}, f32[384,384]{1,0:T(8,128)S(1)}, f32[1,384]{1,0:T(1,128)S(1)}, f32[8,128]{1,0:T(8,128)S(1)}, bf16[416,384]{1,0:T(8,128)(2,1)S(1)}) custom-call(s32[8]{0:T(128)S(1)} %copy-done.1, f32[416,384]{1,0:T(8,128)S(1)} %get-tuple-element.103.grad_middle_ref, bf16[416,1152]{1,0:T(8,128)(2,1)S(1)} %get-tuple-element.107.qkv_ref, ...), custom_call_target="tpu_custom_call" | custom-call | flops 1 | bytes 1 | tf_op jit(solution)/shard_map/pallas_call | solution.py:505
  62.7 1.5 %collective-permute-start.19 = (bf16[4,296,128]{2,1,0:T(8,128)(2,1)S(1)}, bf16[4,296,128]{2,1,0:T(8,128)(2,1)S(1)}, u32[]{:S(2)}, u32[]{:S(2)}) collective-permute-start(bf16[4,296,128]{2,1,0:T(8,128)(2,1)S(1)} %get-tuple-element.133), channel_id=1, source_target_pairs={{0,6},{1,7},{2,4},{3,5},{4,2},{5,3},{6,0},{7,1},{8,14},{9,15},{10,... | collective-permute-start | bytes 909320 | tf_op jit(solution)/shard_map/ppermute | solution.py:63
  64.2 5.4 %shard_map.103 = (bf16[256,384]{1,0:T(8,128)(2,1)S(1)}, f32[256,384]{1,0:T(8,128)S(1)}, bf16[112,768]{1,0:T(8,128)(2,1)S(1)}, bf16[112,768]{1,0:T(8,128)(2,1)S(1...) custom-call(s32[8]{0:T(128)S(1)} %copy-done.1, ...), custom_call_target="tpu_custom_call" | custom-call | flops 1 | bytes 1 | tf_op jit(solution)/shard_map/pallas_call | solution.py:505
  70.2 2.4 %collective-permute-start.16 = (bf16[4,4,152,128]{3,2,1,0:T(8,128)(2,1)S(1)}, bf16[4,4,152,128]{3,2,1,0:T(8,128)(2,1)S(1)}, u32[]{:S(2)}, u32[]{:S(2)}) collective-permute-start(bf16[4,4,152,128]{3,2,1,0:T(8,128)(2,1)S(1)} %get-tuple-element.129), channel_id=1, source_target_pairs={{0,1},{1,0},{2,3},{3,2},{4,5},{5,4},{6,7},{7,6},{8,9},{9,8},{10,11... | collective-permute-start | bytes 1867784 | tf_op jit(solution)/shard_map/ppermute | solution.py:63
  72.6 4.7 %collective-permute-done.18.refs_2_ = bf16[4,296,128]{2,1,0:T(8,128)(2,1)S(1)} collective-permute-done((bf16[4,296,128]{2,1,0:T(8,128)(2,1)S(1)}, bf16[4,296,128]{2,1,0:T(8,128)(2,1)S(1)}, u32[]{:S(2)}, u32[]{:S(2)}) %collective-permute-start.18) | collective-permute-done | bytes 303136 | tf_op jit(solution)/shard_map/ppermute | solution.py:63
  77.9 3.7 %collective-permute-start.21 = (bf16[4,152,128]{2,1,0:T(8,128)(2,1)S(1)}, bf16[4,152,128]{2,1,0:T(8,128)(2,1)S(1)}, u32[]{:S(2)}, u32[]{:S(2)}) collective-permute-start(bf16[4,152,128]{2,1,0:T(8,128)(2,1)S(1)} %get-tuple-element.139), channel_id=1, source_target_pairs={{0,2},{1,3},{2,0},{3,1},{4,6},{5,7},{6,4},{7,5},{8,10},{9,11},{10,... | collective-permute-start | bytes 466952 | tf_op jit(solution)/shard_map/ppermute | solution.py:63
  83.1 3.8 %collective-permute-start.27 = (bf16[2,296,128]{2,1,0:T(8,128)(2,1)S(1)}, bf16[2,296,128]{2,1,0:T(8,128)(2,1)S(1)}, u32[]{:S(2)}, u32[]{:S(2)}) collective-permute-start(bf16[2,296,128]{2,1,0:T(8,128)(2,1)S(1)} %get-tuple-element.153), channel_id=1, source_target_pairs={{0,16},{1,17},{2,18},{3,19},{4,20},{5,21},{6,22},{7,23},{8,24},{9,... | collective-permute-start | bytes 454664 | tf_op jit(solution)/shard_map/ppermute | solution.py:63
  86.9 3.9 %collective-permute-done.22.refs_2_ = bf16[4,152,128]{2,1,0:T(8,128)(2,1)S(1)} collective-permute-done((bf16[4,152,128]{2,1,0:T(8,128)(2,1)S(1)}, bf16[4,152,128]{2,1,0:T(8,128)(2,1)S(1)}, u32[]{:S(2)}, u32[]{:S(2)}) %collective-permute-start.22) | collective-permute-done | bytes 155680 | tf_op jit(solution)/shard_map/ppermute | solution.py:63
  90.9 3.4 %collective-permute-start.25 = (bf16[2,152,128]{2,1,0:T(8,128)(2,1)S(1)}, bf16[2,152,128]{2,1,0:T(8,128)(2,1)S(1)}, u32[]{:S(2)}, u32[]{:S(2)}) collective-permute-start(bf16[2,152,128]{2,1,0:T(8,128)(2,1)S(1)} %get-tuple-element.149), channel_id=1, source_target_pairs={{0,16},{1,17},{2,18},{3,19},{4,20},{5,21},{6,22},{7,23},{8,24},{9,... | collective-permute-start | bytes 233480 | tf_op jit(solution)/shard_map/ppermute | solution.py:63
  94.5 3.5 %collective-permute-done.25.other_ref = bf16[2,152,128]{2,1,0:T(8,128)(2,1)S(1)} collective-permute-done((bf16[2,152,128]{2,1,0:T(8,128)(2,1)S(1)}, bf16[2,152,128]{2,1,0:T(8,128)(2,1)S(1)}, u32[]{:S(2)}, u32[]{:S(2)}) %collective-permute-start.25) | collective-permute-done | bytes 77856 | tf_op jit(solution)/shard_map/ppermute | solution.py:63
  99.7 2.4 %collective-permute-done.26 = bf16[1,152,128]{2,1,0:T(8,128)(2,1)S(1)} collective-permute-done((bf16[1,152,128]{2,1,0:T(8,128)(2,1)S(1)}, bf16[1,152,128]{2,1,0:T(8,128)(2,1)S(1)}, u32[]{:S(2)}, u32[]{:S(2)}) %collective-permute-start.26) | collective-permute-done | bytes 38944 | tf_op jit(solution)/shard_map/ppermute | solution.py:63
  (67 shorter events, 19.1 us)
Async XLA Ops:
  1.7 10.6 %collective-permute-start.2 = (bf16[152,128]{1,0:T(8,128)(2,1)S(1)}, bf16[152,128]{1,0:T(8,128)(2,1)S(1)}, u32[]{:S(2)}, u32[]{:S(2)}) collective-permute-start(bf16[152,128]{1,0:T(8,128)(2,1)S(1)} %pad.8.refs_0_), channel_id=1, source_target_pairs={{0,24},{1,25},{2,26},{3,27},{4,28},{5,29},{6,30},{7,31},{8,16},{9,... | collective-permute-start | bytes 116744 | tf_op jit(solution)/shard_map/ppermute | solution.py:63
  6.9 5.5 %collective-permute-start.1 = (bf16[152,128]{1,0:T(8,128)(2,1)S(1)}, bf16[152,128]{1,0:T(8,128)(2,1)S(1)}, u32[]{:S(2)}, u32[]{:S(2)}) collective-permute-start(bf16[152,128]{1,0:T(8,128)(2,1)S(1)} %pad.8.refs_0_), channel_id=1, source_target_pairs={{0,16},{1,17},{2,18},{3,19},{4,20},{5,21},{6,22},{7,23},{8,24},{9,... | collective-permute-start | bytes 116744 | tf_op jit(solution)/shard_map/ppermute | solution.py:63
  6.9 5.5 %collective-permute-start = (bf16[152,128]{1,0:T(8,128)(2,1)S(1)}, bf16[152,128]{1,0:T(8,128)(2,1)S(1)}, u32[]{:S(2)}, u32[]{:S(2)}) collective-permute-start(bf16[152,128]{1,0:T(8,128)(2,1)S(1)} %pad.8.refs_0_), channel_id=1, source_target_pairs={{0,8},{1,9},{2,10},{3,11},{4,12},{5,13},{6,14},{7,15},{8,0},{9,1},... | collective-permute-start | bytes 116744 | tf_op jit(solution)/shard_map/ppermute | solution.py:63
  13.3 6.3 %collective-permute-start.7 = (bf16[112,896]{1,0:T(8,128)(2,1)S(1)}, bf16[112,896]{1,0:T(8,128)(2,1)S(1)}, u32[]{:S(2)}, u32[]{:S(2)}) collective-permute-start(bf16[112,896]{1,0:T(8,128)(2,1)S(1)} %copy-done.3), channel_id=1, source_target_pairs={{0,1},{1,0},{2,3},{3,2},{4,5},{5,4},{6,7},{7,6},{8,9},{9,8},{10,11... | collective-permute-start | bytes 602120 | tf_op jit(solution)/shard_map/ppermute | solution.py:63
  13.4 7.8 %collective-permute-start.6 = (bf16[4,152,128]{2,1,0:T(8,128)(2,1)S(1)}, bf16[4,152,128]{2,1,0:T(8,128)(2,1)S(1)}, u32[]{:S(2)}, u32[]{:S(2)}) collective-permute-start(bf16[4,152,128]{2,1,0:T(8,128)(2,1)S(1)} %shard_map.94.refs_0_), channel_id=1, source_target_pairs={{0,6},{1,7},{2,4},{3,5},{4,2},{5,3},{6,0},{7,1},{8,14},{9,15},{10,... | collective-permute-start | bytes 466952 | tf_op jit(solution)/shard_map/ppermute | solution.py:63
  16.1 8.0 %collective-permute-start.5 = (bf16[4,152,128]{2,1,0:T(8,128)(2,1)S(1)}, bf16[4,152,128]{2,1,0:T(8,128)(2,1)S(1)}, u32[]{:S(2)}, u32[]{:S(2)}) collective-permute-start(bf16[4,152,128]{2,1,0:T(8,128)(2,1)S(1)} %shard_map.94.refs_0_), channel_id=1, source_target_pairs={{0,4},{1,5},{2,6},{3,7},{4,0},{5,1},{6,2},{7,3},{8,12},{9,13},{10,... | collective-permute-start | bytes 466952 | tf_op jit(solution)/shard_map/ppermute | solution.py:63
  16.6 7.8 %collective-permute-start.4 = (bf16[4,152,128]{2,1,0:T(8,128)(2,1)S(1)}, bf16[4,152,128]{2,1,0:T(8,128)(2,1)S(1)}, u32[]{:S(2)}, u32[]{:S(2)}) collective-permute-start(bf16[4,152,128]{2,1,0:T(8,128)(2,1)S(1)} %shard_map.94.refs_0_), channel_id=1, source_target_pairs={{0,2},{1,3},{2,0},{3,1},{4,6},{5,7},{6,4},{7,5},{8,10},{9,11},{10,... | collective-permute-start | bytes 466952 | tf_op jit(solution)/shard_map/ppermute | solution.py:63
  17.0 9.8 %collective-permute-start.9 = (bf16[2,296,128]{2,1,0:T(8,128)(2,1)S(1)}, bf16[2,296,128]{2,1,0:T(8,128)(2,1)S(1)}, u32[]{:S(2)}, u32[]{:S(2)}) collective-permute-start(bf16[2,296,128]{2,1,0:T(8,128)(2,1)S(1)} %shard_map.95.near_ref), channel_id=1, source_target_pairs={{0,16},{1,17},{2,18},{3,19},{4,20},{5,21},{6,22},{7,23},{8,24},{9,... | collective-permute-start | bytes 454664 | tf_op jit(solution)/shard_map/ppermute | solution.py:63
  19.7 7.1 %collective-permute-start.8 = (bf16[112,896]{1,0:T(8,128)(2,1)S(1)}, bf16[112,896]{1,0:T(8,128)(2,1)S(1)}, u32[]{:S(2)}, u32[]{:S(2)}) collective-permute-start(bf16[112,896]{1,0:T(8,128)(2,1)S(1)} %copy-done.2), channel_id=1, source_target_pairs={{1,2},{3,4},{5,6},{7,8},{9,10},{11,12},{13,14},{15,16},{17,18},{19... | collective-permute-start | bytes 602120 | tf_op jit(solution)/shard_map/ppermute | solution.py:603
  26.8 5.2 %collective-permute-start.13 = (bf16[4,4,152,128]{3,2,1,0:T(8,128)(2,1)S(1)}, bf16[4,4,152,128]{3,2,1,0:T(8,128)(2,1)S(1)}, u32[]{:S(2)}, u32[]{:S(2)}) collective-permute-start(bf16[4,4,152,128]{3,2,1,0:T(8,128)(2,1)S(1)} %shard_map.96.mine_ref), channel_id=1, source_target_pairs={{0,1},{1,0},{2,3},{3,2},{4,5},{5,4},{6,7},{7,6},{8,9},{9,8},{10,11... | collective-permute-start | bytes 1867784 | tf_op jit(solution)/shard_map/ppermute | solution.py:63
  27.9 11.2 %collective-permute-start.12 = (bf16[4,296,128]{2,1,0:T(8,128)(2,1)S(1)}, bf16[4,296,128]{2,1,0:T(8,128)(2,1)S(1)}, u32[]{:S(2)}, u32[]{:S(2)}) collective-permute-start(bf16[4,296,128]{2,1,0:T(8,128)(2,1)S(1)} %shard_map.97.refs_0_), channel_id=1, source_target_pairs={{0,6},{1,7},{2,4},{3,5},{4,2},{5,3},{6,0},{7,1},{8,14},{9,15},{10,... | collective-permute-start | bytes 909320 | tf_op jit(solution)/shard_map/ppermute | solution.py:63
  31.1 14.1 %collective-permute-start.11 = (bf16[4,296,128]{2,1,0:T(8,128)(2,1)S(1)}, bf16[4,296,128]{2,1,0:T(8,128)(2,1)S(1)}, u32[]{:S(2)}, u32[]{:S(2)}) collective-permute-start(bf16[4,296,128]{2,1,0:T(8,128)(2,1)S(1)} %shard_map.97.refs_0_), channel_id=1, source_target_pairs={{0,4},{1,5},{2,6},{3,7},{4,0},{5,1},{6,2},{7,3},{8,12},{9,13},{10,... | collective-permute-start | bytes 909320 | tf_op jit(solution)/shard_map/ppermute | solution.py:63
  31.8 14.3 %collective-permute-start.10 = (bf16[4,296,128]{2,1,0:T(8,128)(2,1)S(1)}, bf16[4,296,128]{2,1,0:T(8,128)(2,1)S(1)}, u32[]{:S(2)}, u32[]{:S(2)}) collective-permute-start(bf16[4,296,128]{2,1,0:T(8,128)(2,1)S(1)} %shard_map.97.refs_0_), channel_id=1, source_target_pairs={{0,2},{1,3},{2,0},{3,1},{4,6},{5,7},{6,4},{7,5},{8,10},{9,11},{10,... | collective-permute-start | bytes 909320 | tf_op jit(solution)/shard_map/ppermute | solution.py:63
  60.6 12.0 %collective-permute-start.17 = (bf16[4,296,128]{2,1,0:T(8,128)(2,1)S(1)}, bf16[4,296,128]{2,1,0:T(8,128)(2,1)S(1)}, u32[]{:S(2)}, u32[]{:S(2)}) collective-permute-start(bf16[4,296,128]{2,1,0:T(8,128)(2,1)S(1)} %get-tuple-element.131), channel_id=1, source_target_pairs={{0,2},{1,3},{2,0},{3,1},{4,6},{5,7},{6,4},{7,5},{8,10},{9,11},{10,... | collective-permute-start | bytes 909320 | tf_op jit(solution)/shard_map/ppermute | solution.py:63
  61.7 15.7 %collective-permute-start.18 = (bf16[4,296,128]{2,1,0:T(8,128)(2,1)S(1)}, bf16[4,296,128]{2,1,0:T(8,128)(2,1)S(1)}, u32[]{:S(2)}, u32[]{:S(2)}) collective-permute-start(bf16[4,296,128]{2,1,0:T(8,128)(2,1)S(1)} %get-tuple-element.132), channel_id=1, source_target_pairs={{0,4},{1,5},{2,6},{3,7},{4,0},{5,1},{6,2},{7,3},{8,12},{9,13},{10,... | collective-permute-start | bytes 909320 | tf_op jit(solution)/shard_map/ppermute | solution.py:63
  62.7 14.9 %collective-permute-start.19 = (bf16[4,296,128]{2,1,0:T(8,128)(2,1)S(1)}, bf16[4,296,128]{2,1,0:T(8,128)(2,1)S(1)}, u32[]{:S(2)}, u32[]{:S(2)}) collective-permute-start(bf16[4,296,128]{2,1,0:T(8,128)(2,1)S(1)} %get-tuple-element.133), channel_id=1, source_target_pairs={{0,6},{1,7},{2,4},{3,5},{4,2},{5,3},{6,0},{7,1},{8,14},{9,15},{10,... | collective-permute-start | bytes 909320 | tf_op jit(solution)/shard_map/ppermute | solution.py:63
  69.5 8.2 %collective-permute-start.20 = (bf16[112,768]{1,0:T(8,128)(2,1)S(1)}, bf16[112,768]{1,0:T(8,128)(2,1)S(1)}, u32[]{:S(2)}, u32[]{:S(2)}) collective-permute-start(bf16[112,768]{1,0:T(8,128)(2,1)S(1)} %get-tuple-element.136), channel_id=1, source_target_pairs={{1,2},{3,4},{5,6},{7,8},{9,10},{11,12},{13,14},{15,16},{17,18},{19... | collective-permute-start | bytes 516104 | tf_op jit(solution)/shard_map/ppermute | solution.py:694
  70.2 7.5 %collective-permute-start.16 = (bf16[4,4,152,128]{3,2,1,0:T(8,128)(2,1)S(1)}, bf16[4,4,152,128]{3,2,1,0:T(8,128)(2,1)S(1)}, u32[]{:S(2)}, u32[]{:S(2)}) collective-permute-start(bf16[4,4,152,128]{3,2,1,0:T(8,128)(2,1)S(1)} %get-tuple-element.129), channel_id=1, source_target_pairs={{0,1},{1,0},{2,3},{3,2},{4,5},{5,4},{6,7},{7,6},{8,9},{9,8},{10,11... | collective-permute-start | bytes 1867784 | tf_op jit(solution)/shard_map/ppermute | solution.py:63
  77.9 9.0 %collective-permute-start.21 = (bf16[4,152,128]{2,1,0:T(8,128)(2,1)S(1)}, bf16[4,152,128]{2,1,0:T(8,128)(2,1)S(1)}, u32[]{:S(2)}, u32[]{:S(2)}) collective-permute-start(bf16[4,152,128]{2,1,0:T(8,128)(2,1)S(1)} %get-tuple-element.139), channel_id=1, source_target_pairs={{0,2},{1,3},{2,0},{3,1},{4,6},{5,7},{6,4},{7,5},{8,10},{9,11},{10,... | collective-permute-start | bytes 466952 | tf_op jit(solution)/shard_map/ppermute | solution.py:63
  81.6 9.2 %collective-permute-start.22 = (bf16[4,152,128]{2,1,0:T(8,128)(2,1)S(1)}, bf16[4,152,128]{2,1,0:T(8,128)(2,1)S(1)}, u32[]{:S(2)}, u32[]{:S(2)}) collective-permute-start(bf16[4,152,128]{2,1,0:T(8,128)(2,1)S(1)} %get-tuple-element.140), channel_id=1, source_target_pairs={{0,4},{1,5},{2,6},{3,7},{4,0},{5,1},{6,2},{7,3},{8,12},{9,13},{10,... | collective-permute-start | bytes 466952 | tf_op jit(solution)/shard_map/ppermute | solution.py:63
  82.0 8.8 %collective-permute-start.23 = (bf16[4,152,128]{2,1,0:T(8,128)(2,1)S(1)}, bf16[4,152,128]{2,1,0:T(8,128)(2,1)S(1)}, u32[]{:S(2)}, u32[]{:S(2)}) collective-permute-start(bf16[4,152,128]{2,1,0:T(8,128)(2,1)S(1)} %get-tuple-element.141), channel_id=1, source_target_pairs={{0,6},{1,7},{2,4},{3,5},{4,2},{5,3},{6,0},{7,1},{8,14},{9,15},{10,... | collective-permute-start | bytes 466952 | tf_op jit(solution)/shard_map/ppermute | solution.py:63
  83.1 11.2 %collective-permute-start.27 = (bf16[2,296,128]{2,1,0:T(8,128)(2,1)S(1)}, bf16[2,296,128]{2,1,0:T(8,128)(2,1)S(1)}, u32[]{:S(2)}, u32[]{:S(2)}) collective-permute-start(bf16[2,296,128]{2,1,0:T(8,128)(2,1)S(1)} %get-tuple-element.153), channel_id=1, source_target_pairs={{0,16},{1,17},{2,18},{3,19},{4,20},{5,21},{6,22},{7,23},{8,24},{9,... | collective-permute-start | bytes 454664 | tf_op jit(solution)/shard_map/ppermute | solution.py:63
  90.9 7.1 %collective-permute-start.25 = (bf16[2,152,128]{2,1,0:T(8,128)(2,1)S(1)}, bf16[2,152,128]{2,1,0:T(8,128)(2,1)S(1)}, u32[]{:S(2)}, u32[]{:S(2)}) collective-permute-start(bf16[2,152,128]{2,1,0:T(8,128)(2,1)S(1)} %get-tuple-element.149), channel_id=1, source_target_pairs={{0,16},{1,17},{2,18},{3,19},{4,20},{5,21},{6,22},{7,23},{8,24},{9,... | collective-permute-start | bytes 233480 | tf_op jit(solution)/shard_map/ppermute | solution.py:63
  94.5 8.4 %collective-permute-start.24 = (bf16[112,768]{1,0:T(8,128)(2,1)S(1)}, bf16[112,768]{1,0:T(8,128)(2,1)S(1)}, u32[]{:S(2)}, u32[]{:S(2)}) collective-permute-start(bf16[112,768]{1,0:T(8,128)(2,1)S(1)} %get-tuple-element.144), channel_id=1, source_target_pairs={{0,1},{1,0},{2,3},{3,2},{4,5},{5,4},{6,7},{7,6},{8,9},{9,8},{10,11... | collective-permute-start | bytes 516104 | tf_op jit(solution)/shard_map/ppermute | solution.py:63
  (9 other events, 65.4 us)

commit v8 on v7

--- a/solution.py
+++ b/solution.py
@@ -554,7 +554,10 @@
         half //= 2
         halves = [struct((half, padded, lanes), bf16)] * 2
         keep, send = call_kernel(add_layers_kernel, halves, [], 1, [keep, other])
-    other = pass_on(send, CORES * SQUARE, devices)
+    return (keep, pass_on(send, CORES * SQUARE, devices))
+
+
+def add_last(keep, other):
     return keep[0].astype(f32) + other[0].astype(f32)
 
 
@@ -698,8 +701,8 @@
     attn_keep, attn_send = add_chips(attn_parts, attn_passed)
     attn_keep, inner = barrier((attn_keep, inner))
     inner = pass_cores(inner, devices)
-    feed_sum = add_layers(feed_keep, feed_send, devices)
-    attn_sum = add_layers(attn_keep, attn_send, devices)
+    feed_keep, feed_other = add_layers(feed_keep, feed_send, devices)
+    attn_keep, attn_other = add_layers(attn_keep, attn_send, devices)
     output, grad_inputs = call_kernel(
         combine_kernel,
         [struct((token_rows, D), bf16), struct((token_rows, D), f32)],
@@ -707,6 +710,9 @@
         1,
         [meta, own_output, own_grad, inner, outer],
     )
+    attn_other, output, grad_inputs = barrier((attn_other, output, grad_inputs))
+    attn_sum = add_last(attn_keep, attn_other)
+    feed_sum = add_last(feed_keep, feed_other)
     return (output, grad_inputs, as_block(attn_sum, attn_blocks), as_block(feed_sum, mlp_blocks))
 
 

time: 104 us -> 103 us (level)
  waiting for transfers between devices: 35.1 us -> 33.7 us
    ppermute x27, waiting for transfers between devices: 35.1 us -> 33.7 us  [pass_on(): return lax.ppermute(value, 'fsdp', [(i, i ^ step) for i in range(devices)])]
  transfers between devices with their start and end apart: 29 -> 29, of which waited for: 15 -> 15; matrix products, arithmetic and copies ran while one was open for 3% -> 2% of each run, Pallas kernels for 15% -> 17%
where the time goes in v8:
time: 103 us
  starting transfers between devices  39.2 us (38%)
  waiting for transfers between devices  33.7 us (33%)
  Pallas kernels  25 us (24%)
  other arithmetic  2.44 us (2%)
  local copies, waits for them, and re-layouts  1.56 us (2%)
    ppermute x27, starting transfers between devices, pass_on(): return lax.ppermute(value, 'fsdp', [(i, i ^ step) for i in range(devices)])  37.8 us
    ppermute x27, waiting for transfers between devices, pass_on(): return lax.ppermute(value, 'fsdp', [(i, i ^ step) for i in range(devices)])  33.7 us
    pallas_call x17, Pallas kernels, call_kernel(): pl.pallas_call(kernel, out_shape=out_shapes, in_specs=specs, out_specs=[s...  25 us
    unnamed x4, other arithmetic  2.44 us
  transfers between devices with their start and end apart: 29, of which 15 were waited for; matrix products, arithmetic and copies ran while one was open for 2% of the time, Pallas kernels for 17%

profile of v8, /device:TPU:0, one launch (start us, length us, event | category | flops | bytes accessed | tf_op | source)
XLA Modules:
  0.0 102.8 jit_solution(15951549387485476610)
XLA Ops:
  1.7 5.1 %collective-permute-start.2 = (bf16[152,128]{1,0:T(8,128)(2,1)S(1)}, bf16[152,128]{1,0:T(8,128)(2,1)S(1)}, u32[]{:S(2)}, u32[]{:S(2)}) collective-permute-start(bf16[152,128]{1,0:T(8,128)(2,1)S(1)} %pad.8.refs_0_), channel_id=1, source_target_pairs={{0,24},{1,25},{2,26},{3,27},{4,28},{5,29},{6,30},{7,31},{8,16},{9,... | collective-permute-start | bytes 116744 | tf_op jit(solution)/shard_map/ppermute | solution.py:63
  8.8 1.5 %collective-permute-start.3 = (bf16[1,296,128]{2,1,0:T(8,128)(2,1)S(1)}, bf16[1,296,128]{2,1,0:T(8,128)(2,1)S(1)}, u32[]{:S(2)}, u32[]{:S(2)}) collective-permute-start(bf16[1,296,128]{2,1,0:T(8,128)(2,1)S(1)} %pad_bitcast_fusion.near_ref), channel_id=1, source_target_pairs={{0,8},{1,9},{2,10},{3,11},{4,12},{5,13},{6,14},{7,15},{8,0},{9,1},... | collective-permute-start | bytes 227336 | tf_op jit(solution)/shard_map/ppermute | solution.py:63
  10.3 2.0 %shard_map.93 = (bf16[256,896]{1,0:T(8,128)(2,1)}, bf16[112,896]{1,0:T(8,128)(2,1)}, bf16[112,896]{1,0:T(8,128)(2,1)}, s32[8]{0:T(128)}) custom-call(s32[1]{0:T(128)} %bitcast.device_ref, s32[2,128]{1,0:T(2,128)} %bitcast.21, s32[2,128]{1,0:T(2,128)} %bitcast.22, bf16[256,384]{1,0:T(8,128)(2,1)} %inputs_hbm.1, bf16[256,384]{1,0:T(8,128)(2,1)} %out_grad_hbm.1), custom_call_target="tpu_custom_call" | custom-call | flops 1 | bytes 1 | tf_op jit(solution)/shard_map/pallas_call | solution.py:505
  13.4 2.7 %collective-permute-start.6 = (bf16[4,152,128]{2,1,0:T(8,128)(2,1)S(1)}, bf16[4,152,128]{2,1,0:T(8,128)(2,1)S(1)}, u32[]{:S(2)}, u32[]{:S(2)}) collective-permute-start(bf16[4,152,128]{2,1,0:T(8,128)(2,1)S(1)} %shard_map.94.refs_0_), channel_id=1, source_target_pairs={{0,6},{1,7},{2,4},{3,5},{4,2},{5,3},{6,0},{7,1},{8,14},{9,15},{10,... | collective-permute-start | bytes 466952 | tf_op jit(solution)/shard_map/ppermute | solution.py:63
  17.0 2.7 %collective-permute-start.9 = (bf16[2,296,128]{2,1,0:T(8,128)(2,1)S(1)}, bf16[2,296,128]{2,1,0:T(8,128)(2,1)S(1)}, u32[]{:S(2)}, u32[]{:S(2)}) collective-permute-start(bf16[2,296,128]{2,1,0:T(8,128)(2,1)S(1)} %shard_map.95.near_ref), channel_id=1, source_target_pairs={{0,16},{1,17},{2,18},{3,19},{4,20},{5,21},{6,22},{7,23},{8,24},{9,... | collective-permute-start | bytes 454664 | tf_op jit(solution)/shard_map/ppermute | solution.py:63
  21.2 2.9 %collective-permute-done.5.refs_2_ = bf16[4,152,128]{2,1,0:T(8,128)(2,1)S(1)} collective-permute-done((bf16[4,152,128]{2,1,0:T(8,128)(2,1)S(1)}, bf16[4,152,128]{2,1,0:T(8,128)(2,1)S(1)}, u32[]{:S(2)}, u32[]{:S(2)}) %collective-permute-start.5) | collective-permute-done | bytes 155680 | tf_op jit(solution)/shard_map/ppermute | solution.py:63
  24.4 2.4 %collective-permute-done.9.far_ref = bf16[2,296,128]{2,1,0:T(8,128)(2,1)S(1)} collective-permute-done((bf16[2,296,128]{2,1,0:T(8,128)(2,1)S(1)}, bf16[2,296,128]{2,1,0:T(8,128)(2,1)S(1)}, u32[]{:S(2)}, u32[]{:S(2)}) %collective-permute-start.9) | collective-permute-done | bytes 151584 | tf_op jit(solution)/shard_map/ppermute | solution.py:63
  27.9 3.2 %collective-permute-start.12 = (bf16[4,296,128]{2,1,0:T(8,128)(2,1)S(1)}, bf16[4,296,128]{2,1,0:T(8,128)(2,1)S(1)}, u32[]{:S(2)}, u32[]{:S(2)}) collective-permute-start(bf16[4,296,128]{2,1,0:T(8,128)(2,1)S(1)} %shard_map.97.refs_0_), channel_id=1, source_target_pairs={{0,6},{1,7},{2,4},{3,5},{4,2},{5,3},{6,0},{7,1},{8,14},{9,15},{10,... | collective-permute-start | bytes 909320 | tf_op jit(solution)/shard_map/ppermute | solution.py:63
  32.0 4.3 %shard_map.98 = (f32[416,384]{1,0:T(8,128)S(1)}, bf16[416,384]{1,0:T(8,128)(2,1)S(1)}, bf16[416,384]{1,0:T(8,128)(2,1)S(1)}, bf16[416,384]{1,0:T(8,128)(2,1)S(1)...) custom-call(s32[8]{0:T(128)S(1)} %copy-done.1, ...), custom_call_target="tpu_custom_call" | custom-call | flops 1 | bytes 1 | tf_op jit(solution)/shard_map/pallas_call | solution.py:505
  36.4 2.8 %collective-permute-done.12.refs_3_ = bf16[4,296,128]{2,1,0:T(8,128)(2,1)S(1)} collective-permute-done((bf16[4,296,128]{2,1,0:T(8,128)(2,1)S(1)}, bf16[4,296,128]{2,1,0:T(8,128)(2,1)S(1)}, u32[]{:S(2)}, u32[]{:S(2)}) %collective-permute-start.12) | collective-permute-done | bytes 303136 | tf_op jit(solution)/shard_map/ppermute | solution.py:63
  39.1 6.1 %collective-permute-done.11.refs_2_ = bf16[4,296,128]{2,1,0:T(8,128)(2,1)S(1)} collective-permute-done((bf16[4,296,128]{2,1,0:T(8,128)(2,1)S(1)}, bf16[4,296,128]{2,1,0:T(8,128)(2,1)S(1)}, u32[]{:S(2)}, u32[]{:S(2)}) %collective-permute-start.11) | collective-permute-done | bytes 303136 | tf_op jit(solution)/shard_map/ppermute | solution.py:63
  46.2 2.9 %collective-permute-done.14.other_ref = bf16[4,4,296,128]{3,2,1,0:T(8,128)(2,1)S(1)} collective-permute-done((bf16[4,4,296,128]{3,2,1,0:T(8,128)(2,1)S(1)}, bf16[4,4,296,128]{3,2,1,0:T(8,128)(2,1)S(1)}, u32[]{:S(2)}, u32[]{:S(2)}) %collective-permute-start.14) | collective-permute-done | bytes 1212448 | tf_op jit(solution)/shard_map/ppermute | solution.py:63
  49.1 7.5 %shard_map.100 = (bf16[480,384]{1,0:T(8,128)(2,1)S(1)}, f32[416,384]{1,0:T(8,128)S(1)}, bf16[4,4,296,128]{3,2,1,0:T(8,128)(2,1)S(1)}, bf16[4,4,296,128]{3,2,1,0:T(8,128)(2,1)S(1)}) custom-call(s32[8]{0:T(128)S(1)} %copy-done.1, f32[416,384]{1,0:T(8,128)S(1)} %get-tuple-element.101.middle_ref, bf16[416,384]{1,0:T(8,128)(2,1)S(1)} %get-tuple-element.102.cotangent_ref, ...), custom_call_target="tpu_custom_call" | custom-call | flops 1 | bytes 1 | tf_op jit(solution)/shard_map/pallas_call | solution.py:505
  56.8 3.5 %shard_map.102 = (bf16[208,1152]{1,0:T(8,128)(2,1)S(1)}, f32[384,384]{1,0:T(8,128)S(1)}, f32[1,384]{1,0:T(1,128)S(1)}, f32[8,128]{1,0:T(8,128)S(1)}, bf16[416,384]{1,0:T(8,128)(2,1)S(1)}) custom-call(s32[8]{0:T(128)S(1)} %copy-done.1, f32[416,384]{1,0:T(8,128)S(1)} %get-tuple-element.106.grad_middle_ref, bf16[416,1152]{1,0:T(8,128)(2,1)S(1)} %get-tuple-element.110.qkv_ref, ...), custom_call_target="tpu_custom_call" | custom-call | flops 1 | bytes 1 | tf_op jit(solution)/shard_map/pallas_call | solution.py:505
  62.7 1.5 %collective-permute-start.19 = (bf16[4,296,128]{2,1,0:T(8,128)(2,1)S(1)}, bf16[4,296,128]{2,1,0:T(8,128)(2,1)S(1)}, u32[]{:S(2)}, u32[]{:S(2)}) collective-permute-start(bf16[4,296,128]{2,1,0:T(8,128)(2,1)S(1)} %get-tuple-element.134), channel_id=1, source_target_pairs={{0,6},{1,7},{2,4},{3,5},{4,2},{5,3},{6,0},{7,1},{8,14},{9,15},{10,... | collective-permute-start | bytes 909320 | tf_op jit(solution)/shard_map/ppermute | solution.py:63
  64.2 5.4 %shard_map.103 = (bf16[256,384]{1,0:T(8,128)(2,1)S(1)}, f32[256,384]{1,0:T(8,128)S(1)}, bf16[112,768]{1,0:T(8,128)(2,1)S(1)}, bf16[112,768]{1,0:T(8,128)(2,1)S(1...) custom-call(s32[8]{0:T(128)S(1)} %copy-done.1, ...), custom_call_target="tpu_custom_call" | custom-call | flops 1 | bytes 1 | tf_op jit(solution)/shard_map/pallas_call | solution.py:505
  70.2 2.4 %collective-permute-start.16 = (bf16[4,4,152,128]{3,2,1,0:T(8,128)(2,1)S(1)}, bf16[4,4,152,128]{3,2,1,0:T(8,128)(2,1)S(1)}, u32[]{:S(2)}, u32[]{:S(2)}) collective-permute-start(bf16[4,4,152,128]{3,2,1,0:T(8,128)(2,1)S(1)} %get-tuple-element.130), channel_id=1, source_target_pairs={{0,1},{1,0},{2,3},{3,2},{4,5},{5,4},{6,7},{7,6},{8,9},{9,8},{10,11... | collective-permute-start | bytes 1867784 | tf_op jit(solution)/shard_map/ppermute | solution.py:63
  72.6 4.7 %collective-permute-done.18.refs_2_ = bf16[4,296,128]{2,1,0:T(8,128)(2,1)S(1)} collective-permute-done((bf16[4,296,128]{2,1,0:T(8,128)(2,1)S(1)}, bf16[4,296,128]{2,1,0:T(8,128)(2,1)S(1)}, u32[]{:S(2)}, u32[]{:S(2)}) %collective-permute-start.18) | collective-permute-done | bytes 303136 | tf_op jit(solution)/shard_map/ppermute | solution.py:63
  77.9 3.7 %collective-permute-start.21 = (bf16[4,152,128]{2,1,0:T(8,128)(2,1)S(1)}, bf16[4,152,128]{2,1,0:T(8,128)(2,1)S(1)}, u32[]{:S(2)}, u32[]{:S(2)}) collective-permute-start(bf16[4,152,128]{2,1,0:T(8,128)(2,1)S(1)} %get-tuple-element.140), channel_id=1, source_target_pairs={{0,2},{1,3},{2,0},{3,1},{4,6},{5,7},{6,4},{7,5},{8,10},{9,11},{10,... | collective-permute-start | bytes 466952 | tf_op jit(solution)/shard_map/ppermute | solution.py:63
  83.1 3.8 %collective-permute-start.27 = (bf16[2,296,128]{2,1,0:T(8,128)(2,1)S(1)}, bf16[2,296,128]{2,1,0:T(8,128)(2,1)S(1)}, u32[]{:S(2)}, u32[]{:S(2)}) collective-permute-start(bf16[2,296,128]{2,1,0:T(8,128)(2,1)S(1)} %get-tuple-element.159), channel_id=1, source_target_pairs={{0,16},{1,17},{2,18},{3,19},{4,20},{5,21},{6,22},{7,23},{8,24},{9,... | collective-permute-start | bytes 454664 | tf_op jit(solution)/shard_map/ppermute | solution.py:63
  86.9 3.9 %collective-permute-done.22.refs_2_ = bf16[4,152,128]{2,1,0:T(8,128)(2,1)S(1)} collective-permute-done((bf16[4,152,128]{2,1,0:T(8,128)(2,1)S(1)}, bf16[4,152,128]{2,1,0:T(8,128)(2,1)S(1)}, u32[]{:S(2)}, u32[]{:S(2)}) %collective-permute-start.22) | collective-permute-done | bytes 155680 | tf_op jit(solution)/shard_map/ppermute | solution.py:63
  90.9 3.4 %collective-permute-start.24 = (bf16[2,152,128]{2,1,0:T(8,128)(2,1)S(1)}, bf16[2,152,128]{2,1,0:T(8,128)(2,1)S(1)}, u32[]{:S(2)}, u32[]{:S(2)}) collective-permute-start(bf16[2,152,128]{2,1,0:T(8,128)(2,1)S(1)} %get-tuple-element.146), channel_id=1, source_target_pairs={{0,16},{1,17},{2,18},{3,19},{4,20},{5,21},{6,22},{7,23},{8,24},{9,... | collective-permute-start | bytes 233480 | tf_op jit(solution)/shard_map/ppermute | solution.py:63
  94.5 3.5 %collective-permute-done.24.other_ref = bf16[2,152,128]{2,1,0:T(8,128)(2,1)S(1)} collective-permute-done((bf16[2,152,128]{2,1,0:T(8,128)(2,1)S(1)}, bf16[2,152,128]{2,1,0:T(8,128)(2,1)S(1)}, u32[]{:S(2)}, u32[]{:S(2)}) %collective-permute-start.24) | collective-permute-done | bytes 77856 | tf_op jit(solution)/shard_map/ppermute | solution.py:63
  99.7 1.4 %shard_map.108 = (bf16[256,384]{1,0:T(8,128)(2,1)}, f32[256,384]{1,0:T(8,128)}) custom-call(s32[8]{0:T(128)S(1)} %copy-done.1, bf16[256,384]{1,0:T(8,128)(2,1)S(1)} %get-tuple-element.148.own_output_ref, f32[256,384]{1,0:T(8,128)S(1)} %get-tuple-element.149.own_grad_ref, bf16[112,768]{1,0:T(8,128)(2,1)S(1)} %collective-permute-done.26.inner_ref, ...), custom_call_target="tpu_custom_call" | custom-call | flops 1 | bytes 1 | tf_op jit(solution)/shard_map/pallas_call | solution.py:505
  (67 shorter events, 18.7 us)
Async XLA Ops:
  1.7 10.6 %collective-permute-start.2 = (bf16[152,128]{1,0:T(8,128)(2,1)S(1)}, bf16[152,128]{1,0:T(8,128)(2,1)S(1)}, u32[]{:S(2)}, u32[]{:S(2)}) collective-permute-start(bf16[152,128]{1,0:T(8,128)(2,1)S(1)} %pad.8.refs_0_), channel_id=1, source_target_pairs={{0,24},{1,25},{2,26},{3,27},{4,28},{5,29},{6,30},{7,31},{8,16},{9,... | collective-permute-start | bytes 116744 | tf_op jit(solution)/shard_map/ppermute | solution.py:63
  6.9 5.5 %collective-permute-start.1 = (bf16[152,128]{1,0:T(8,128)(2,1)S(1)}, bf16[152,128]{1,0:T(8,128)(2,1)S(1)}, u32[]{:S(2)}, u32[]{:S(2)}) collective-permute-start(bf16[152,128]{1,0:T(8,128)(2,1)S(1)} %pad.8.refs_0_), channel_id=1, source_target_pairs={{0,16},{1,17},{2,18},{3,19},{4,20},{5,21},{6,22},{7,23},{8,24},{9,... | collective-permute-start | bytes 116744 | tf_op jit(solution)/shard_map/ppermute | solution.py:63
  6.9 5.5 %collective-permute-start = (bf16[152,128]{1,0:T(8,128)(2,1)S(1)}, bf16[152,128]{1,0:T(8,128)(2,1)S(1)}, u32[]{:S(2)}, u32[]{:S(2)}) collective-permute-start(bf16[152,128]{1,0:T(8,128)(2,1)S(1)} %pad.8.refs_0_), channel_id=1, source_target_pairs={{0,8},{1,9},{2,10},{3,11},{4,12},{5,13},{6,14},{7,15},{8,0},{9,1},... | collective-permute-start | bytes 116744 | tf_op jit(solution)/shard_map/ppermute | solution.py:63
  13.3 6.3 %collective-permute-start.7 = (bf16[112,896]{1,0:T(8,128)(2,1)S(1)}, bf16[112,896]{1,0:T(8,128)(2,1)S(1)}, u32[]{:S(2)}, u32[]{:S(2)}) collective-permute-start(bf16[112,896]{1,0:T(8,128)(2,1)S(1)} %copy-done.3), channel_id=1, source_target_pairs={{0,1},{1,0},{2,3},{3,2},{4,5},{5,4},{6,7},{7,6},{8,9},{9,8},{10,11... | collective-permute-start | bytes 602120 | tf_op jit(solution)/shard_map/ppermute | solution.py:63
  13.4 7.8 %collective-permute-start.6 = (bf16[4,152,128]{2,1,0:T(8,128)(2,1)S(1)}, bf16[4,152,128]{2,1,0:T(8,128)(2,1)S(1)}, u32[]{:S(2)}, u32[]{:S(2)}) collective-permute-start(bf16[4,152,128]{2,1,0:T(8,128)(2,1)S(1)} %shard_map.94.refs_0_), channel_id=1, source_target_pairs={{0,6},{1,7},{2,4},{3,5},{4,2},{5,3},{6,0},{7,1},{8,14},{9,15},{10,... | collective-permute-start | bytes 466952 | tf_op jit(solution)/shard_map/ppermute | solution.py:63
  16.1 8.0 %collective-permute-start.5 = (bf16[4,152,128]{2,1,0:T(8,128)(2,1)S(1)}, bf16[4,152,128]{2,1,0:T(8,128)(2,1)S(1)}, u32[]{:S(2)}, u32[]{:S(2)}) collective-permute-start(bf16[4,152,128]{2,1,0:T(8,128)(2,1)S(1)} %shard_map.94.refs_0_), channel_id=1, source_target_pairs={{0,4},{1,5},{2,6},{3,7},{4,0},{5,1},{6,2},{7,3},{8,12},{9,13},{10,... | collective-permute-start | bytes 466952 | tf_op jit(solution)/shard_map/ppermute | solution.py:63
  16.6 7.8 %collective-permute-start.4 = (bf16[4,152,128]{2,1,0:T(8,128)(2,1)S(1)}, bf16[4,152,128]{2,1,0:T(8,128)(2,1)S(1)}, u32[]{:S(2)}, u32[]{:S(2)}) collective-permute-start(bf16[4,152,128]{2,1,0:T(8,128)(2,1)S(1)} %shard_map.94.refs_0_), channel_id=1, source_target_pairs={{0,2},{1,3},{2,0},{3,1},{4,6},{5,7},{6,4},{7,5},{8,10},{9,11},{10,... | collective-permute-start | bytes 466952 | tf_op jit(solution)/shard_map/ppermute | solution.py:63
  17.0 9.8 %collective-permute-start.9 = (bf16[2,296,128]{2,1,0:T(8,128)(2,1)S(1)}, bf16[2,296,128]{2,1,0:T(8,128)(2,1)S(1)}, u32[]{:S(2)}, u32[]{:S(2)}) collective-permute-start(bf16[2,296,128]{2,1,0:T(8,128)(2,1)S(1)} %shard_map.95.near_ref), channel_id=1, source_target_pairs={{0,16},{1,17},{2,18},{3,19},{4,20},{5,21},{6,22},{7,23},{8,24},{9,... | collective-permute-start | bytes 454664 | tf_op jit(solution)/shard_map/ppermute | solution.py:63
  19.7 7.1 %collective-permute-start.8 = (bf16[112,896]{1,0:T(8,128)(2,1)S(1)}, bf16[112,896]{1,0:T(8,128)(2,1)S(1)}, u32[]{:S(2)}, u32[]{:S(2)}) collective-permute-start(bf16[112,896]{1,0:T(8,128)(2,1)S(1)} %copy-done.2), channel_id=1, source_target_pairs={{1,2},{3,4},{5,6},{7,8},{9,10},{11,12},{13,14},{15,16},{17,18},{19... | collective-permute-start | bytes 602120 | tf_op jit(solution)/shard_map/ppermute | solution.py:606
  26.8 5.2 %collective-permute-start.13 = (bf16[4,4,152,128]{3,2,1,0:T(8,128)(2,1)S(1)}, bf16[4,4,152,128]{3,2,1,0:T(8,128)(2,1)S(1)}, u32[]{:S(2)}, u32[]{:S(2)}) collective-permute-start(bf16[4,4,152,128]{3,2,1,0:T(8,128)(2,1)S(1)} %shard_map.96.mine_ref), channel_id=1, source_target_pairs={{0,1},{1,0},{2,3},{3,2},{4,5},{5,4},{6,7},{7,6},{8,9},{9,8},{10,11... | collective-permute-start | bytes 1867784 | tf_op jit(solution)/shard_map/ppermute | solution.py:63
  27.9 11.2 %collective-permute-start.12 = (bf16[4,296,128]{2,1,0:T(8,128)(2,1)S(1)}, bf16[4,296,128]{2,1,0:T(8,128)(2,1)S(1)}, u32[]{:S(2)}, u32[]{:S(2)}) collective-permute-start(bf16[4,296,128]{2,1,0:T(8,128)(2,1)S(1)} %shard_map.97.refs_0_), channel_id=1, source_target_pairs={{0,6},{1,7},{2,4},{3,5},{4,2},{5,3},{6,0},{7,1},{8,14},{9,15},{10,... | collective-permute-start | bytes 909320 | tf_op jit(solution)/shard_map/ppermute | solution.py:63
  31.1 14.1 %collective-permute-start.11 = (bf16[4,296,128]{2,1,0:T(8,128)(2,1)S(1)}, bf16[4,296,128]{2,1,0:T(8,128)(2,1)S(1)}, u32[]{:S(2)}, u32[]{:S(2)}) collective-permute-start(bf16[4,296,128]{2,1,0:T(8,128)(2,1)S(1)} %shard_map.97.refs_0_), channel_id=1, source_target_pairs={{0,4},{1,5},{2,6},{3,7},{4,0},{5,1},{6,2},{7,3},{8,12},{9,13},{10,... | collective-permute-start | bytes 909320 | tf_op jit(solution)/shard_map/ppermute | solution.py:63
  31.8 14.3 %collective-permute-start.10 = (bf16[4,296,128]{2,1,0:T(8,128)(2,1)S(1)}, bf16[4,296,128]{2,1,0:T(8,128)(2,1)S(1)}, u32[]{:S(2)}, u32[]{:S(2)}) collective-permute-start(bf16[4,296,128]{2,1,0:T(8,128)(2,1)S(1)} %shard_map.97.refs_0_), channel_id=1, source_target_pairs={{0,2},{1,3},{2,0},{3,1},{4,6},{5,7},{6,4},{7,5},{8,10},{9,11},{10,... | collective-permute-start | bytes 909320 | tf_op jit(solution)/shard_map/ppermute | solution.py:63
  60.6 12.0 %collective-permute-start.17 = (bf16[4,296,128]{2,1,0:T(8,128)(2,1)S(1)}, bf16[4,296,128]{2,1,0:T(8,128)(2,1)S(1)}, u32[]{:S(2)}, u32[]{:S(2)}) collective-permute-start(bf16[4,296,128]{2,1,0:T(8,128)(2,1)S(1)} %get-tuple-element.132), channel_id=1, source_target_pairs={{0,2},{1,3},{2,0},{3,1},{4,6},{5,7},{6,4},{7,5},{8,10},{9,11},{10,... | collective-permute-start | bytes 909320 | tf_op jit(solution)/shard_map/ppermute | solution.py:63
  61.7 15.7 %collective-permute-start.18 = (bf16[4,296,128]{2,1,0:T(8,128)(2,1)S(1)}, bf16[4,296,128]{2,1,0:T(8,128)(2,1)S(1)}, u32[]{:S(2)}, u32[]{:S(2)}) collective-permute-start(bf16[4,296,128]{2,1,0:T(8,128)(2,1)S(1)} %get-tuple-element.133), channel_id=1, source_target_pairs={{0,4},{1,5},{2,6},{3,7},{4,0},{5,1},{6,2},{7,3},{8,12},{9,13},{10,... | collective-permute-start | bytes 909320 | tf_op jit(solution)/shard_map/ppermute | solution.py:63
  62.7 14.9 %collective-permute-start.19 = (bf16[4,296,128]{2,1,0:T(8,128)(2,1)S(1)}, bf16[4,296,128]{2,1,0:T(8,128)(2,1)S(1)}, u32[]{:S(2)}, u32[]{:S(2)}) collective-permute-start(bf16[4,296,128]{2,1,0:T(8,128)(2,1)S(1)} %get-tuple-element.134), channel_id=1, source_target_pairs={{0,6},{1,7},{2,4},{3,5},{4,2},{5,3},{6,0},{7,1},{8,14},{9,15},{10,... | collective-permute-start | bytes 909320 | tf_op jit(solution)/shard_map/ppermute | solution.py:63
  69.5 8.2 %collective-permute-start.20 = (bf16[112,768]{1,0:T(8,128)(2,1)S(1)}, bf16[112,768]{1,0:T(8,128)(2,1)S(1)}, u32[]{:S(2)}, u32[]{:S(2)}) collective-permute-start(bf16[112,768]{1,0:T(8,128)(2,1)S(1)} %get-tuple-element.137), channel_id=1, source_target_pairs={{1,2},{3,4},{5,6},{7,8},{9,10},{11,12},{13,14},{15,16},{17,18},{19... | collective-permute-start | bytes 516104 | tf_op jit(solution)/shard_map/ppermute | solution.py:697
  70.2 7.5 %collective-permute-start.16 = (bf16[4,4,152,128]{3,2,1,0:T(8,128)(2,1)S(1)}, bf16[4,4,152,128]{3,2,1,0:T(8,128)(2,1)S(1)}, u32[]{:S(2)}, u32[]{:S(2)}) collective-permute-start(bf16[4,4,152,128]{3,2,1,0:T(8,128)(2,1)S(1)} %get-tuple-element.130), channel_id=1, source_target_pairs={{0,1},{1,0},{2,3},{3,2},{4,5},{5,4},{6,7},{7,6},{8,9},{9,8},{10,11... | collective-permute-start | bytes 1867784 | tf_op jit(solution)/shard_map/ppermute | solution.py:63
  77.9 9.0 %collective-permute-start.21 = (bf16[4,152,128]{2,1,0:T(8,128)(2,1)S(1)}, bf16[4,152,128]{2,1,0:T(8,128)(2,1)S(1)}, u32[]{:S(2)}, u32[]{:S(2)}) collective-permute-start(bf16[4,152,128]{2,1,0:T(8,128)(2,1)S(1)} %get-tuple-element.140), channel_id=1, source_target_pairs={{0,2},{1,3},{2,0},{3,1},{4,6},{5,7},{6,4},{7,5},{8,10},{9,11},{10,... | collective-permute-start | bytes 466952 | tf_op jit(solution)/shard_map/ppermute | solution.py:63
  81.6 9.2 %collective-permute-start.22 = (bf16[4,152,128]{2,1,0:T(8,128)(2,1)S(1)}, bf16[4,152,128]{2,1,0:T(8,128)(2,1)S(1)}, u32[]{:S(2)}, u32[]{:S(2)}) collective-permute-start(bf16[4,152,128]{2,1,0:T(8,128)(2,1)S(1)} %get-tuple-element.141), channel_id=1, source_target_pairs={{0,4},{1,5},{2,6},{3,7},{4,0},{5,1},{6,2},{7,3},{8,12},{9,13},{10,... | collective-permute-start | bytes 466952 | tf_op jit(solution)/shard_map/ppermute | solution.py:63
  82.0 8.8 %collective-permute-start.23 = (bf16[4,152,128]{2,1,0:T(8,128)(2,1)S(1)}, bf16[4,152,128]{2,1,0:T(8,128)(2,1)S(1)}, u32[]{:S(2)}, u32[]{:S(2)}) collective-permute-start(bf16[4,152,128]{2,1,0:T(8,128)(2,1)S(1)} %get-tuple-element.142), channel_id=1, source_target_pairs={{0,6},{1,7},{2,4},{3,5},{4,2},{5,3},{6,0},{7,1},{8,14},{9,15},{10,... | collective-permute-start | bytes 466952 | tf_op jit(solution)/shard_map/ppermute | solution.py:63
  83.1 11.2 %collective-permute-start.27 = (bf16[2,296,128]{2,1,0:T(8,128)(2,1)S(1)}, bf16[2,296,128]{2,1,0:T(8,128)(2,1)S(1)}, u32[]{:S(2)}, u32[]{:S(2)}) collective-permute-start(bf16[2,296,128]{2,1,0:T(8,128)(2,1)S(1)} %get-tuple-element.159), channel_id=1, source_target_pairs={{0,16},{1,17},{2,18},{3,19},{4,20},{5,21},{6,22},{7,23},{8,24},{9,... | collective-permute-start | bytes 454664 | tf_op jit(solution)/shard_map/ppermute | solution.py:63
  90.9 7.1 %collective-permute-start.24 = (bf16[2,152,128]{2,1,0:T(8,128)(2,1)S(1)}, bf16[2,152,128]{2,1,0:T(8,128)(2,1)S(1)}, u32[]{:S(2)}, u32[]{:S(2)}) collective-permute-start(bf16[2,152,128]{2,1,0:T(8,128)(2,1)S(1)} %get-tuple-element.146), channel_id=1, source_target_pairs={{0,16},{1,17},{2,18},{3,19},{4,20},{5,21},{6,22},{7,23},{8,24},{9,... | collective-permute-start | bytes 233480 | tf_op jit(solution)/shard_map/ppermute | solution.py:63
  94.5 5.2 %collective-permute-start.26 = (bf16[112,768]{1,0:T(8,128)(2,1)S(1)}, bf16[112,768]{1,0:T(8,128)(2,1)S(1)}, u32[]{:S(2)}, u32[]{:S(2)}) collective-permute-start(bf16[112,768]{1,0:T(8,128)(2,1)S(1)} %get-tuple-element.150), channel_id=1, source_target_pairs={{0,1},{1,0},{2,3},{3,2},{4,5},{5,4},{6,7},{7,6},{8,9},{9,8},{10,11... | collective-permute-start | bytes 516104 | tf_op jit(solution)/shard_map/ppermute | solution.py:63
  (9 other events, 65.4 us)
